TPU v7x, 32 devices: a whole 2x2x4 slice. The times are simulated.
32 devices in a mesh: row: 8 (over z, x), col: 4 (over y, core).
Axes of the slice: x: 2, y: 2, z: 4, core: 2. Of those that a mesh axis runs over, the one named last changes fastest.
Arguments:
- southeast_edges: bfloat16 [8, 4, 2, 2, 2, 96, 768], P('row', 'col'), may hold values from -6 to 6
- northwest_edges: bfloat16 [8, 4, 2, 2, 2, 96, 768], P('row', 'col'), may hold values from -6 to 6
- southeast_corners: bfloat16 [8, 4, 2, 2, 96, 128], P('row', 'col'), may hold values from -6 to 6
- northwest_corners: bfloat16 [8, 4, 2, 2, 96, 128], P('row', 'col'), may hold values from -6 to 6
- operators: bfloat16 [8, 4, 2, 2, 768, 768], P('row', 'col'), may hold values from -0.109375 to 0.109375
- sources: bfloat16 [8, 4, 2, 2, 96, 768], P('row', 'col'), may hold values from -3 to 3
- roster: int32 [2, 3, 2], replicated, may hold values from 0 to 1, as said below
Outputs:
- southeast_out: bfloat16 [8, 4, 2, 2, 2, 96, 768], P('row', 'col')
- northwest_out: bfloat16 [8, 4, 2, 2, 2, 96, 768], P('row', 'col')
- southeast_corner_out: bfloat16 [8, 4, 2, 2, 96, 128], P('row', 'col')
- northwest_corner_out: bfloat16 [8, 4, 2, 2, 96, 128], P('row', 'col')
Inputs may be any that keep to these rules, and one draw needn't show every extreme that they name: roster[d, k, b] is the class, modulo 2, of the antidiagonals on which batch b of direction d stands at tick k. It rises by one modulo 2 from each tick to the next, and at every tick the 2 batches of one direction take all classes, each once.
All inputs are finite; a program needn't handle non-finite values.
Results may differ from a plain program's by a relative error of at most 0.0051.
Values may be sent and summed in bfloat16 or wider, within the bound.
No kernel may reach another device: no remote copies, remote signals or barrier semaphores. Data moves between devices by JAX's collectives and lax.ppermute only.
A program may use at most 64 MiB of HBM per device.

v0:
```python
import jax
import jax.numpy as jnp
from jax import lax
from jax.sharding import PartitionSpec as P

TICKS = 3


def from_behind(array, axis, by):
    count = lax.axis_size(axis)
    return lax.ppermute(array, axis, [(i, (i + by) % count) for i in range(count)])


def trace_update(first_in, second_in, corner_in, cell_operators, source, flipped):
    shot_count = first_in.shape[1]
    edge_width = first_in.shape[2]
    corner_width = corner_in.shape[-1]
    stacked = jnp.stack([first_in, second_in]).reshape(4 * shot_count, edge_width)
    form = "qe,mpfe->mpqf" if flipped else "qe,mpef->mpqf"
    products = jnp.einsum(form, stacked, cell_operators, preferred_element_type=jnp.float32)
    products = products.reshape(2, 2, 2, 2, shot_count, edge_width)

    def complex_product(source_index, operator_index):
        real_part = (
            products[operator_index, 0, source_index, 0]
            - products[operator_index, 1, source_index, 1]
        )
        imag_part = (
            products[operator_index, 1, source_index, 0]
            + products[operator_index, 0, source_index, 1]
        )
        return jnp.stack([real_part, imag_part])

    source_value = source.astype(jnp.float32)
    corner_value = corner_in.astype(jnp.float32)
    first_out = complex_product(0, 0) + complex_product(1, 1) + source_value
    second_out = complex_product(0, 1) + complex_product(1, 0) + source_value
    if flipped:
        first_out = first_out.at[:, :, edge_width - corner_width :].add(corner_value)
        second_out = second_out.at[:, :, edge_width - corner_width :].add(corner_value)
        corner_out = 0.5 * (first_out[:, :, :corner_width] + second_out[:, :, :corner_width])
    else:
        first_out = first_out.at[:, :, :corner_width].add(corner_value)
        second_out = second_out.at[:, :, :corner_width].add(corner_value)
        corner_out = 0.5 * (
            first_out[:, :, edge_width - corner_width :]
            + second_out[:, :, edge_width - corner_width :]
        )
    return (
        first_out.astype(jnp.bfloat16),
        second_out.astype(jnp.bfloat16),
        corner_out.astype(jnp.bfloat16),
    )


def southeast_moves(first_send, second_send, corner_send):
    from_west, corner_half = from_behind((second_send, corner_send), "col", 1)
    from_north, from_corner = from_behind((first_send, corner_half), "row", 1)
    return (from_north, from_west, from_corner)


def northwest_moves(first_send, second_send, corner_send):
    from_east, corner_half = from_behind((second_send, corner_send), "col", -1)
    from_south, from_corner = from_behind((first_send, corner_half), "row", -1)
    return (from_south, from_east, from_corner)


def sweep_tick(
    states, corner_states, front_plan, frame_row, frame_col, local_operators, local_sources, flipped
):
    batch_count = front_plan.shape[0]
    klass = (frame_row + frame_col) % batch_count
    first_send = states[0]
    second_send = states[1]
    corner_send = corner_states
    if flipped:
        got_first, got_second, got_corner = northwest_moves(first_send, second_send, corner_send)
    else:
        got_first, got_second, got_corner = southeast_moves(first_send, second_send, corner_send)
    chosen = jnp.argmax((front_plan == klass).astype(jnp.int32))
    first_in = got_first[chosen]
    second_in = got_second[chosen]
    corner_in = got_corner[chosen]
    new_first, new_second, new_corner = trace_update(
        first_in, second_in, corner_in, local_operators, local_sources[chosen], flipped
    )
    states = states.at[:, chosen].set(jnp.stack([new_first, new_second]))
    corner_states = corner_states.at[chosen].set(new_corner)
    return (states, corner_states)


def shards(
    southeast_edges,
    northwest_edges,
    southeast_corners,
    northwest_corners,
    operators,
    sources,
    roster,
):
    down_states = southeast_edges[0, 0]
    up_states = northwest_edges[0, 0]
    down_corners = southeast_corners[0, 0]
    up_corners = northwest_corners[0, 0]
    local_operators = operators[0, 0]
    local_sources = sources[0, 0]
    row_count = lax.axis_size("row")
    col_count = lax.axis_size("col")
    row_place = lax.axis_index("row")
    col_place = lax.axis_index("col")
    up_row = row_count - 1 - row_place
    up_col = col_count - 1 - col_place
    for tick_index in range(TICKS):
        down_states, down_corners = sweep_tick(
            down_states,
            down_corners,
            roster[0, tick_index],
            row_place,
            col_place,
            local_operators,
            local_sources,
            False,
        )
        up_states, up_corners = sweep_tick(
            up_states,
            up_corners,
            roster[1, tick_index],
            up_row,
            up_col,
            local_operators,
            local_sources,
            True,
        )
    return (
        down_states[None, None],
        up_states[None, None],
        down_corners[None, None],
        up_corners[None, None],
    )


def solution(mesh):
    placed = (
        P("row", "col", None, None, None, None, None),
        P("row", "col", None, None, None, None, None),
        P("row", "col", None, None, None, None),
        P("row", "col", None, None, None, None),
        P("row", "col", None, None, None, None),
        P("row", "col", None, None, None, None),
        P(),
    )
    return jax.shard_map(
        shards,
        mesh=mesh,
        in_specs=placed,
        out_specs=(
            P("row", "col", None, None, None, None, None),
            P("row", "col", None, None, None, None, None),
            P("row", "col", None, None, None, None),
            P("row", "col", None, None, None, None),
        ),
        check_vma=False,
    )
```

profile of v0, /device:TPU:0, one launch (start us, length us, event | category | flops | bytes accessed | tf_op | source)
XLA Modules:
  0.0 144.6 jit_solution(5280916518099492817)
XLA Ops:
  0.6 2.4 %slice_bitcast_fusion.9 = (bf16[2,2,96,768]{3,2,1,0:T(8,128)(2,1)}, bf16[2,2,96,768]{3,2,1,0:T(8,128)(2,1)}) fusion(bf16[1,1,2,2,2,96,768]{6,5,4,3,2,1,0:T(8,128)(2,1)} %param.56), kind=kLoop, calls=%fused_computation.71 | loop fusion | bytes 2359296 | tf_op jit(solution)/shard_map/squeeze | solution.py:73
  3.1 2.4 %collective-permute-start.13 = (bf16[2,2,96,768]{3,2,1,0:T(8,128)(2,1)}, bf16[2,2,96,768]{3,2,1,0:T(8,128)(2,1)}, u32[]{:S(2)}, u32[]{:S(2)}) collective-permute-start(bf16[2,2,96,768]{3,2,1,0:T(8,128)(2,1)} %get-tuple-element.379), channel_id=1, source_target_pairs={{0,3},{1,0},{2,1},{3,2},{4,7},{5,4},{6,5},{7,6},{8,11},{9,8},{10,9... | collective-permute-start | bytes 1769480 | tf_op jit(solution)/shard_map/ppermute | solution.py:11
  5.5 4.5 %collective-permute-start.12 = (bf16[2,2,96,768]{3,2,1,0:T(8,128)(2,1)}, bf16[2,2,96,768]{3,2,1,0:T(8,128)(2,1)}, u32[]{:S(2)}, u32[]{:S(2)}) collective-permute-start(bf16[2,2,96,768]{3,2,1,0:T(8,128)(2,1)} %get-tuple-element.378), channel_id=1, source_target_pairs={{0,28},{4,0},{8,4},{12,8},{16,12},{20,16},{24,20},{28,24},{1,29},{... | collective-permute-start | bytes 1769480 | tf_op jit(solution)/shard_map/ppermute | solution.py:11
  10.4 1.1 slice_bitcast_fusion.11
  18.9 1.5 %copy.38 = bf16[2,2,96,128]{3,2,1,0:T(8,128)(2,1)} copy(bf16[2,2,96,128]{3,2,1,0:T(8,128)(2,1)} %bitcast.96) | data formatting | bytes 196608
  25.3 1.6 %copy.45 = bf16[2,2,96,128]{3,2,1,0:T(8,128)(2,1)} copy(bf16[2,2,96,128]{3,2,1,0:T(8,128)(2,1)} %bitcast.16) | data formatting | bytes 196608
  34.4 1.5 %and_reduce_fusion.3 = (pred[]{:T(512)}, pred[]{:T(512)}, pred[]{:T(512)}, pred[]{:T(512)}, pred[]{:T(512)}, /*index=5*/pred[]{:T(512)}) fusion(s32[5]{0:T(128)} %constant.561.clone.1, s32[5]{0:T(128)} %concatenate.90, s32[5]{0:T(128)} %concatenate.88, s32[5]{0:T(128)} %concatenate.87, s32[5]{0:T(128)S(1)} %concatenate.85, s32[5]{0:T(128)S(1)} %concatenate.83, ...), kind=kLoop, calls=%fused_computation.259 | loop fusion | flops 114 | bytes 146 | tf_op jit(solution)/shard_map/reduce.64
  36.6 4.7 %collective-permute-start.15 = (bf16[2,2,96,128]{3,2,1,0:T(8,128)(2,1)}, bf16[2,2,96,128]{3,2,1,0:T(8,128)(2,1)S(1)}, u32[]{:S(2)}, u32[]{:S(2)}) collective-permute-start(bf16[2,2,96,128]{3,2,1,0:T(8,128)(2,1)} %collective-permute-done.14), channel_id=1, source_target_pairs={{0,28},{4,0},{8,4},{12,8},{16,12},{20,16},{24,20},{28,24},{1,29},{... | collective-permute-start | bytes 294920 | tf_op jit(solution)/shard_map/ppermute | solution.py:11
  43.4 4.5 %fusion.4 = f32[384,2,2,768]{3,0,2,1:T(8,128)S(1)} fusion(bf16[384,768,1,1]{1,0,3,2:T(8,128)(2,1)S(1)} %bitcast.390, bf16[1,1,2,2,768,768]{5,4,3,2,1,0:T(8,128)(2,1)} %param.59), kind=kOutput, calls=%fused_computation.4 | convolution fusion | flops 1811939328 | bytes 10027008 | tf_op jit(solution)/shard_map/qe,mpfe->mpqf/dot_general | solution.py:20
  50.3 7.7 %collective-permute-start.16 = (bf16[2,2,96,768]{3,2,1,0:T(8,128)(2,1)S(1)}, bf16[2,2,96,768]{3,2,1,0:T(8,128)(2,1)S(1)}, u32[]{:S(2)}, u32[]{:S(2)}) collective-permute-start(bf16[2,2,96,768]{3,2,1,0:T(8,128)(2,1)S(1)} %get-tuple-element.376), channel_id=1, source_target_pairs={{0,28},{4,0},{8,4},{12,8},{16,12},{20,16},{24,20},{28,24},{1,29},{... | collective-permute-start | bytes 1769480 | tf_op jit(solution)/shard_map/ppermute | solution.py:11
  58.8 1.5 %fusion.104 = bf16[2,2,96,128]{3,2,1,0:T(8,128)(2,1)S(1)} fusion(bf16[2,2,96,128]{3,2,1,0:T(8,128)(2,1)S(1)} %copy-done.6, s32[]{:T(128)} %select_n.101, f32[2,96,768]{2,1,0:T(8,128)S(1)} %get-tuple-element.403, f32[2,96,768]{2,1,0:T(8,128)S(1)} %get-tuple-element.402, bf16[1,1,2,2,96,128]{5,4,3,2,1,0:T(8,128)(2,1)} %param.58, pred[]{:T(512)} %get-tuple-element.323), kind=kLoop, calls=%fused_computation.232 | loop fusion | flops 98304 | bytes 294917 | tf_op jit(solution)/shard_map/scatter | solution.py:88
  62.2 5.1 %collective-permute-done.18 = bf16[2,2,96,128]{3,2,1,0:T(8,128)(2,1)S(1)} collective-permute-done((bf16[2,2,96,128]{3,2,1,0:T(8,128)(2,1)S(1)}, bf16[2,2,96,128]{3,2,1,0:T(8,128)(2,1)S(1)}, u32[]{:S(2)}, u32[]{:S(2)}) %collective-permute-start.18) | collective-permute-done | bytes 98336 | tf_op jit(solution)/shard_map/ppermute | solution.py:11
  67.3 2.4 %collective-permute-start.19 = (bf16[2,2,96,128]{3,2,1,0:T(8,128)(2,1)S(1)}, bf16[2,2,96,128]{3,2,1,0:T(8,128)(2,1)S(1)}, u32[]{:S(2)}, u32[]{:S(2)}) collective-permute-start(bf16[2,2,96,128]{3,2,1,0:T(8,128)(2,1)S(1)} %collective-permute-done.18), channel_id=1, source_target_pairs={{0,28},{4,0},{8,4},{12,8},{16,12},{20,16},{24,20},{28,24},{1,29},{... | collective-permute-start | bytes 294920 | tf_op jit(solution)/shard_map/ppermute | solution.py:11
  69.6 1.1 collective-permute-done.16
  70.9 2.0 %fusion.2 = f32[384,2,2,768]{3,0,2,1:T(8,128)S(1)} fusion(bf16[384,768,1,1]{1,0,3,2:T(8,128)(2,1)S(1)} %bitcast.391, bf16[1,1,2,2,768,768]{5,4,3,2,1,0:T(8,128)(2,1)S(1)} %bitcast.396), kind=kOutput, calls=%fused_computation.2 | convolution fusion | flops 1811939328 | bytes 10027008 | tf_op jit(solution)/shard_map/qe,mpfe->mpqf/dot_general | solution.py:20
  74.6 5.2 %collective-permute-start.20 = (bf16[2,2,96,768]{3,2,1,0:T(8,128)(2,1)S(1)}, bf16[2,2,96,768]{3,2,1,0:T(8,128)(2,1)S(1)}, u32[]{:S(2)}, u32[]{:S(2)}) collective-permute-start(bf16[2,2,96,768]{3,2,1,0:T(8,128)(2,1)S(1)} %get-tuple-element.374), channel_id=1, source_target_pairs={{0,28},{4,0},{8,4},{12,8},{16,12},{20,16},{24,20},{28,24},{1,29},{... | collective-permute-start | bytes 1769480 | tf_op jit(solution)/shard_map/ppermute | solution.py:11
  79.8 2.0 %fusion.10 = f32[384,2,2,768]{3,0,2,1:T(8,128)S(1)} fusion(bf16[384,768,1,1]{1,0,3,2:T(8,128)(2,1)S(1)} %bitcast.389, bf16[1,1,2,2,768,768]{5,4,3,2,1,0:T(8,128)(2,1)S(1)} %bitcast.396), kind=kOutput, calls=%fused_computation.10 | convolution fusion | flops 1811939328 | bytes 10027008 | tf_op jit(solution)/shard_map/qe,mpef->mpqf/dot_general | solution.py:20
  82.6 1.6 %collective-permute-start.22 = (bf16[2,2,96,128]{3,2,1,0:T(8,128)(2,1)S(1)}, bf16[2,2,96,128]{3,2,1,0:T(8,128)(2,1)S(1)}, u32[]{:S(2)}, u32[]{:S(2)}) collective-permute-start(bf16[2,2,96,128]{3,2,1,0:T(8,128)(2,1)S(1)} %fusion.107), channel_id=1, source_target_pairs={{0,3},{1,0},{2,1},{3,2},{4,7},{5,4},{6,5},{7,6},{8,11},{9,8},{10,9... | collective-permute-start | bytes 294920 | tf_op jit(solution)/shard_map/ppermute | solution.py:11
  84.5 5.8 %collective-permute-done.22 = bf16[2,2,96,128]{3,2,1,0:T(8,128)(2,1)S(1)} collective-permute-done((bf16[2,2,96,128]{3,2,1,0:T(8,128)(2,1)S(1)}, bf16[2,2,96,128]{3,2,1,0:T(8,128)(2,1)S(1)}, u32[]{:S(2)}, u32[]{:S(2)}) %collective-permute-start.22) | collective-permute-done | bytes 98336 | tf_op jit(solution)/shard_map/ppermute | solution.py:11
  91.9 2.0 %fusion = f32[384,2,2,768]{3,0,2,1:T(8,128)S(1)} fusion(bf16[384,768,1,1]{1,0,3,2:T(8,128)(2,1)S(1)} %bitcast.392, bf16[1,1,2,2,768,768]{5,4,3,2,1,0:T(8,128)(2,1)S(1)} %bitcast.396), kind=kOutput, calls=%fused_computation | convolution fusion | flops 1811939328 | bytes 10027008 | tf_op jit(solution)/shard_map/qe,mpfe->mpqf/dot_general | solution.py:20
  94.9 1.1 copy-done.3
  97.7 1.4 fusion.98
  99.1 1.1 collective-permute-start.6
  100.9 2.3 %collective-permute-done.6 = bf16[2,2,96,128]{3,2,1,0:T(8,128)(2,1)S(1)} collective-permute-done((bf16[2,2,96,128]{3,2,1,0:T(8,128)(2,1)S(1)}, bf16[2,2,96,128]{3,2,1,0:T(8,128)(2,1)S(1)}, u32[]{:S(2)}, u32[]{:S(2)}) %collective-permute-start.6) | collective-permute-done | bytes 98336 | tf_op jit(solution)/shard_map/ppermute | solution.py:11
  103.8 12.4 %collective-permute-done.4 = bf16[2,2,96,768]{3,2,1,0:T(8,128)(2,1)S(1)} collective-permute-done((bf16[2,2,96,768]{3,2,1,0:T(8,128)(2,1)S(1)}, bf16[2,2,96,768]{3,2,1,0:T(8,128)(2,1)S(1)}, u32[]{:S(2)}, u32[]{:S(2)}) %collective-permute-start.4) | collective-permute-done | bytes 589856 | tf_op jit(solution)/shard_map/ppermute | solution.py:11
  116.4 2.0 %fusion.8 = f32[384,2,2,768]{3,0,2,1:T(8,128)S(1)} fusion(bf16[384,768,1,1]{1,0,3,2:T(8,128)(2,1)S(1)} %bitcast.393, bf16[1,1,2,2,768,768]{5,4,3,2,1,0:T(8,128)(2,1)S(1)} %bitcast.396), kind=kOutput, calls=%fused_computation.8 | convolution fusion | flops 1811939328 | bytes 10027008 | tf_op jit(solution)/shard_map/qe,mpef->mpqf/dot_general | solution.py:20
  121.5 1.3 collective-permute-start.10
  123.5 1.1 copy.20
  124.7 5.6 %collective-permute-done.10 = bf16[2,2,96,128]{3,2,1,0:T(8,128)(2,1)S(1)} collective-permute-done((bf16[2,2,96,128]{3,2,1,0:T(8,128)(2,1)S(1)}, bf16[2,2,96,128]{3,2,1,0:T(8,128)(2,1)S(1)}, u32[]{:S(2)}, u32[]{:S(2)}) %collective-permute-start.10) | collective-permute-done | bytes 98336 | tf_op jit(solution)/shard_map/ppermute | solution.py:11
  130.4 8.3 %collective-permute-done.8 = bf16[2,2,96,768]{3,2,1,0:T(8,128)(2,1)S(1)} collective-permute-done((bf16[2,2,96,768]{3,2,1,0:T(8,128)(2,1)S(1)}, bf16[2,2,96,768]{3,2,1,0:T(8,128)(2,1)S(1)}, u32[]{:S(2)}, u32[]{:S(2)}) %collective-permute-start.8) | collective-permute-done | bytes 589856 | tf_op jit(solution)/shard_map/ppermute | solution.py:11
  138.8 2.0 %fusion.6 = f32[384,2,2,768]{3,0,2,1:T(8,128)S(1)} fusion(bf16[384,768,1,1]{1,0,3,2:T(8,128)(2,1)S(1)} %bitcast.394, bf16[1,1,2,2,768,768]{5,4,3,2,1,0:T(8,128)(2,1)S(1)} %bitcast.396), kind=kOutput, calls=%fused_computation.6 | convolution fusion | flops 1811939328 | bytes 10027008 | tf_op jit(solution)/shard_map/qe,mpef->mpqf/dot_general | solution.py:20
  142.3 1.1 copy.19
  (140 shorter events, 31.8 us)
Async XLA Ops:
  0.6 9.8 %copy-start.1 = (bf16[1,1,2,2,2,96,768]{6,5,4,3,2,1,0:T(8,128)(2,1)S(1)}, bf16[1,1,2,2,2,96,768]{6,5,4,3,2,1,0:T(8,128)(2,1)}, u32[]{:S(2)}) copy-start(bf16[1,1,2,2,2,96,768]{6,5,4,3,2,1,0:T(8,128)(2,1)} %param.55) | copy-start | bytes 3538948
  3.1 38.3 %collective-permute-start.13 = (bf16[2,2,96,768]{3,2,1,0:T(8,128)(2,1)}, bf16[2,2,96,768]{3,2,1,0:T(8,128)(2,1)}, u32[]{:S(2)}, u32[]{:S(2)}) collective-permute-start(bf16[2,2,96,768]{3,2,1,0:T(8,128)(2,1)} %get-tuple-element.379), channel_id=1, source_target_pairs={{0,3},{1,0},{2,1},{3,2},{4,7},{5,4},{6,5},{7,6},{8,11},{9,8},{10,9... | collective-permute-start | bytes 1769480 | tf_op jit(solution)/shard_map/ppermute | solution.py:11
  5.5 36.9 %collective-permute-start.12 = (bf16[2,2,96,768]{3,2,1,0:T(8,128)(2,1)}, bf16[2,2,96,768]{3,2,1,0:T(8,128)(2,1)}, u32[]{:S(2)}, u32[]{:S(2)}) collective-permute-start(bf16[2,2,96,768]{3,2,1,0:T(8,128)(2,1)} %get-tuple-element.378), channel_id=1, source_target_pairs={{0,28},{4,0},{8,4},{12,8},{16,12},{20,16},{24,20},{28,24},{1,29},{... | collective-permute-start | bytes 1769480 | tf_op jit(solution)/shard_map/ppermute | solution.py:11
  10.0 2.1 %copy-start.9 = (s32[2,3,2]{1,2,0:T(2,128)S(1)}, s32[2,3,2]{1,2,0:T(2,128)}, u32[]{:S(2)}) copy-start(s32[2,3,2]{1,2,0:T(2,128)} %param.61) | copy-start | bytes 148
  10.0 15.2 %copy-start = (bf16[1,1,2,2,2,96,768]{6,5,4,3,2,1,0:T(8,128)(2,1)S(1)}, bf16[1,1,2,2,2,96,768]{6,5,4,3,2,1,0:T(8,128)(2,1)}, u32[]{:S(2)}) copy-start(bf16[1,1,2,2,2,96,768]{6,5,4,3,2,1,0:T(8,128)(2,1)} %param.56) | copy-start | bytes 3538948
  10.0 26.6 %collective-permute-start.14 = (bf16[2,2,96,128]{3,2,1,0:T(8,128)(2,1)}, bf16[2,2,96,128]{3,2,1,0:T(8,128)(2,1)}, u32[]{:S(2)}, u32[]{:S(2)}) collective-permute-start(bf16[2,2,96,128]{3,2,1,0:T(8,128)(2,1)} %bitcast.96), channel_id=1, source_target_pairs={{0,3},{1,0},{2,1},{3,2},{4,7},{5,4},{6,5},{7,6},{8,11},{9,8},{10,9... | collective-permute-start | bytes 294920 | tf_op jit(solution)/shard_map/ppermute | solution.py:11
  11.5 48.8 %collective-permute-start.1 = (bf16[2,2,96,768]{3,2,1,0:T(8,128)(2,1)}, bf16[2,2,96,768]{3,2,1,0:T(8,128)(2,1)}, u32[]{:S(2)}, u32[]{:S(2)}) collective-permute-start(bf16[2,2,96,768]{3,2,1,0:T(8,128)(2,1)} %get-tuple-element.385), channel_id=1, source_target_pairs={{0,1},{1,2},{2,3},{3,0},{4,5},{5,6},{6,7},{7,4},{8,9},{9,10},{10,1... | collective-permute-start | bytes 1769480 | tf_op jit(solution)/shard_map/ppermute | solution.py:11
  11.6 25.0 %collective-permute-start.2 = (bf16[2,2,96,128]{3,2,1,0:T(8,128)(2,1)}, bf16[2,2,96,128]{3,2,1,0:T(8,128)(2,1)}, u32[]{:S(2)}, u32[]{:S(2)}) collective-permute-start(bf16[2,2,96,128]{3,2,1,0:T(8,128)(2,1)} %bitcast.16), channel_id=1, source_target_pairs={{0,1},{1,2},{2,3},{3,0},{4,5},{5,6},{6,7},{7,4},{8,9},{9,10},{10,1... | collective-permute-start | bytes 294920 | tf_op jit(solution)/shard_map/ppermute | solution.py:11
  26.9 5.9 %copy-start.10 = (s32[4]{0:T(128)S(1)}, s32[4]{0:T(128)}, u32[]{:S(2)}) copy-start(s32[4]{0:T(128)} %constant.563.clone.1) | copy-start | bytes 52
  36.6 25.5 %collective-permute-start = (bf16[2,2,96,768]{3,2,1,0:T(8,128)(2,1)}, bf16[2,2,96,768]{3,2,1,0:T(8,128)(2,1)S(1)}, u32[]{:S(2)}, u32[]{:S(2)}) collective-permute-start(bf16[2,2,96,768]{3,2,1,0:T(8,128)(2,1)} %get-tuple-element.384), channel_id=1, source_target_pairs={{0,4},{4,8},{8,12},{12,16},{16,20},{20,24},{24,28},{28,0},{1,5},{5... | collective-permute-start | bytes 1769480 | tf_op jit(solution)/shard_map/ppermute | solution.py:11
  36.6 12.6 %collective-permute-start.15 = (bf16[2,2,96,128]{3,2,1,0:T(8,128)(2,1)}, bf16[2,2,96,128]{3,2,1,0:T(8,128)(2,1)S(1)}, u32[]{:S(2)}, u32[]{:S(2)}) collective-permute-start(bf16[2,2,96,128]{3,2,1,0:T(8,128)(2,1)} %collective-permute-done.14), channel_id=1, source_target_pairs={{0,28},{4,0},{8,4},{12,8},{16,12},{20,16},{24,20},{28,24},{1,29},{... | collective-permute-start | bytes 294920 | tf_op jit(solution)/shard_map/ppermute | solution.py:11
  41.3 53.4 %collective-permute-start.3 = (bf16[2,2,96,128]{3,2,1,0:T(8,128)(2,1)}, bf16[2,2,96,128]{3,2,1,0:T(8,128)(2,1)S(1)}, u32[]{:S(2)}, u32[]{:S(2)}) collective-permute-start(bf16[2,2,96,128]{3,2,1,0:T(8,128)(2,1)} %collective-permute-done.2), channel_id=1, source_target_pairs={{0,4},{4,8},{8,12},{12,16},{16,20},{20,24},{24,28},{28,0},{1,5},{5... | collective-permute-start | bytes 294920 | tf_op jit(solution)/shard_map/ppermute | solution.py:11
  43.4 27.5 %slice-start = ((s8[4718592]{0:T(1024)(128)(4,1)}), s8[4194304]{0:T(1024)(128)(4,1)S(1)}, s32[]{:S(2)}) async-start(s8[4718592]{0:T(1024)(128)(4,1)} %bitcast.395), calls=%async_computation | async-start | bytes 8388608
  47.9 23.0 %slice-start.1 = ((s8[4718592]{0:T(1024)(128)(4,1)}), s8[524288]{0:T(1024)(128)(4,1)S(1)}, s32[]{:S(2)}) async-start(s8[4718592]{0:T(1024)(128)(4,1)} %bitcast.395), calls=%async_computation.1 | async-start | bytes 1048576
  50.2 8.6 %copy-start.6 = (bf16[2,2,96,128]{3,2,1,0:T(8,128)(2,1)S(1)}, bf16[2,2,96,128]{3,2,1,0:T(8,128)(2,1)}, u32[]{:S(2)}) copy-start(bf16[2,2,96,128]{3,2,1,0:T(8,128)(2,1)} %copy.38) | copy-start | bytes 294916
  50.3 20.5 %collective-permute-start.16 = (bf16[2,2,96,768]{3,2,1,0:T(8,128)(2,1)S(1)}, bf16[2,2,96,768]{3,2,1,0:T(8,128)(2,1)S(1)}, u32[]{:S(2)}, u32[]{:S(2)}) collective-permute-start(bf16[2,2,96,768]{3,2,1,0:T(8,128)(2,1)S(1)} %get-tuple-element.376), channel_id=1, source_target_pairs={{0,28},{4,0},{8,4},{12,8},{16,12},{20,16},{24,20},{28,24},{1,29},{... | collective-permute-start | bytes 1769480 | tf_op jit(solution)/shard_map/ppermute | solution.py:11
  58.0 12.8 %collective-permute-start.17 = (bf16[2,2,96,768]{3,2,1,0:T(8,128)(2,1)S(1)}, bf16[2,2,96,768]{3,2,1,0:T(8,128)(2,1)S(1)}, u32[]{:S(2)}, u32[]{:S(2)}) collective-permute-start(bf16[2,2,96,768]{3,2,1,0:T(8,128)(2,1)S(1)} %get-tuple-element.377), channel_id=1, source_target_pairs={{0,3},{1,0},{2,1},{3,2},{4,7},{5,4},{6,5},{7,6},{8,11},{9,8},{10,9... | collective-permute-start | bytes 1769480 | tf_op jit(solution)/shard_map/ppermute | solution.py:11
  60.3 7.0 %collective-permute-start.18 = (bf16[2,2,96,128]{3,2,1,0:T(8,128)(2,1)S(1)}, bf16[2,2,96,128]{3,2,1,0:T(8,128)(2,1)S(1)}, u32[]{:S(2)}, u32[]{:S(2)}) collective-permute-start(bf16[2,2,96,128]{3,2,1,0:T(8,128)(2,1)S(1)} %fusion.104), channel_id=1, source_target_pairs={{0,3},{1,0},{2,1},{3,2},{4,7},{5,4},{6,5},{7,6},{8,11},{9,8},{10,9... | collective-permute-start | bytes 294920 | tf_op jit(solution)/shard_map/ppermute | solution.py:11
  67.3 6.3 %collective-permute-start.19 = (bf16[2,2,96,128]{3,2,1,0:T(8,128)(2,1)S(1)}, bf16[2,2,96,128]{3,2,1,0:T(8,128)(2,1)S(1)}, u32[]{:S(2)}, u32[]{:S(2)}) collective-permute-start(bf16[2,2,96,128]{3,2,1,0:T(8,128)(2,1)S(1)} %collective-permute-done.18), channel_id=1, source_target_pairs={{0,28},{4,0},{8,4},{12,8},{16,12},{20,16},{24,20},{28,24},{1,29},{... | collective-permute-start | bytes 294920 | tf_op jit(solution)/shard_map/ppermute | solution.py:11
  74.6 17.2 %collective-permute-start.20 = (bf16[2,2,96,768]{3,2,1,0:T(8,128)(2,1)S(1)}, bf16[2,2,96,768]{3,2,1,0:T(8,128)(2,1)S(1)}, u32[]{:S(2)}, u32[]{:S(2)}) collective-permute-start(bf16[2,2,96,768]{3,2,1,0:T(8,128)(2,1)S(1)} %get-tuple-element.374), channel_id=1, source_target_pairs={{0,28},{4,0},{8,4},{12,8},{16,12},{20,16},{24,20},{28,24},{1,29},{... | collective-permute-start | bytes 1769480 | tf_op jit(solution)/shard_map/ppermute | solution.py:11
  81.8 10.0 %collective-permute-start.21 = (bf16[2,2,96,768]{3,2,1,0:T(8,128)(2,1)S(1)}, bf16[2,2,96,768]{3,2,1,0:T(8,128)(2,1)S(1)}, u32[]{:S(2)}, u32[]{:S(2)}) collective-permute-start(bf16[2,2,96,768]{3,2,1,0:T(8,128)(2,1)S(1)} %get-tuple-element.375), channel_id=1, source_target_pairs={{0,3},{1,0},{2,1},{3,2},{4,7},{5,4},{6,5},{7,6},{8,11},{9,8},{10,9... | collective-permute-start | bytes 1769480 | tf_op jit(solution)/shard_map/ppermute | solution.py:11
  82.6 7.8 %collective-permute-start.22 = (bf16[2,2,96,128]{3,2,1,0:T(8,128)(2,1)S(1)}, bf16[2,2,96,128]{3,2,1,0:T(8,128)(2,1)S(1)}, u32[]{:S(2)}, u32[]{:S(2)}) collective-permute-start(bf16[2,2,96,128]{3,2,1,0:T(8,128)(2,1)S(1)} %fusion.107), channel_id=1, source_target_pairs={{0,3},{1,0},{2,1},{3,2},{4,7},{5,4},{6,5},{7,6},{8,11},{9,8},{10,9... | collective-permute-start | bytes 294920 | tf_op jit(solution)/shard_map/ppermute | solution.py:11
  90.3 10.5 %collective-permute-start.23 = (bf16[2,2,96,128]{3,2,1,0:T(8,128)(2,1)S(1)}, bf16[2,2,96,128]{3,2,1,0:T(8,128)(2,1)S(1)}, u32[]{:S(2)}, u32[]{:S(2)}) collective-permute-start(bf16[2,2,96,128]{3,2,1,0:T(8,128)(2,1)S(1)} %collective-permute-done.22), channel_id=1, source_target_pairs={{0,28},{4,0},{8,4},{12,8},{16,12},{20,16},{24,20},{28,24},{1,29},{... | collective-permute-start | bytes 294920 | tf_op jit(solution)/shard_map/ppermute | solution.py:11
  96.9 19.3 %collective-permute-start.4 = (bf16[2,2,96,768]{3,2,1,0:T(8,128)(2,1)S(1)}, bf16[2,2,96,768]{3,2,1,0:T(8,128)(2,1)S(1)}, u32[]{:S(2)}, u32[]{:S(2)}) collective-permute-start(bf16[2,2,96,768]{3,2,1,0:T(8,128)(2,1)S(1)} %get-tuple-element.382), channel_id=1, source_target_pairs={{0,4},{4,8},{8,12},{12,16},{16,20},{20,24},{24,28},{28,0},{1,5},{5... | collective-permute-start | bytes 1769480 | tf_op jit(solution)/shard_map/ppermute | solution.py:11
  99.1 4.1 %collective-permute-start.6 = (bf16[2,2,96,128]{3,2,1,0:T(8,128)(2,1)S(1)}, bf16[2,2,96,128]{3,2,1,0:T(8,128)(2,1)S(1)}, u32[]{:S(2)}, u32[]{:S(2)}) collective-permute-start(bf16[2,2,96,128]{3,2,1,0:T(8,128)(2,1)S(1)} %fusion.98), channel_id=1, source_target_pairs={{0,1},{1,2},{2,3},{3,0},{4,5},{5,6},{6,7},{7,4},{8,9},{9,10},{10,1... | collective-permute-start | bytes 294920 | tf_op jit(solution)/shard_map/ppermute | solution.py:11
  100.2 16.1 %collective-permute-start.5 = (bf16[2,2,96,768]{3,2,1,0:T(8,128)(2,1)S(1)}, bf16[2,2,96,768]{3,2,1,0:T(8,128)(2,1)S(1)}, u32[]{:S(2)}, u32[]{:S(2)}) collective-permute-start(bf16[2,2,96,768]{3,2,1,0:T(8,128)(2,1)S(1)} %get-tuple-element.383), channel_id=1, source_target_pairs={{0,1},{1,2},{2,3},{3,0},{4,5},{5,6},{6,7},{7,4},{8,9},{9,10},{10,1... | collective-permute-start | bytes 1769480 | tf_op jit(solution)/shard_map/ppermute | solution.py:11
  103.2 15.8 %collective-permute-start.7 = (bf16[2,2,96,128]{3,2,1,0:T(8,128)(2,1)S(1)}, bf16[2,2,96,128]{3,2,1,0:T(8,128)(2,1)S(1)}, u32[]{:S(2)}, u32[]{:S(2)}) collective-permute-start(bf16[2,2,96,128]{3,2,1,0:T(8,128)(2,1)S(1)} %collective-permute-done.6), channel_id=1, source_target_pairs={{0,4},{4,8},{8,12},{12,16},{16,20},{20,24},{24,28},{28,0},{1,5},{5... | collective-permute-start | bytes 294920 | tf_op jit(solution)/shard_map/ppermute | solution.py:11
  119.9 10.4 %collective-permute-start.9 = (bf16[2,2,96,768]{3,2,1,0:T(8,128)(2,1)S(1)}, bf16[2,2,96,768]{3,2,1,0:T(8,128)(2,1)S(1)}, u32[]{:S(2)}, u32[]{:S(2)}) collective-permute-start(bf16[2,2,96,768]{3,2,1,0:T(8,128)(2,1)S(1)} %get-tuple-element.381), channel_id=1, source_target_pairs={{0,1},{1,2},{2,3},{3,0},{4,5},{5,6},{6,7},{7,4},{8,9},{9,10},{10,1... | collective-permute-start | bytes 1769480 | tf_op jit(solution)/shard_map/ppermute | solution.py:11
  120.0 18.6 %collective-permute-start.8 = (bf16[2,2,96,768]{3,2,1,0:T(8,128)(2,1)S(1)}, bf16[2,2,96,768]{3,2,1,0:T(8,128)(2,1)S(1)}, u32[]{:S(2)}, u32[]{:S(2)}) collective-permute-start(bf16[2,2,96,768]{3,2,1,0:T(8,128)(2,1)S(1)} %get-tuple-element.380), channel_id=1, source_target_pairs={{0,4},{4,8},{8,12},{12,16},{16,20},{20,24},{24,28},{28,0},{1,5},{5... | collective-permute-start | bytes 1769480 | tf_op jit(solution)/shard_map/ppermute | solution.py:11
  120.8 3.8 %copy-start.7 = (bf16[1,1,2,2,96,128]{5,4,3,2,1,0:T(8,128)(2,1)}, bf16[1,1,2,2,96,128]{5,4,3,2,1,0:T(8,128)(2,1)S(1)}, u32[]{:S(2)}) copy-start(bf16[1,1,2,2,96,128]{5,4,3,2,1,0:T(8,128)(2,1)S(1)} %fusion.115) | copy-start | bytes 294916
  121.5 8.9 %collective-permute-start.10 = (bf16[2,2,96,128]{3,2,1,0:T(8,128)(2,1)S(1)}, bf16[2,2,96,128]{3,2,1,0:T(8,128)(2,1)S(1)}, u32[]{:S(2)}, u32[]{:S(2)}) collective-permute-start(bf16[2,2,96,128]{3,2,1,0:T(8,128)(2,1)S(1)} %fusion.101), channel_id=1, source_target_pairs={{0,1},{1,2},{2,3},{3,0},{4,5},{5,6},{6,7},{7,4},{8,9},{9,10},{10,1... | collective-permute-start | bytes 294920 | tf_op jit(solution)/shard_map/ppermute | solution.py:11
  130.3 11.0 %collective-permute-start.11 = (bf16[2,2,96,128]{3,2,1,0:T(8,128)(2,1)S(1)}, bf16[2,2,96,128]{3,2,1,0:T(8,128)(2,1)S(1)}, u32[]{:S(2)}, u32[]{:S(2)}) collective-permute-start(bf16[2,2,96,128]{3,2,1,0:T(8,128)(2,1)S(1)} %collective-permute-done.10), channel_id=1, source_target_pairs={{0,4},{4,8},{8,12},{12,16},{16,20},{20,24},{24,28},{28,0},{1,5},{5... | collective-permute-start | bytes 294920 | tf_op jit(solution)/shard_map/ppermute | solution.py:11
  (5 other events, 5.6 us)
where the time goes:
time: 146 us; the launch traced here: 145 us
  waiting for transfers between devices  41.5 us (28%)
  starting transfers between devices  36.3 us (25%)
  other arithmetic  22.5 us (15%)
  local copies, waits for them, and re-layouts  17.4 us (12%)
  matrix products  14.5 us (10%)
  between operations  12.3 us (8%)
    ppermute x24, waiting for transfers between devices, from_behind(): lax.ppermute(array, axis, [(i, (i + by) % count) for i in range(count)])  41.5 us
    ppermute x24, starting transfers between devices, from_behind(): lax.ppermute(array, axis, [(i, (i + by) % count) for i in range(count)])  36.3 us
    dot_general x6, matrix products, trace_update(): jnp.einsum(form, stacked, cell_operators, preferred_element_type=jnp.floa...  14.5 us
    unnamed x36, local copies, waits for them, and re-layouts  8.28 us
    scatter x6, other arithmetic, sweep_tick(): corner_states = corner_states.at[chosen].set(new_corner)  5.46 us
    scatter x6, other arithmetic, sweep_tick(): states = states.at[:, chosen].set(jnp.stack([new_first, new_second]))  4.74 us
    another operation x6, other arithmetic, sweep_tick(): chosen = jnp.argmax((front_plan == klass).astype(jnp.int32))  4.04 us
    squeeze x6, local copies, waits for them, and re-layouts, sweep_tick(): first_send = states[0]  3.82 us
  transfers between devices with their start and end apart: 24, of which 8 were waited for; matrix products, arithmetic and copies ran while one was open for 32% of the time, Pallas kernels for 0%

commit v1 on v0

v1 whole, which is shorter than its diff:
```python
import functools

import jax
import jax.numpy as jnp
from jax import lax
from jax.experimental import pallas as pl
from jax.experimental.pallas import tpu as pltpu
from jax.sharding import PartitionSpec as P

ANY = pl.BlockSpec(memory_space=pl.ANY)
VMEM = pl.BlockSpec(memory_space=pltpu.VMEM)
SMEM = pl.BlockSpec(memory_space=pltpu.SMEM)
VMEM_LIMIT = 40 * 1024 * 1024


def chosen_at_start(roster_ref, direction, row_count, col_count):
    row = lax.axis_index("row")
    col = lax.axis_index("col")
    if direction:
        row = row_count - 1 - row
        col = col_count - 1 - col
    klass = lax.rem(row + col, 2)
    return jnp.where(roster_ref[direction, 0, 0] == klass, 0, 1)


def run_copies(copies):
    for copy in copies:
        copy.start()
    for copy in copies:
        copy.wait()


def select_kernel(
    counts, roster, se_edges, nw_edges, se_corners, nw_corners, *refs
):
    outs, sems = refs[:6], refs[6]
    copies = []
    for direction, (edges, corners) in enumerate(
        ((se_edges, se_corners), (nw_edges, nw_corners))
    ):
        mine = chosen_at_start(roster, direction, *counts)
        other = 1 - mine
        by_row, by_col, by_diagonal = outs[3 * direction : 3 * direction + 3]
        edge_width = edges.shape[-1]
        corner_width = corners.shape[-1]
        pairs = (
            (edges.at[0, other], by_row),
            (edges.at[1, other], by_col.at[:, :, pl.ds(0, edge_width)]),
            (corners.at[other], by_col.at[:, :, pl.ds(edge_width, corner_width)]),
            (corners.at[mine], by_diagonal),
        )
        for index, (source, target) in enumerate(pairs):
            copies.append(
                pltpu.make_async_copy(source, target, sems.at[direction, index])
            )
    run_copies(copies)


def select_initial(counts, roster, se_edges, nw_edges, se_corners, nw_corners):
    _, _, parts, shots, edge_width = se_edges.shape
    corner_width = se_corners.shape[-1]
    kind = se_edges.dtype
    shapes = [
        jax.ShapeDtypeStruct((parts, shots, edge_width), kind),
        jax.ShapeDtypeStruct((parts, shots, edge_width + corner_width), kind),
        jax.ShapeDtypeStruct((parts, shots, corner_width), kind),
    ] * 2
    return pl.pallas_call(
        functools.partial(select_kernel, counts),
        out_shape=shapes,
        in_specs=[SMEM] + [ANY] * 4,
        out_specs=[ANY] * 6,
        scratch_shapes=[pltpu.SemaphoreType.DMA((2, 4))],
        name="select_initial",
    )(roster, se_edges, nw_edges, se_corners, nw_corners)


def load_kernel(operators, plain, flipped, sems):
    count = operators.shape[0]
    edge_width = operators.shape[1]
    copies = [
        pltpu.make_async_copy(
            operators.at[i], plain.at[pl.ds(i * edge_width, edge_width)], sems.at[i]
        )
        for i in range(count)
    ]
    for copy in copies:
        copy.start()
    for i in range(count):
        copies[i].wait()
        rows = pl.ds(i * edge_width, edge_width)
        flipped[rows, :] = plain[rows, :].T


def load_operators(operators):
    count = operators.shape[0] * operators.shape[1]
    edge_width = operators.shape[-1]
    shape = (count * edge_width, edge_width)
    return pl.pallas_call(
        load_kernel,
        out_shape=[pltpu.VMEM(shape, operators.dtype), pltpu.VMEM(shape, operators.dtype)],
        in_specs=[ANY],
        out_specs=[VMEM, VMEM],
        scratch_shapes=[pltpu.SemaphoreType.DMA((count,))],
        compiler_params=pltpu.CompilerParams(vmem_limit_bytes=VMEM_LIMIT),
        name="load_operators",
    )(operators.reshape(count, edge_width, edge_width))


def tick_kernel(
    counts, direction, tick, last, edge_width, corner_width, roster, first_in, second_in,
    corner_in, sources, operators, *refs
):
    if last:
        old_first, old_second, old_corner, edges_out, corners_out = refs[:5]
        refs = refs[5:]
    else:
        first_out, second_out, corner_out = refs[:3]
        refs = refs[3:]
    first_v, second_v, corner_v, source_v, left, first_o, second_o, corner_o, sems = refs
    parts, shots, _ = source_v.shape
    rows = parts * shots
    chosen = chosen_at_start(roster, direction, *counts)
    if tick % 2:
        chosen = 1 - chosen
    edge_part = pl.ds(0, edge_width)
    corner_part = pl.ds(edge_width, corner_width)

    first_copy = pltpu.make_async_copy(first_in, first_v, sems.at[0])
    second_copy = pltpu.make_async_copy(second_in, second_v, sems.at[1])
    source_copy = pltpu.make_async_copy(sources.at[chosen], source_v, sems.at[2])
    inputs = [first_copy, second_copy, source_copy]
    if tick == 0:
        corner_copy = pltpu.make_async_copy(corner_in, corner_v, sems.at[3])
        inputs.append(corner_copy)
    for copy in inputs:
        copy.start()
    history = []
    if last:
        history = [
            pltpu.make_async_copy(
                old_first.at[:, :, edge_part], edges_out.at[0, 1 - chosen], sems.at[4]
            ),
            pltpu.make_async_copy(
                old_second.at[:, :, edge_part], edges_out.at[1, 1 - chosen], sems.at[5]
            ),
            pltpu.make_async_copy(old_corner, corners_out.at[1 - chosen], sems.at[6]),
        ]
        for copy in history:
            copy.start()
    for copy in inputs:
        copy.wait()

    for place, ref in ((0, first_v), (2, second_v)):
        other_place = 2 - place
        real = ref[0, :, edge_part]
        imag = ref[1, :, edge_part]
        minus = -imag
        for slot, block in ((place, 0), (other_place, 1)):
            row = block * rows
            column = slot * edge_width
            left[pl.ds(row, shots), pl.ds(column, edge_width)] = real
            left[pl.ds(row + shots, shots), pl.ds(column, edge_width)] = imag
            left[pl.ds(row, shots), pl.ds(column + edge_width, edge_width)] = minus
            left[pl.ds(row + shots, shots), pl.ds(column + edge_width, edge_width)] = real

    if tick == 0:
        corner = corner_v[...]
    else:
        corner = first_v[:, :, corner_part]
    corner = corner.astype(jnp.float32).reshape(rows, corner_width)
    if not last and first_o.shape[-1] > edge_width:
        first_o[:, :, corner_part] = second_v[:, :, corner_part]

    tile = edge_width // 3 if edge_width % 3 == 0 else edge_width
    steps = edge_width // tile
    for step in range(steps):
        at = pl.ds(step * tile, tile)
        value = jnp.dot(left[...], operators[:, at], preferred_element_type=jnp.float32)
        source = source_v[:, :, at].astype(jnp.float32).reshape(rows, tile)
        first = value[:rows] + source
        second = value[rows:] + source
        low, high = step == 0, step == steps - 1
        adds, gives = (high, low) if direction else (low, high)

        def at_corner(array, flag):
            if flag:
                return array[:, tile - corner_width :]
            return array[:, :corner_width]

        if adds:
            widths = ((0, 0), (tile - corner_width, 0) if direction else (0, tile - corner_width))
            padded = jnp.pad(corner, widths)
            first = first + padded
            second = second + padded
        if gives:
            value = 0.5 * (at_corner(first, not direction) + at_corner(second, not direction))
            value = value.astype(corner_o.dtype).reshape(parts, shots, corner_width)
            corner_o[...] = value
            if not last and second_o.shape[-1] > edge_width:
                second_o[:, :, corner_part] = value
        first_o[:, :, at] = first.astype(first_o.dtype).reshape(parts, shots, tile)
        second_o[:, :, at] = second.astype(second_o.dtype).reshape(parts, shots, tile)

    if last:
        copies = [
            pltpu.make_async_copy(first_o, edges_out.at[0, chosen], sems.at[7]),
            pltpu.make_async_copy(second_o, edges_out.at[1, chosen], sems.at[8]),
            pltpu.make_async_copy(corner_o, corners_out.at[chosen], sems.at[9]),
        ]
    else:
        copies = [
            pltpu.make_async_copy(first_o, first_out, sems.at[7]),
            pltpu.make_async_copy(second_o, second_out, sems.at[8]),
            pltpu.make_async_copy(corner_o, corner_out, sems.at[9]),
        ]
    run_copies(copies)
    for copy in history:
        copy.wait()


def tick_update(
    counts, direction, tick, ticks, roster, first_in, second_in, corner_in, sources, operators,
    history,
):
    batches, parts, shots, edge_width = sources.shape
    corner_width = corner_in.shape[-1]
    kind = sources.dtype
    last = tick == ticks - 1
    first_width = edge_width + (0 if last else corner_width)
    second_width = edge_width + (0 if tick >= ticks - 2 else corner_width)
    shapes = [
        jax.ShapeDtypeStruct((parts, shots, first_width), kind),
        jax.ShapeDtypeStruct((parts, shots, second_width), kind),
        jax.ShapeDtypeStruct((parts, shots, corner_width), kind),
    ]
    if last:
        outs = [
            jax.ShapeDtypeStruct((2, batches, parts, shots, edge_width), kind),
            jax.ShapeDtypeStruct((batches, parts, shots, corner_width), kind),
        ]
    else:
        outs = shapes
    operands = [roster, first_in, second_in, corner_in, sources, operators]
    if last:
        operands += list(history)
    rows = parts * shots
    return pl.pallas_call(
        functools.partial(tick_kernel, counts, direction, tick, last, edge_width, corner_width),
        out_shape=outs,
        in_specs=[SMEM, ANY, ANY, ANY, ANY, VMEM] + [ANY] * (len(operands) - 6),
        out_specs=[ANY] * len(outs),
        scratch_shapes=[
            pltpu.VMEM(first_in.shape, kind),
            pltpu.VMEM(second_in.shape, kind),
            pltpu.VMEM((parts, shots, corner_width), kind),
            pltpu.VMEM((parts, shots, edge_width), kind),
            pltpu.VMEM((2 * rows, 4 * edge_width), kind),
            pltpu.VMEM(shapes[0].shape, kind),
            pltpu.VMEM(shapes[1].shape, kind),
            pltpu.VMEM(shapes[2].shape, kind),
            pltpu.SemaphoreType.DMA((10,)),
        ],
        compiler_params=pltpu.CompilerParams(vmem_limit_bytes=VMEM_LIMIT),
        cost_estimate=pl.CostEstimate(
            flops=2 * 2 * rows * 4 * edge_width * edge_width,
            bytes_accessed=6 * rows * edge_width * 2,
            transcendentals=0,
        ),
        name="tick" + str(tick) + ("nw" if direction else "se"),
    )(*operands)


def neighbours(counts, row_step, col_step):
    row_count, col_count = counts
    return [
        (r * col_count + c, (r + row_step) % row_count * col_count + (c + col_step) % col_count)
        for r in range(row_count)
        for c in range(col_count)
    ]


def move(array, counts, row_step, col_step):
    return lax.ppermute(array, ("row", "col"), neighbours(counts, row_step, col_step))


def shards(
    southeast_edges, northwest_edges, southeast_corners, northwest_corners, operators, sources,
    roster,
):
    counts = (lax.axis_size("row"), lax.axis_size("col"))
    ticks = roster.shape[1]
    local_sources = sources[0, 0]
    picked = select_initial(
        counts, roster, southeast_edges[0, 0], northwest_edges[0, 0], southeast_corners[0, 0],
        northwest_corners[0, 0],
    )
    prepared = load_operators(operators[0, 0])
    sends = [picked[:3], picked[3:]]
    history = [None, None]
    outs = [None, None]
    corners = [None, None]
    for tick in range(ticks):
        arrived = []
        for direction in range(2):
            by = -1 if direction else 1
            first, second, corner = sends[direction]
            first_in = move(first, counts, by, 0)
            second_in = move(second, counts, 0, by)
            if tick == 0:
                corners[direction] = move(corner, counts, by, by)
            arrived.append((first_in, second_in))
        for direction in range(2):
            first_in, second_in = arrived[direction]
            done = tick_update(
                counts, direction, tick, ticks, roster, first_in, second_in, corners[direction],
                local_sources, prepared[direction], history[direction],
            )
            if tick == ticks - 1:
                outs[direction] = done
            else:
                sends[direction] = done
                history[direction] = done
    return (
        outs[0][0][None, None],
        outs[1][0][None, None],
        outs[0][1][None, None],
        outs[1][1][None, None],
    )


def solution(mesh):
    edges = P("row", "col", None, None, None, None, None)
    corners = P("row", "col", None, None, None, None)
    return jax.shard_map(
        shards,
        mesh=mesh,
        in_specs=(edges, edges, corners, corners, corners, corners, P()),
        out_specs=(edges, edges, corners, corners),
        check_vma=False,
    )
```

time: 146 us -> 114 us (0.78)
  the two profiles are of different devices: /device:TPU:0 before, /device:TPU:8 now
where the time goes in v1:
time: 114 us
  Pallas kernels  67.9 us (60%)
  waiting for transfers between devices  28.4 us (25%)
  starting transfers between devices  13.1 us (11%)
  local copies, waits for them, and re-layouts  3.71 us (3%)
    pallas_call x1, Pallas kernels, select_initial(): pl.pallas_call(functools.partial(select_kernel, counts), out_shape=shapes...  43.6 us
    ppermute x14, waiting for transfers between devices, move(): lax.ppermute(array, ('row', 'col'), neighbours(counts, row_step, col_step))  28.4 us
    pallas_call x6, Pallas kernels, tick_update(): pl.pallas_call(functools.partial(tick_kernel, counts, direction, tick, la...  21.9 us
    ppermute x14, starting transfers between devices, move(): lax.ppermute(array, ('row', 'col'), neighbours(counts, row_step, col_step))  13.1 us
    unnamed x9, local copies, waits for them, and re-layouts  3.71 us
    pallas_call x1, Pallas kernels, load_operators(): pl.pallas_call(load_kernel, out_shape=[pltpu.VMEM(shape, operators.dtype)...  2.43 us
  transfers between devices with their start and end apart: 14, of which 4 were waited for; matrix products, arithmetic and copies ran while one was open for 0% of the time, Pallas kernels for 18%

profile of v1, /device:TPU:8, one launch (start us, length us, event | category | flops | bytes accessed | tf_op | source)
XLA Modules:
  0.0 113.9 jit_solution(8007222087806495288)
XLA Ops:
  0.6 1.4 %copy.14.roster = s32[2,3,2]{2,1,0:T(4,128)} copy(s32[2,3,2]{1,2,0:T(2,128)} %param.13) | data formatting | bytes 96 | tf_op args[6]
  2.0 43.6 %select_initial.1 = (bf16[2,96,768]{2,1,0:T(8,128)(2,1)}, bf16[2,96,896]{2,1,0:T(8,128)(2,1)}, bf16[2,96,128]{2,1,0:T(8,128)(2,1)}, bf16[2,96,768]{2,1,0:T(8,128...) custom-call(s32[2,3,2]{2,1,0:T(4,128)} %copy.14.roster, bf16[2,2,2,96,768]{4,3,2,1,0:T(8,128)(2,1)} %bitcast.17, ...), custom_call_target="tpu_custom_call" | custom-call | tf_op jit(solution)/shard_map/select_initial/pallas_call | solution.py:68
  45.6 1.0 collective-permute-start.8
  46.6 1.4 %collective-permute-start.7 = (bf16[2,96,768]{2,1,0:T(8,128)(2,1)}, bf16[2,96,768]{2,1,0:T(8,128)(2,1)S(1)}, u32[]{:S(2)}, u32[]{:S(2)}) collective-permute-start(bf16[2,96,768]{2,1,0:T(8,128)(2,1)} %get-tuple-element.36), channel_id=1, source_target_pairs={{0,28},{1,29},{2,30},{3,31},{4,0},{5,1},{6,2},{7,3},{8,4},{9,5},{1... | collective-permute-start | bytes 884744 | tf_op jit(solution)/shard_map/ppermute | solution.py:284
  48.0 0.0 collective-permute-start.1
  48.0 0.6 collective-permute-start
  48.6 3.2 %collective-permute-start.9 = (bf16[2,96,128]{2,1,0:T(8,128)(2,1)}, bf16[2,96,128]{2,1,0:T(8,128)(2,1)S(1)}, u32[]{:S(2)}, u32[]{:S(2)}) collective-permute-start(bf16[2,96,128]{2,1,0:T(8,128)(2,1)} %get-tuple-element.38), channel_id=1, source_target_pairs={{0,31},{1,28},{2,29},{3,30},{4,3},{5,0},{6,1},{7,2},{8,7},{9,4},{1... | collective-permute-start | bytes 147464 | tf_op jit(solution)/shard_map/ppermute | solution.py:284
  51.8 2.3 %copy-done = bf16[1,1,2,2,768,768]{5,4,3,2,1,0:T(8,128)(2,1)S(1)} copy-done((bf16[1,1,2,2,768,768]{5,4,3,2,1,0:T(8,128)(2,1)S(1)}, bf16[1,1,2,2,768,768]{5,4,3,2,1,0:T(8,128)(2,1)}, u32[]{:S(2)}) %copy-start) | copy-done | bytes 4718616
  54.2 2.4 %load_operators.1 = (bf16[3072,768]{1,0:T(8,128)(2,1)S(1)}, bf16[3072,768]{1,0:T(8,128)(2,1)S(1)}) custom-call(bf16[4,768,768]{2,1,0:T(8,128)(2,1)S(1)} %bitcast.10), custom_call_target="tpu_custom_call" | custom-call | tf_op jit(solution)/shard_map/load_operators/pallas_call | solution.py:99
  56.6 4.6 %collective-permute-done.9.corner_in = bf16[2,96,128]{2,1,0:T(8,128)(2,1)S(1)} collective-permute-done((bf16[2,96,128]{2,1,0:T(8,128)(2,1)}, bf16[2,96,128]{2,1,0:T(8,128)(2,1)S(1)}, u32[]{:S(2)}, u32[]{:S(2)}) %collective-permute-start.9) | collective-permute-done | bytes 49184 | tf_op jit(solution)/shard_map/ppermute | solution.py:284
  61.2 0.0 collective-permute-start.2
  61.2 0.9 collective-permute-done.7.first_in
  62.1 0.0 collective-permute-done.8.second_in
  62.1 3.9 %tick0nw.1 = (bf16[2,96,896]{2,1,0:T(8,128)(2,1)S(1)}, bf16[2,96,896]{2,1,0:T(8,128)(2,1)S(1)}, bf16[2,96,128]{2,1,0:T(8,128)(2,1)}) custom-call(s32[2,3,2]{2,1,0:T(4,128)S(1)} %copy-done.1, bf16[2,96,768]{2,1,0:T(8,128)(2,1)S(1)} %collective-permute-done.7.first_in, bf16[2,96,896]{2,1,0:T(8,128)(2,1)S(1)} %collective-permute-done.8.second_in, ...), custom_call_target="tpu_custom_call" | custom-call | flops 1811939328 | bytes 1769472 | tf_op jit(solution)/shard_map/tick0nw/pallas_call | solution.py:248
  66.1 3.9 %collective-permute-start.10 = (bf16[2,96,896]{2,1,0:T(8,128)(2,1)S(1)}, bf16[2,96,896]{2,1,0:T(8,128)(2,1)S(1)}, u32[]{:S(2)}, u32[]{:S(2)}) collective-permute-start(bf16[2,96,896]{2,1,0:T(8,128)(2,1)S(1)} %get-tuple-element.40), channel_id=1, source_target_pairs={{0,28},{1,29},{2,30},{3,31},{4,0},{5,1},{6,2},{7,3},{8,4},{9,5},{1... | collective-permute-start | bytes 1032200 | tf_op jit(solution)/shard_map/ppermute | solution.py:284
  70.0 0.0 collective-permute-done.first_in
  70.0 3.9 %tick0se.1 = (bf16[2,96,896]{2,1,0:T(8,128)(2,1)S(1)}, bf16[2,96,896]{2,1,0:T(8,128)(2,1)S(1)}, bf16[2,96,128]{2,1,0:T(8,128)(2,1)}) custom-call(s32[2,3,2]{2,1,0:T(4,128)S(1)} %copy-done.1, bf16[2,96,768]{2,1,0:T(8,128)(2,1)S(1)} %collective-permute-done.first_in, bf16[2,96,896]{2,1,0:T(8,128)(2,1)S(1)} %collective-permute-done.1.second_in, ...), custom_call_target="tpu_custom_call" | custom-call | flops 1811939328 | bytes 1769472 | tf_op jit(solution)/shard_map/tick0se/pallas_call | solution.py:248
  73.9 0.3 collective-permute-start.3
  74.2 0.4 collective-permute-start.4
  74.5 11.4 %collective-permute-done.10.first_in = bf16[2,96,896]{2,1,0:T(8,128)(2,1)S(1)} collective-permute-done((bf16[2,96,896]{2,1,0:T(8,128)(2,1)S(1)}, bf16[2,96,896]{2,1,0:T(8,128)(2,1)S(1)}, u32[]{:S(2)}, u32[]{:S(2)}) %collective-permute-start.10) | collective-permute-done | bytes 344096 | tf_op jit(solution)/shard_map/ppermute | solution.py:284
  85.9 0.0 collective-permute-done.11.second_in
  85.9 3.3 %tick1nw.1 = (bf16[2,96,896]{2,1,0:T(8,128)(2,1)S(1)}, bf16[2,96,768]{2,1,0:T(8,128)(2,1)S(1)}, bf16[2,96,128]{2,1,0:T(8,128)(2,1)S(1)}) custom-call(s32[2,3,2]{2,1,0:T(4,128)S(1)} %copy-done.1, bf16[2,96,896]{2,1,0:T(8,128)(2,1)S(1)} %collective-permute-done.10.first_in, bf16[2,96,896]{2,1,0:T(8,128)(2,1)S(1)} %collective-permute-done.11.second_in, ...), custom_call_target="tpu_custom_call" | custom-call | flops 1811939328 | bytes 1769472 | tf_op jit(solution)/shard_map/tick1nw/pallas_call | solution.py:248
  89.2 0.1 collective-permute-start.12
  89.3 0.1 collective-permute-start.13
  89.4 0.0 collective-permute-done.3.first_in
  89.4 3.3 %tick1se.1 = (bf16[2,96,896]{2,1,0:T(8,128)(2,1)S(1)}, bf16[2,96,768]{2,1,0:T(8,128)(2,1)S(1)}, bf16[2,96,128]{2,1,0:T(8,128)(2,1)S(1)}) custom-call(s32[2,3,2]{2,1,0:T(4,128)S(1)} %copy-done.1, bf16[2,96,896]{2,1,0:T(8,128)(2,1)S(1)} %collective-permute-done.3.first_in, bf16[2,96,896]{2,1,0:T(8,128)(2,1)S(1)} %collective-permute-done.4.second_in, ...), custom_call_target="tpu_custom_call" | custom-call | flops 1811939328 | bytes 1769472 | tf_op jit(solution)/shard_map/tick1se/pallas_call | solution.py:248
  92.7 2.0 %collective-permute-start.5 = (bf16[2,96,896]{2,1,0:T(8,128)(2,1)S(1)}, bf16[2,96,896]{2,1,0:T(8,128)(2,1)S(1)}, u32[]{:S(2)}, u32[]{:S(2)}) collective-permute-start(bf16[2,96,896]{2,1,0:T(8,128)(2,1)S(1)} %get-tuple-element.32.refs_0_), channel_id=1, source_target_pairs={{0,4},{1,5},{2,6},{3,7},{4,8},{5,9},{6,10},{7,11},{8,12},{9,13},{1... | collective-permute-start | bytes 1032200 | tf_op jit(solution)/shard_map/ppermute | solution.py:284
  94.7 0.2 collective-permute-start.6
  94.9 0.0 collective-permute-done.13.second_in
  94.9 11.4 %collective-permute-done.12.first_in = bf16[2,96,896]{2,1,0:T(8,128)(2,1)S(1)} collective-permute-done((bf16[2,96,896]{2,1,0:T(8,128)(2,1)S(1)}, bf16[2,96,896]{2,1,0:T(8,128)(2,1)S(1)}, u32[]{:S(2)}, u32[]{:S(2)}) %collective-permute-start.12) | collective-permute-done | bytes 344096 | tf_op jit(solution)/shard_map/ppermute | solution.py:284
  106.3 3.7 %tick2nw.1 = (bf16[2,2,2,96,768]{4,3,2,1,0:T(8,128)(2,1)}, bf16[2,2,96,128]{3,2,1,0:T(8,128)(2,1)}) custom-call(s32[2,3,2]{2,1,0:T(4,128)S(1)} %copy-done.1, bf16[2,96,896]{2,1,0:T(8,128)(2,1)S(1)} %collective-permute-done.12.first_in, bf16[2,96,768]{2,1,0:T(8,128)(2,1)S(1)} %collective-permute-done.13.second_in, ...), custom_call_target="tpu_custom_call" | custom-call | flops 1811939328 | bytes 1769472 | tf_op jit(solution)/shard_map/tick2nw/pallas_call | solution.py:248
  110.1 3.8 %tick2se.1 = (bf16[2,2,2,96,768]{4,3,2,1,0:T(8,128)(2,1)}, bf16[2,2,96,128]{3,2,1,0:T(8,128)(2,1)}) custom-call(s32[2,3,2]{2,1,0:T(4,128)S(1)} %copy-done.1, bf16[2,96,896]{2,1,0:T(8,128)(2,1)S(1)} %collective-permute-done.5.first_in, bf16[2,96,768]{2,1,0:T(8,128)(2,1)S(1)} %collective-permute-done.6.second_in, ...), custom_call_target="tpu_custom_call" | custom-call | flops 1811939328 | bytes 1769472 | tf_op jit(solution)/shard_map/tick2se/pallas_call | solution.py:248
  (13 shorter events, 0.0 us)
Async XLA Ops:
  45.6 16.5 %collective-permute-start.8 = (bf16[2,96,896]{2,1,0:T(8,128)(2,1)}, bf16[2,96,896]{2,1,0:T(8,128)(2,1)S(1)}, u32[]{:S(2)}, u32[]{:S(2)}) collective-permute-start(bf16[2,96,896]{2,1,0:T(8,128)(2,1)} %get-tuple-element.37), channel_id=1, source_target_pairs={{0,3},{1,0},{2,1},{3,2},{4,7},{5,4},{6,5},{7,6},{8,11},{9,8},{10,9... | collective-permute-start | bytes 1032200 | tf_op jit(solution)/shard_map/ppermute | solution.py:284
  46.6 15.5 %collective-permute-start.7 = (bf16[2,96,768]{2,1,0:T(8,128)(2,1)}, bf16[2,96,768]{2,1,0:T(8,128)(2,1)S(1)}, u32[]{:S(2)}, u32[]{:S(2)}) collective-permute-start(bf16[2,96,768]{2,1,0:T(8,128)(2,1)} %get-tuple-element.36), channel_id=1, source_target_pairs={{0,28},{1,29},{2,30},{3,31},{4,0},{5,1},{6,2},{7,3},{8,4},{9,5},{1... | collective-permute-start | bytes 884744 | tf_op jit(solution)/shard_map/ppermute | solution.py:284
  48.0 22.0 %collective-permute-start.1 = (bf16[2,96,896]{2,1,0:T(8,128)(2,1)}, bf16[2,96,896]{2,1,0:T(8,128)(2,1)S(1)}, u32[]{:S(2)}, u32[]{:S(2)}) collective-permute-start(bf16[2,96,896]{2,1,0:T(8,128)(2,1)} %get-tuple-element.27), channel_id=1, source_target_pairs={{0,1},{1,2},{2,3},{3,0},{4,5},{5,6},{6,7},{7,4},{8,9},{9,10},{10,1... | collective-permute-start | bytes 1032200 | tf_op jit(solution)/shard_map/ppermute | solution.py:284
  48.0 22.0 %collective-permute-start = (bf16[2,96,768]{2,1,0:T(8,128)(2,1)}, bf16[2,96,768]{2,1,0:T(8,128)(2,1)S(1)}, u32[]{:S(2)}, u32[]{:S(2)}) collective-permute-start(bf16[2,96,768]{2,1,0:T(8,128)(2,1)} %get-tuple-element.26), channel_id=1, source_target_pairs={{0,4},{1,5},{2,6},{3,7},{4,8},{5,9},{6,10},{7,11},{8,12},{9,13},{1... | collective-permute-start | bytes 884744 | tf_op jit(solution)/shard_map/ppermute | solution.py:284
  48.6 12.5 %collective-permute-start.9 = (bf16[2,96,128]{2,1,0:T(8,128)(2,1)}, bf16[2,96,128]{2,1,0:T(8,128)(2,1)S(1)}, u32[]{:S(2)}, u32[]{:S(2)}) collective-permute-start(bf16[2,96,128]{2,1,0:T(8,128)(2,1)} %get-tuple-element.38), channel_id=1, source_target_pairs={{0,31},{1,28},{2,29},{3,30},{4,3},{5,0},{6,1},{7,2},{8,7},{9,4},{1... | collective-permute-start | bytes 147464 | tf_op jit(solution)/shard_map/ppermute | solution.py:284
  51.8 2.3 %copy-start = (bf16[1,1,2,2,768,768]{5,4,3,2,1,0:T(8,128)(2,1)S(1)}, bf16[1,1,2,2,768,768]{5,4,3,2,1,0:T(8,128)(2,1)}, u32[]{:S(2)}) copy-start(bf16[1,1,2,2,768,768]{5,4,3,2,1,0:T(8,128)(2,1)} %param.11) | copy-start | bytes 14155780
  54.2 7.0 %copy-start.3 = (bf16[2,96,128]{2,1,0:T(8,128)(2,1)S(1)}, bf16[2,96,128]{2,1,0:T(8,128)(2,1)}, u32[]{:S(2)}) copy-start(bf16[2,96,128]{2,1,0:T(8,128)(2,1)} %get-tuple-element.28) | copy-start | bytes 147460
  54.2 8.0 %copy-start.1 = (s32[2,3,2]{2,1,0:T(4,128)S(1)}, s32[2,3,2]{2,1,0:T(4,128)}, u32[]{:S(2)}) copy-start(s32[2,3,2]{2,1,0:T(4,128)} %copy.14.roster) | copy-start | bytes 148
  54.2 8.0 %copy-start.2 = (bf16[1,1,2,2,96,768]{5,4,3,2,1,0:T(8,128)(2,1)S(1)}, bf16[1,1,2,2,96,768]{5,4,3,2,1,0:T(8,128)(2,1)}, u32[]{:S(2)}) copy-start(bf16[1,1,2,2,96,768]{5,4,3,2,1,0:T(8,128)(2,1)} %param.12) | copy-start | bytes 1769476
  61.2 8.8 %collective-permute-start.2 = (bf16[2,96,128]{2,1,0:T(8,128)(2,1)S(1)}, bf16[2,96,128]{2,1,0:T(8,128)(2,1)S(1)}, u32[]{:S(2)}, u32[]{:S(2)}) collective-permute-start(bf16[2,96,128]{2,1,0:T(8,128)(2,1)S(1)} %copy-done.3), channel_id=1, source_target_pairs={{0,5},{1,6},{2,7},{3,4},{4,9},{5,10},{6,11},{7,8},{8,13},{9,14},{1... | collective-permute-start | bytes 147464 | tf_op jit(solution)/shard_map/ppermute | solution.py:284
  66.1 19.8 %collective-permute-start.10 = (bf16[2,96,896]{2,1,0:T(8,128)(2,1)S(1)}, bf16[2,96,896]{2,1,0:T(8,128)(2,1)S(1)}, u32[]{:S(2)}, u32[]{:S(2)}) collective-permute-start(bf16[2,96,896]{2,1,0:T(8,128)(2,1)S(1)} %get-tuple-element.40), channel_id=1, source_target_pairs={{0,28},{1,29},{2,30},{3,31},{4,0},{5,1},{6,2},{7,3},{8,4},{9,5},{1... | collective-permute-start | bytes 1032200 | tf_op jit(solution)/shard_map/ppermute | solution.py:284
  70.0 16.0 %collective-permute-start.11 = (bf16[2,96,896]{2,1,0:T(8,128)(2,1)S(1)}, bf16[2,96,896]{2,1,0:T(8,128)(2,1)S(1)}, u32[]{:S(2)}, u32[]{:S(2)}) collective-permute-start(bf16[2,96,896]{2,1,0:T(8,128)(2,1)S(1)} %get-tuple-element.41), channel_id=1, source_target_pairs={{0,3},{1,0},{2,1},{3,2},{4,7},{5,4},{6,5},{7,6},{8,11},{9,8},{10,9... | collective-permute-start | bytes 1032200 | tf_op jit(solution)/shard_map/ppermute | solution.py:284
  73.9 15.5 %collective-permute-start.3 = (bf16[2,96,896]{2,1,0:T(8,128)(2,1)S(1)}, bf16[2,96,896]{2,1,0:T(8,128)(2,1)S(1)}, u32[]{:S(2)}, u32[]{:S(2)}) collective-permute-start(bf16[2,96,896]{2,1,0:T(8,128)(2,1)S(1)} %get-tuple-element.30), channel_id=1, source_target_pairs={{0,4},{1,5},{2,6},{3,7},{4,8},{5,9},{6,10},{7,11},{8,12},{9,13},{1... | collective-permute-start | bytes 1032200 | tf_op jit(solution)/shard_map/ppermute | solution.py:284
  74.2 15.2 %collective-permute-start.4 = (bf16[2,96,896]{2,1,0:T(8,128)(2,1)S(1)}, bf16[2,96,896]{2,1,0:T(8,128)(2,1)S(1)}, u32[]{:S(2)}, u32[]{:S(2)}) collective-permute-start(bf16[2,96,896]{2,1,0:T(8,128)(2,1)S(1)} %get-tuple-element.31), channel_id=1, source_target_pairs={{0,1},{1,2},{2,3},{3,0},{4,5},{5,6},{6,7},{7,4},{8,9},{9,10},{10,1... | collective-permute-start | bytes 1032200 | tf_op jit(solution)/shard_map/ppermute | solution.py:284
  89.2 17.1 %collective-permute-start.12 = (bf16[2,96,896]{2,1,0:T(8,128)(2,1)S(1)}, bf16[2,96,896]{2,1,0:T(8,128)(2,1)S(1)}, u32[]{:S(2)}, u32[]{:S(2)}) collective-permute-start(bf16[2,96,896]{2,1,0:T(8,128)(2,1)S(1)} %get-tuple-element.42.refs_0_), channel_id=1, source_target_pairs={{0,28},{1,29},{2,30},{3,31},{4,0},{5,1},{6,2},{7,3},{8,4},{9,5},{1... | collective-permute-start | bytes 1032200 | tf_op jit(solution)/shard_map/ppermute | solution.py:284
  89.3 5.6 %collective-permute-start.13 = (bf16[2,96,768]{2,1,0:T(8,128)(2,1)S(1)}, bf16[2,96,768]{2,1,0:T(8,128)(2,1)S(1)}, u32[]{:S(2)}, u32[]{:S(2)}) collective-permute-start(bf16[2,96,768]{2,1,0:T(8,128)(2,1)S(1)} %get-tuple-element.43.refs_1_), channel_id=1, source_target_pairs={{0,3},{1,0},{2,1},{3,2},{4,7},{5,4},{6,5},{7,6},{8,11},{9,8},{10,9... | collective-permute-start | bytes 884744 | tf_op jit(solution)/shard_map/ppermute | solution.py:284
  92.7 17.4 %collective-permute-start.5 = (bf16[2,96,896]{2,1,0:T(8,128)(2,1)S(1)}, bf16[2,96,896]{2,1,0:T(8,128)(2,1)S(1)}, u32[]{:S(2)}, u32[]{:S(2)}) collective-permute-start(bf16[2,96,896]{2,1,0:T(8,128)(2,1)S(1)} %get-tuple-element.32.refs_0_), channel_id=1, source_target_pairs={{0,4},{1,5},{2,6},{3,7},{4,8},{5,9},{6,10},{7,11},{8,12},{9,13},{1... | collective-permute-start | bytes 1032200 | tf_op jit(solution)/shard_map/ppermute | solution.py:284
  94.7 15.4 %collective-permute-start.6 = (bf16[2,96,768]{2,1,0:T(8,128)(2,1)S(1)}, bf16[2,96,768]{2,1,0:T(8,128)(2,1)S(1)}, u32[]{:S(2)}, u32[]{:S(2)}) collective-permute-start(bf16[2,96,768]{2,1,0:T(8,128)(2,1)S(1)} %get-tuple-element.33.refs_1_), channel_id=1, source_target_pairs={{0,1},{1,2},{2,3},{3,0},{4,5},{5,6},{6,7},{7,4},{8,9},{9,10},{10,1... | collective-permute-start | bytes 884744 | tf_op jit(solution)/shard_map/ppermute | solution.py:284

commit v2 on v1

--- a/solution.py
+++ b/solution.py
@@ -10,6 +10,7 @@
 ANY = pl.BlockSpec(memory_space=pl.ANY)
 VMEM = pl.BlockSpec(memory_space=pltpu.VMEM)
 SMEM = pl.BlockSpec(memory_space=pltpu.SMEM)
+HBM = pl.BlockSpec(memory_space=pltpu.HBM)
 VMEM_LIMIT = 40 * 1024 * 1024
 
 
@@ -21,6 +22,10 @@
         col = col_count - 1 - col
     klass = lax.rem(row + col, 2)
     return jnp.where(roster_ref[direction, 0, 0] == klass, 0, 1)
+
+
+def in_hbm(array):
+    return pltpu.with_memory_space_constraint(array, pltpu.HBM)
 
 
 def run_copies(copies):
@@ -61,18 +66,19 @@
     corner_width = se_corners.shape[-1]
     kind = se_edges.dtype
     shapes = [
-        jax.ShapeDtypeStruct((parts, shots, edge_width), kind),
-        jax.ShapeDtypeStruct((parts, shots, edge_width + corner_width), kind),
-        jax.ShapeDtypeStruct((parts, shots, corner_width), kind),
+        pltpu.VMEM((parts, shots, edge_width), kind),
+        pltpu.VMEM((parts, shots, edge_width + corner_width), kind),
+        pltpu.VMEM((parts, shots, corner_width), kind),
     ] * 2
     return pl.pallas_call(
         functools.partial(select_kernel, counts),
         out_shape=shapes,
-        in_specs=[SMEM] + [ANY] * 4,
-        out_specs=[ANY] * 6,
+        in_specs=[SMEM] + [HBM] * 4,
+        out_specs=[VMEM] * 6,
         scratch_shapes=[pltpu.SemaphoreType.DMA((2, 4))],
+        compiler_params=pltpu.CompilerParams(vmem_limit_bytes=VMEM_LIMIT),
         name="select_initial",
-    )(roster, se_edges, nw_edges, se_corners, nw_corners)
+    )(roster, *map(in_hbm, (se_edges, nw_edges, se_corners, nw_corners)))
 
 
 def load_kernel(operators, plain, flipped, sems):
@@ -99,12 +105,12 @@
     return pl.pallas_call(
         load_kernel,
         out_shape=[pltpu.VMEM(shape, operators.dtype), pltpu.VMEM(shape, operators.dtype)],
-        in_specs=[ANY],
+        in_specs=[HBM],
         out_specs=[VMEM, VMEM],
         scratch_shapes=[pltpu.SemaphoreType.DMA((count,))],
         compiler_params=pltpu.CompilerParams(vmem_limit_bytes=VMEM_LIMIT),
         name="load_operators",
-    )(operators.reshape(count, edge_width, edge_width))
+    )(in_hbm(operators.reshape(count, edge_width, edge_width)))
 
 
 def tick_kernel(
@@ -113,12 +119,10 @@
 ):
     if last:
         old_first, old_second, old_corner, edges_out, corners_out = refs[:5]
-        refs = refs[5:]
+        left, first_out, second_out, corner_out, sems = refs[5:]
     else:
-        first_out, second_out, corner_out = refs[:3]
-        refs = refs[3:]
-    first_v, second_v, corner_v, source_v, left, first_o, second_o, corner_o, sems = refs
-    parts, shots, _ = source_v.shape
+        first_out, second_out, corner_out, left = refs
+    parts, shots = sources.shape[1:3]
     rows = parts * shots
     chosen = chosen_at_start(roster, direction, *counts)
     if tick % 2:
@@ -126,32 +130,21 @@
     edge_part = pl.ds(0, edge_width)
     corner_part = pl.ds(edge_width, corner_width)
 
-    first_copy = pltpu.make_async_copy(first_in, first_v, sems.at[0])
-    second_copy = pltpu.make_async_copy(second_in, second_v, sems.at[1])
-    source_copy = pltpu.make_async_copy(sources.at[chosen], source_v, sems.at[2])
-    inputs = [first_copy, second_copy, source_copy]
-    if tick == 0:
-        corner_copy = pltpu.make_async_copy(corner_in, corner_v, sems.at[3])
-        inputs.append(corner_copy)
-    for copy in inputs:
-        copy.start()
     history = []
     if last:
         history = [
             pltpu.make_async_copy(
-                old_first.at[:, :, edge_part], edges_out.at[0, 1 - chosen], sems.at[4]
+                old_first.at[:, :, edge_part], edges_out.at[0, 1 - chosen], sems.at[0]
             ),
             pltpu.make_async_copy(
-                old_second.at[:, :, edge_part], edges_out.at[1, 1 - chosen], sems.at[5]
+                old_second.at[:, :, edge_part], edges_out.at[1, 1 - chosen], sems.at[1]
             ),
-            pltpu.make_async_copy(old_corner, corners_out.at[1 - chosen], sems.at[6]),
+            pltpu.make_async_copy(old_corner, corners_out.at[1 - chosen], sems.at[2]),
         ]
         for copy in history:
             copy.start()
-    for copy in inputs:
-        copy.wait()
-
-    for place, ref in ((0, first_v), (2, second_v)):
+
+    for place, ref in ((0, first_in), (2, second_in)):
         other_place = 2 - place
         real = ref[0, :, edge_part]
         imag = ref[1, :, edge_part]
@@ -164,20 +157,17 @@
             left[pl.ds(row, shots), pl.ds(column + edge_width, edge_width)] = minus
             left[pl.ds(row + shots, shots), pl.ds(column + edge_width, edge_width)] = real
 
-    if tick == 0:
-        corner = corner_v[...]
-    else:
-        corner = first_v[:, :, corner_part]
+    corner = corner_in[...] if tick == 0 else first_in[:, :, corner_part]
     corner = corner.astype(jnp.float32).reshape(rows, corner_width)
-    if not last and first_o.shape[-1] > edge_width:
-        first_o[:, :, corner_part] = second_v[:, :, corner_part]
+    if first_out.shape[-1] > edge_width:
+        first_out[:, :, corner_part] = second_in[:, :, corner_part]
 
     tile = edge_width // 3 if edge_width % 3 == 0 else edge_width
     steps = edge_width // tile
     for step in range(steps):
         at = pl.ds(step * tile, tile)
         value = jnp.dot(left[...], operators[:, at], preferred_element_type=jnp.float32)
-        source = source_v[:, :, at].astype(jnp.float32).reshape(rows, tile)
+        source = sources[chosen, :, :, at].astype(jnp.float32).reshape(rows, tile)
         first = value[:rows] + source
         second = value[rows:] + source
         low, high = step == 0, step == steps - 1
@@ -195,26 +185,21 @@
             second = second + padded
         if gives:
             value = 0.5 * (at_corner(first, not direction) + at_corner(second, not direction))
-            value = value.astype(corner_o.dtype).reshape(parts, shots, corner_width)
-            corner_o[...] = value
-            if not last and second_o.shape[-1] > edge_width:
-                second_o[:, :, corner_part] = value
-        first_o[:, :, at] = first.astype(first_o.dtype).reshape(parts, shots, tile)
-        second_o[:, :, at] = second.astype(second_o.dtype).reshape(parts, shots, tile)
+            value = value.astype(corner_out.dtype).reshape(parts, shots, corner_width)
+            corner_out[...] = value
+            if second_out.shape[-1] > edge_width:
+                second_out[:, :, corner_part] = value
+        first_out[:, :, at] = first.astype(first_out.dtype).reshape(parts, shots, tile)
+        second_out[:, :, at] = second.astype(second_out.dtype).reshape(parts, shots, tile)
 
     if last:
-        copies = [
-            pltpu.make_async_copy(first_o, edges_out.at[0, chosen], sems.at[7]),
-            pltpu.make_async_copy(second_o, edges_out.at[1, chosen], sems.at[8]),
-            pltpu.make_async_copy(corner_o, corners_out.at[chosen], sems.at[9]),
-        ]
-    else:
-        copies = [
-            pltpu.make_async_copy(first_o, first_out, sems.at[7]),
-            pltpu.make_async_copy(second_o, second_out, sems.at[8]),
-            pltpu.make_async_copy(corner_o, corner_out, sems.at[9]),
-        ]
-    run_copies(copies)
+        run_copies(
+            [
+                pltpu.make_async_copy(first_out, edges_out.at[0, chosen], sems.at[3]),
+                pltpu.make_async_copy(second_out, edges_out.at[1, chosen], sems.at[4]),
+                pltpu.make_async_copy(corner_out, corners_out.at[chosen], sems.at[5]),
+            ]
+        )
     for copy in history:
         copy.wait()
 
@@ -229,38 +214,33 @@
     last = tick == ticks - 1
     first_width = edge_width + (0 if last else corner_width)
     second_width = edge_width + (0 if tick >= ticks - 2 else corner_width)
+    rows = parts * shots
     shapes = [
-        jax.ShapeDtypeStruct((parts, shots, first_width), kind),
-        jax.ShapeDtypeStruct((parts, shots, second_width), kind),
-        jax.ShapeDtypeStruct((parts, shots, corner_width), kind),
+        pltpu.VMEM((parts, shots, first_width), kind),
+        pltpu.VMEM((parts, shots, second_width), kind),
+        pltpu.VMEM((parts, shots, corner_width), kind),
     ]
+    scratch = [pltpu.VMEM((2 * rows, 4 * edge_width), kind)]
+    operands = [roster, first_in, second_in, corner_in, sources, operators]
+    in_specs = [SMEM] + [VMEM] * 5
     if last:
         outs = [
             jax.ShapeDtypeStruct((2, batches, parts, shots, edge_width), kind),
             jax.ShapeDtypeStruct((batches, parts, shots, corner_width), kind),
         ]
+        out_specs = [HBM] * 2
+        scratch += shapes + [pltpu.SemaphoreType.DMA((6,))]
+        operands += list(history)
+        in_specs += [VMEM] * 3
     else:
         outs = shapes
-    operands = [roster, first_in, second_in, corner_in, sources, operators]
-    if last:
-        operands += list(history)
-    rows = parts * shots
+        out_specs = [VMEM] * 3
     return pl.pallas_call(
         functools.partial(tick_kernel, counts, direction, tick, last, edge_width, corner_width),
         out_shape=outs,
-        in_specs=[SMEM, ANY, ANY, ANY, ANY, VMEM] + [ANY] * (len(operands) - 6),
-        out_specs=[ANY] * len(outs),
-        scratch_shapes=[
-            pltpu.VMEM(first_in.shape, kind),
-            pltpu.VMEM(second_in.shape, kind),
-            pltpu.VMEM((parts, shots, corner_width), kind),
-            pltpu.VMEM((parts, shots, edge_width), kind),
-            pltpu.VMEM((2 * rows, 4 * edge_width), kind),
-            pltpu.VMEM(shapes[0].shape, kind),
-            pltpu.VMEM(shapes[1].shape, kind),
-            pltpu.VMEM(shapes[2].shape, kind),
-            pltpu.SemaphoreType.DMA((10,)),
-        ],
+        in_specs=in_specs,
+        out_specs=out_specs,
+        scratch_shapes=scratch,
         compiler_params=pltpu.CompilerParams(vmem_limit_bytes=VMEM_LIMIT),
         cost_estimate=pl.CostEstimate(
             flops=2 * 2 * rows * 4 * edge_width * edge_width,
@@ -290,6 +270,7 @@
 ):
     counts = (lax.axis_size("row"), lax.axis_size("col"))
     ticks = roster.shape[1]
+    roster = roster.transpose(0, 2, 1)
     local_sources = sources[0, 0]
     picked = select_initial(
         counts, roster, southeast_edges[0, 0], northwest_edges[0, 0], southeast_corners[0, 0],

time: 114 us -> 69 us (0.61)
  Pallas kernels: 67.9 us -> 22.8 us
  waiting for transfers between devices: 28.4 us -> 31.7 us
  local copies, waits for them, and re-layouts: 3.71 us -> 0.68 us
    pallas_call x1, Pallas kernels: 43.6 us -> 1.91 us  [select_initial(): pl.pallas_call(functools.partial(select_kernel, counts), out_shape=shapes...]
    pallas_call x6, Pallas kernels: 21.9 us -> 18.1 us  [tick_update(): pl.pallas_call(functools.partial(tick_kernel, counts, direction, tick, la...]
    ppermute x14, waiting for transfers between devices: 28.4 us -> 31.7 us  [move(): lax.ppermute(array, ('row', 'col'), neighbours(counts, row_step, col_step))]
    unnamed x9 -> x6, local copies, waits for them, and re-layouts: 3.71 us -> 0.68 us
  transfers between devices with their start and end apart: 14 -> 14, of which waited for: 4 -> 4; matrix products, arithmetic and copies ran while one was open for 0% -> 0% of each run, Pallas kernels for 18% -> 25%
where the time goes in v2:
time: 69 us; the launch traced here: 68.8 us
  waiting for transfers between devices  31.7 us (46%)
  Pallas kernels  22.8 us (33%)
  starting transfers between devices  12.9 us (19%)
  between operations  0.75 us (1%)
    ppermute x14, waiting for transfers between devices, move(): lax.ppermute(array, ('row', 'col'), neighbours(counts, row_step, col_step))  31.7 us
    pallas_call x6, Pallas kernels, tick_update(): pl.pallas_call(functools.partial(tick_kernel, counts, direction, tick, la...  18.1 us
    ppermute x14, starting transfers between devices, move(): lax.ppermute(array, ('row', 'col'), neighbours(counts, row_step, col_step))  12.9 us
    pallas_call x1, Pallas kernels, load_operators(): pl.pallas_call(load_kernel, out_shape=[pltpu.VMEM(shape, operators.dtype)...  2.8 us
    pallas_call x1, Pallas kernels, select_initial(): pl.pallas_call(functools.partial(select_kernel, counts), out_shape=shapes...  1.91 us
  transfers between devices with their start and end apart: 14, of which 4 were waited for; matrix products, arithmetic and copies ran while one was open for 0% of the time, Pallas kernels for 25%

profile of v2, /device:TPU:8, one launch (start us, length us, event | category | flops | bytes accessed | tf_op | source)
XLA Modules:
  0.0 68.8 jit_solution(16773423226601558671)
XLA Ops:
  0.6 0.0 copy-start
  0.6 0.7 copy-done
  1.3 1.9 %select_initial.1 = (bf16[2,96,768]{2,1,0:T(8,128)(2,1)S(1)}, bf16[2,96,896]{2,1,0:T(8,128)(2,1)S(1)}, bf16[2,96,128]{2,1,0:T(8,128)(2,1)S(1)}, bf16[2,96,768]{2...) custom-call(s32[2,2,3]{2,1,0:T(2,128)S(1)} %bitcast.11, ...), custom_call_target="tpu_custom_call" | custom-call | tf_op jit(solution)/shard_map/select_initial/pallas_call | solution.py:73
  3.2 1.0 %collective-permute-start.8 = (bf16[2,96,896]{2,1,0:T(8,128)(2,1)S(1)}, bf16[2,96,896]{2,1,0:T(8,128)(2,1)S(1)}, u32[]{:S(2)}, u32[]{:S(2)}) collective-permute-start(bf16[2,96,896]{2,1,0:T(8,128)(2,1)S(1)} %get-tuple-element.37), channel_id=1, source_target_pairs={{0,3},{1,0},{2,1},{3,2},{4,7},{5,4},{6,5},{7,6},{8,11},{9,8},{10,9... | collective-permute-start | bytes 1032200 | tf_op jit(solution)/shard_map/ppermute | solution.py:264
  4.3 1.4 %collective-permute-start.7 = (bf16[2,96,768]{2,1,0:T(8,128)(2,1)S(1)}, bf16[2,96,768]{2,1,0:T(8,128)(2,1)S(1)}, u32[]{:S(2)}, u32[]{:S(2)}) collective-permute-start(bf16[2,96,768]{2,1,0:T(8,128)(2,1)S(1)} %get-tuple-element.36), channel_id=1, source_target_pairs={{0,28},{1,29},{2,30},{3,31},{4,0},{5,1},{6,2},{7,3},{8,4},{9,5},{1... | collective-permute-start | bytes 884744 | tf_op jit(solution)/shard_map/ppermute | solution.py:264
  5.6 0.0 collective-permute-start.1
  5.6 0.6 collective-permute-start
  6.3 3.2 %collective-permute-start.9 = (bf16[2,96,128]{2,1,0:T(8,128)(2,1)S(1)}, bf16[2,96,128]{2,1,0:T(8,128)(2,1)S(1)}, u32[]{:S(2)}, u32[]{:S(2)}) collective-permute-start(bf16[2,96,128]{2,1,0:T(8,128)(2,1)S(1)} %get-tuple-element.38), channel_id=1, source_target_pairs={{0,31},{1,28},{2,29},{3,30},{4,3},{5,0},{6,1},{7,2},{8,7},{9,4},{1... | collective-permute-start | bytes 147464 | tf_op jit(solution)/shard_map/ppermute | solution.py:264
  9.5 2.8 %load_operators.1 = (bf16[3072,768]{1,0:T(8,128)(2,1)S(1)}, bf16[3072,768]{1,0:T(8,128)(2,1)S(1)}) custom-call(bf16[4,768,768]{2,1,0:T(8,128)(2,1)} %bitcast.24), custom_call_target="tpu_custom_call" | custom-call | tf_op jit(solution)/shard_map/load_operators/pallas_call | solution.py:105
  12.3 6.3 %collective-permute-done.9.corner_in = bf16[2,96,128]{2,1,0:T(8,128)(2,1)S(1)} collective-permute-done((bf16[2,96,128]{2,1,0:T(8,128)(2,1)S(1)}, bf16[2,96,128]{2,1,0:T(8,128)(2,1)S(1)}, u32[]{:S(2)}, u32[]{:S(2)}) %collective-permute-start.9) | collective-permute-done | bytes 49184 | tf_op jit(solution)/shard_map/ppermute | solution.py:264
  18.6 0.0 collective-permute-start.2
  18.6 0.9 %collective-permute-done.7.first_in = bf16[2,96,768]{2,1,0:T(8,128)(2,1)S(1)} collective-permute-done((bf16[2,96,768]{2,1,0:T(8,128)(2,1)S(1)}, bf16[2,96,768]{2,1,0:T(8,128)(2,1)S(1)}, u32[]{:S(2)}, u32[]{:S(2)}) %collective-permute-start.7) | collective-permute-done | bytes 294944 | tf_op jit(solution)/shard_map/ppermute | solution.py:264
  19.6 3.0 %tick0nw.1 = (bf16[2,96,896]{2,1,0:T(8,128)(2,1)S(1)}, bf16[2,96,896]{2,1,0:T(8,128)(2,1)S(1)}, bf16[2,96,128]{2,1,0:T(8,128)(2,1)}) custom-call(s32[2,2,3]{2,1,0:T(2,128)S(1)} %bitcast.12, bf16[2,96,768]{2,1,0:T(8,128)(2,1)S(1)} %collective-permute-done.7.first_in, bf16[2,96,896]{2,1,0:T(8,128)(2,1)S(1)} %collective-permute-done.8.second_in, ...), custom_call_target="tpu_custom_call" | custom-call | flops 1811939328 | bytes 1769472 | tf_op jit(solution)/shard_map/tick0nw/pallas_call | solution.py:238
  22.5 3.8 %collective-permute-start.10 = (bf16[2,96,896]{2,1,0:T(8,128)(2,1)S(1)}, bf16[2,96,896]{2,1,0:T(8,128)(2,1)S(1)}, u32[]{:S(2)}, u32[]{:S(2)}) collective-permute-start(bf16[2,96,896]{2,1,0:T(8,128)(2,1)S(1)} %get-tuple-element.40), channel_id=1, source_target_pairs={{0,28},{1,29},{2,30},{3,31},{4,0},{5,1},{6,2},{7,3},{8,4},{9,5},{1... | collective-permute-start | bytes 1032200 | tf_op jit(solution)/shard_map/ppermute | solution.py:264
  26.4 0.0 collective-permute-done.2.corner_in
  26.4 0.0 collective-permute-done.first_in
  26.4 3.2 %tick0se.1 = (bf16[2,96,896]{2,1,0:T(8,128)(2,1)S(1)}, bf16[2,96,896]{2,1,0:T(8,128)(2,1)S(1)}, bf16[2,96,128]{2,1,0:T(8,128)(2,1)}) custom-call(s32[2,2,3]{2,1,0:T(2,128)S(1)} %bitcast.13, bf16[2,96,768]{2,1,0:T(8,128)(2,1)S(1)} %collective-permute-done.first_in, bf16[2,96,896]{2,1,0:T(8,128)(2,1)S(1)} %collective-permute-done.1.second_in, ...), custom_call_target="tpu_custom_call" | custom-call | flops 1811939328 | bytes 1769472 | tf_op jit(solution)/shard_map/tick0se/pallas_call | solution.py:238
  29.6 0.1 collective-permute-start.3
  29.7 0.4 collective-permute-start.4
  30.1 12.2 %collective-permute-done.10.first_in = bf16[2,96,896]{2,1,0:T(8,128)(2,1)S(1)} collective-permute-done((bf16[2,96,896]{2,1,0:T(8,128)(2,1)S(1)}, bf16[2,96,896]{2,1,0:T(8,128)(2,1)S(1)}, u32[]{:S(2)}, u32[]{:S(2)}) %collective-permute-start.10) | collective-permute-done | bytes 344096 | tf_op jit(solution)/shard_map/ppermute | solution.py:264
  42.3 0.0 collective-permute-done.11.second_in
  42.3 2.6 %tick1nw.1 = (bf16[2,96,896]{2,1,0:T(8,128)(2,1)S(1)}, bf16[2,96,768]{2,1,0:T(8,128)(2,1)S(1)}, bf16[2,96,128]{2,1,0:T(8,128)(2,1)S(1)}) custom-call(s32[2,2,3]{2,1,0:T(2,128)S(1)} %bitcast.14, bf16[2,96,896]{2,1,0:T(8,128)(2,1)S(1)} %collective-permute-done.10.first_in, bf16[2,96,896]{2,1,0:T(8,128)(2,1)S(1)} %collective-permute-done.11.second_in, ...), custom_call_target="tpu_custom_call" | custom-call | flops 1811939328 | bytes 1769472 | tf_op jit(solution)/shard_map/tick1nw/pallas_call | solution.py:238
  44.9 0.1 collective-permute-start.12
  45.0 0.1 collective-permute-start.13
  45.0 0.0 collective-permute-done.3.first_in
  45.0 0.0 collective-permute-done.4.second_in
  45.1 2.6 %tick1se.1 = (bf16[2,96,896]{2,1,0:T(8,128)(2,1)S(1)}, bf16[2,96,768]{2,1,0:T(8,128)(2,1)S(1)}, bf16[2,96,128]{2,1,0:T(8,128)(2,1)S(1)}) custom-call(s32[2,2,3]{2,1,0:T(2,128)S(1)} %bitcast.15, bf16[2,96,896]{2,1,0:T(8,128)(2,1)S(1)} %collective-permute-done.3.first_in, bf16[2,96,896]{2,1,0:T(8,128)(2,1)S(1)} %collective-permute-done.4.second_in, ...), custom_call_target="tpu_custom_call" | custom-call | flops 1811939328 | bytes 1769472 | tf_op jit(solution)/shard_map/tick1se/pallas_call | solution.py:238
  47.6 2.0 %collective-permute-start.5 = (bf16[2,96,896]{2,1,0:T(8,128)(2,1)S(1)}, bf16[2,96,896]{2,1,0:T(8,128)(2,1)S(1)}, u32[]{:S(2)}, u32[]{:S(2)}) collective-permute-start(bf16[2,96,896]{2,1,0:T(8,128)(2,1)S(1)} %get-tuple-element.32.refs_0_), channel_id=1, source_target_pairs={{0,4},{1,5},{2,6},{3,7},{4,8},{5,9},{6,10},{7,11},{8,12},{9,13},{1... | collective-permute-start | bytes 1032200 | tf_op jit(solution)/shard_map/ppermute | solution.py:264
  49.6 0.2 collective-permute-start.6
  49.9 12.2 %collective-permute-done.12.first_in = bf16[2,96,896]{2,1,0:T(8,128)(2,1)S(1)} collective-permute-done((bf16[2,96,896]{2,1,0:T(8,128)(2,1)S(1)}, bf16[2,96,896]{2,1,0:T(8,128)(2,1)S(1)}, u32[]{:S(2)}, u32[]{:S(2)}) %collective-permute-start.12) | collective-permute-done | bytes 344096 | tf_op jit(solution)/shard_map/ppermute | solution.py:264
  62.0 3.4 %tick2nw.1 = (bf16[2,2,2,96,768]{4,3,2,1,0:T(8,128)(2,1)}, bf16[2,2,96,128]{3,2,1,0:T(8,128)(2,1)}) custom-call(s32[2,2,3]{2,1,0:T(2,128)S(1)} %bitcast.16, bf16[2,96,896]{2,1,0:T(8,128)(2,1)S(1)} %collective-permute-done.12.first_in, bf16[2,96,768]{2,1,0:T(8,128)(2,1)S(1)} %collective-permute-done.13.second_in, ...), custom_call_target="tpu_custom_call" | custom-call | flops 1811939328 | bytes 1769472 | tf_op jit(solution)/shard_map/tick2nw/pallas_call | solution.py:238
  65.4 3.4 %tick2se.1 = (bf16[2,2,2,96,768]{4,3,2,1,0:T(8,128)(2,1)}, bf16[2,2,96,128]{3,2,1,0:T(8,128)(2,1)}) custom-call(s32[2,2,3]{2,1,0:T(2,128)S(1)} %bitcast.17, bf16[2,96,896]{2,1,0:T(8,128)(2,1)S(1)} %collective-permute-done.5.first_in, bf16[2,96,768]{2,1,0:T(8,128)(2,1)S(1)} %collective-permute-done.6.second_in, ...), custom_call_target="tpu_custom_call" | custom-call | flops 1811939328 | bytes 1769472 | tf_op jit(solution)/shard_map/tick2se/pallas_call | solution.py:238
  (10 shorter events, 0.0 us)
Async XLA Ops:
  0.6 0.7 copy-start
  3.2 16.3 %collective-permute-start.8 = (bf16[2,96,896]{2,1,0:T(8,128)(2,1)S(1)}, bf16[2,96,896]{2,1,0:T(8,128)(2,1)S(1)}, u32[]{:S(2)}, u32[]{:S(2)}) collective-permute-start(bf16[2,96,896]{2,1,0:T(8,128)(2,1)S(1)} %get-tuple-element.37), channel_id=1, source_target_pairs={{0,3},{1,0},{2,1},{3,2},{4,7},{5,4},{6,5},{7,6},{8,11},{9,8},{10,9... | collective-permute-start | bytes 1032200 | tf_op jit(solution)/shard_map/ppermute | solution.py:264
  4.3 15.3 %collective-permute-start.7 = (bf16[2,96,768]{2,1,0:T(8,128)(2,1)S(1)}, bf16[2,96,768]{2,1,0:T(8,128)(2,1)S(1)}, u32[]{:S(2)}, u32[]{:S(2)}) collective-permute-start(bf16[2,96,768]{2,1,0:T(8,128)(2,1)S(1)} %get-tuple-element.36), channel_id=1, source_target_pairs={{0,28},{1,29},{2,30},{3,31},{4,0},{5,1},{6,2},{7,3},{8,4},{9,5},{1... | collective-permute-start | bytes 884744 | tf_op jit(solution)/shard_map/ppermute | solution.py:264
  5.6 20.8 %collective-permute-start.1 = (bf16[2,96,896]{2,1,0:T(8,128)(2,1)S(1)}, bf16[2,96,896]{2,1,0:T(8,128)(2,1)S(1)}, u32[]{:S(2)}, u32[]{:S(2)}) collective-permute-start(bf16[2,96,896]{2,1,0:T(8,128)(2,1)S(1)} %get-tuple-element.27), channel_id=1, source_target_pairs={{0,1},{1,2},{2,3},{3,0},{4,5},{5,6},{6,7},{7,4},{8,9},{9,10},{10,1... | collective-permute-start | bytes 1032200 | tf_op jit(solution)/shard_map/ppermute | solution.py:264
  5.6 20.7 %collective-permute-start = (bf16[2,96,768]{2,1,0:T(8,128)(2,1)S(1)}, bf16[2,96,768]{2,1,0:T(8,128)(2,1)S(1)}, u32[]{:S(2)}, u32[]{:S(2)}) collective-permute-start(bf16[2,96,768]{2,1,0:T(8,128)(2,1)S(1)} %get-tuple-element.26), channel_id=1, source_target_pairs={{0,4},{1,5},{2,6},{3,7},{4,8},{5,9},{6,10},{7,11},{8,12},{9,13},{1... | collective-permute-start | bytes 884744 | tf_op jit(solution)/shard_map/ppermute | solution.py:264
  6.3 12.3 %collective-permute-start.9 = (bf16[2,96,128]{2,1,0:T(8,128)(2,1)S(1)}, bf16[2,96,128]{2,1,0:T(8,128)(2,1)S(1)}, u32[]{:S(2)}, u32[]{:S(2)}) collective-permute-start(bf16[2,96,128]{2,1,0:T(8,128)(2,1)S(1)} %get-tuple-element.38), channel_id=1, source_target_pairs={{0,31},{1,28},{2,29},{3,30},{4,3},{5,0},{6,1},{7,2},{8,7},{9,4},{1... | collective-permute-start | bytes 147464 | tf_op jit(solution)/shard_map/ppermute | solution.py:264
  9.5 10.1 %copy-start.1 = (s32[2,3,2]{1,2,0:T(2,128)S(1)}, s32[2,3,2]{1,2,0:T(2,128)}, u32[]{:S(2)}) copy-start(s32[2,3,2]{1,2,0:T(2,128)} %param.13) | copy-start | bytes 148
  9.5 10.1 %copy-start.2 = (bf16[1,1,2,2,96,768]{5,4,3,2,1,0:T(8,128)(2,1)S(1)}, bf16[1,1,2,2,96,768]{5,4,3,2,1,0:T(8,128)(2,1)}, u32[]{:S(2)}) copy-start(bf16[1,1,2,2,96,768]{5,4,3,2,1,0:T(8,128)(2,1)} %param.12) | copy-start | bytes 1769476
  18.6 7.8 %collective-permute-start.2 = (bf16[2,96,128]{2,1,0:T(8,128)(2,1)S(1)}, bf16[2,96,128]{2,1,0:T(8,128)(2,1)S(1)}, u32[]{:S(2)}, u32[]{:S(2)}) collective-permute-start(bf16[2,96,128]{2,1,0:T(8,128)(2,1)S(1)} %get-tuple-element.28), channel_id=1, source_target_pairs={{0,5},{1,6},{2,7},{3,4},{4,9},{5,10},{6,11},{7,8},{8,13},{9,14},{1... | collective-permute-start | bytes 147464 | tf_op jit(solution)/shard_map/ppermute | solution.py:264
  22.5 19.8 %collective-permute-start.10 = (bf16[2,96,896]{2,1,0:T(8,128)(2,1)S(1)}, bf16[2,96,896]{2,1,0:T(8,128)(2,1)S(1)}, u32[]{:S(2)}, u32[]{:S(2)}) collective-permute-start(bf16[2,96,896]{2,1,0:T(8,128)(2,1)S(1)} %get-tuple-element.40), channel_id=1, source_target_pairs={{0,28},{1,29},{2,30},{3,31},{4,0},{5,1},{6,2},{7,3},{8,4},{9,5},{1... | collective-permute-start | bytes 1032200 | tf_op jit(solution)/shard_map/ppermute | solution.py:264
  26.4 15.9 %collective-permute-start.11 = (bf16[2,96,896]{2,1,0:T(8,128)(2,1)S(1)}, bf16[2,96,896]{2,1,0:T(8,128)(2,1)S(1)}, u32[]{:S(2)}, u32[]{:S(2)}) collective-permute-start(bf16[2,96,896]{2,1,0:T(8,128)(2,1)S(1)} %get-tuple-element.41), channel_id=1, source_target_pairs={{0,3},{1,0},{2,1},{3,2},{4,7},{5,4},{6,5},{7,6},{8,11},{9,8},{10,9... | collective-permute-start | bytes 1032200 | tf_op jit(solution)/shard_map/ppermute | solution.py:264
  29.6 15.4 %collective-permute-start.3 = (bf16[2,96,896]{2,1,0:T(8,128)(2,1)S(1)}, bf16[2,96,896]{2,1,0:T(8,128)(2,1)S(1)}, u32[]{:S(2)}, u32[]{:S(2)}) collective-permute-start(bf16[2,96,896]{2,1,0:T(8,128)(2,1)S(1)} %get-tuple-element.30), channel_id=1, source_target_pairs={{0,4},{1,5},{2,6},{3,7},{4,8},{5,9},{6,10},{7,11},{8,12},{9,13},{1... | collective-permute-start | bytes 1032200 | tf_op jit(solution)/shard_map/ppermute | solution.py:264
  29.7 15.3 %collective-permute-start.4 = (bf16[2,96,896]{2,1,0:T(8,128)(2,1)S(1)}, bf16[2,96,896]{2,1,0:T(8,128)(2,1)S(1)}, u32[]{:S(2)}, u32[]{:S(2)}) collective-permute-start(bf16[2,96,896]{2,1,0:T(8,128)(2,1)S(1)} %get-tuple-element.31), channel_id=1, source_target_pairs={{0,1},{1,2},{2,3},{3,0},{4,5},{5,6},{6,7},{7,4},{8,9},{9,10},{10,1... | collective-permute-start | bytes 1032200 | tf_op jit(solution)/shard_map/ppermute | solution.py:264
  44.9 17.1 %collective-permute-start.12 = (bf16[2,96,896]{2,1,0:T(8,128)(2,1)S(1)}, bf16[2,96,896]{2,1,0:T(8,128)(2,1)S(1)}, u32[]{:S(2)}, u32[]{:S(2)}) collective-permute-start(bf16[2,96,896]{2,1,0:T(8,128)(2,1)S(1)} %get-tuple-element.42.refs_0_), channel_id=1, source_target_pairs={{0,28},{1,29},{2,30},{3,31},{4,0},{5,1},{6,2},{7,3},{8,4},{9,5},{1... | collective-permute-start | bytes 1032200 | tf_op jit(solution)/shard_map/ppermute | solution.py:264
  45.0 4.9 %collective-permute-start.13 = (bf16[2,96,768]{2,1,0:T(8,128)(2,1)S(1)}, bf16[2,96,768]{2,1,0:T(8,128)(2,1)S(1)}, u32[]{:S(2)}, u32[]{:S(2)}) collective-permute-start(bf16[2,96,768]{2,1,0:T(8,128)(2,1)S(1)} %get-tuple-element.43.refs_1_), channel_id=1, source_target_pairs={{0,3},{1,0},{2,1},{3,2},{4,7},{5,4},{6,5},{7,6},{8,11},{9,8},{10,9... | collective-permute-start | bytes 884744 | tf_op jit(solution)/shard_map/ppermute | solution.py:264
  47.6 17.8 %collective-permute-start.5 = (bf16[2,96,896]{2,1,0:T(8,128)(2,1)S(1)}, bf16[2,96,896]{2,1,0:T(8,128)(2,1)S(1)}, u32[]{:S(2)}, u32[]{:S(2)}) collective-permute-start(bf16[2,96,896]{2,1,0:T(8,128)(2,1)S(1)} %get-tuple-element.32.refs_0_), channel_id=1, source_target_pairs={{0,4},{1,5},{2,6},{3,7},{4,8},{5,9},{6,10},{7,11},{8,12},{9,13},{1... | collective-permute-start | bytes 1032200 | tf_op jit(solution)/shard_map/ppermute | solution.py:264
  49.6 15.8 %collective-permute-start.6 = (bf16[2,96,768]{2,1,0:T(8,128)(2,1)S(1)}, bf16[2,96,768]{2,1,0:T(8,128)(2,1)S(1)}, u32[]{:S(2)}, u32[]{:S(2)}) collective-permute-start(bf16[2,96,768]{2,1,0:T(8,128)(2,1)S(1)} %get-tuple-element.33.refs_1_), channel_id=1, source_target_pairs={{0,1},{1,2},{2,3},{3,0},{4,5},{5,6},{6,7},{7,4},{8,9},{9,10},{10,1... | collective-permute-start | bytes 884744 | tf_op jit(solution)/shard_map/ppermute | solution.py:264

commit v3 on v2

v3 whole, which is shorter than its diff:
```python
import functools

import jax
import jax.numpy as jnp
from jax import lax
from jax.experimental import pallas as pl
from jax.experimental.pallas import tpu as pltpu
from jax.sharding import PartitionSpec as P

VMEM = pl.BlockSpec(memory_space=pltpu.VMEM)
SMEM = pl.BlockSpec(memory_space=pltpu.SMEM)
HBM = pl.BlockSpec(memory_space=pltpu.HBM)
VMEM_LIMIT = 40 * 1024 * 1024


def direction_at(row, col, tick, stream):
    return (row + col + tick + 1 + stream) % 2


def in_hbm(array):
    return pltpu.with_memory_space_constraint(array, pltpu.HBM)


def own_direction(tick, stream):
    return direction_at(lax.axis_index("row"), lax.axis_index("col"), tick, stream)


def chosen_at_start(roster_ref, direction, counts):
    row = lax.axis_index("row")
    col = lax.axis_index("col")
    if direction:
        row = counts[0] - 1 - row
        col = counts[1] - 1 - col
    klass = lax.rem(row + col, 2)
    return jnp.where(roster_ref[direction, 0, 0] == klass, 0, 1)


def start(copy):
    copy.start()


def wait(copy):
    copy.wait()


def select_slots(counts, stream, roster, edges, corners, outs, sems, act):
    by_row, by_col, by_diagonal = outs
    edge_width = by_row.shape[-1]
    corner_width = by_diagonal.shape[-1]
    for going in range(2):

        @pl.when(own_direction(-1, stream) == going)
        def _():
            other = 1 - chosen_at_start(roster, going, counts)
            own = going if False else 1 - going
            mine = chosen_at_start(roster, own, counts)
            pairs = (
                (edges[going].at[0, other], by_row),
                (corners[own].at[mine], by_diagonal),
                (edges[going].at[1, other], by_col.at[:, :, pl.ds(0, edge_width)]),
                (corners[going].at[other], by_col.at[:, :, pl.ds(edge_width, corner_width)]),
            )
            for index, (source, target) in enumerate(pairs):
                act(pltpu.make_async_copy(source, target, sems.at[index]))


def select_kernel(counts, stream, roster, se_edges, nw_edges, se_corners, nw_corners, *refs):
    outs, sems = refs[:3], refs[3]
    for act in (start, wait):
        select_slots(
            counts, stream, roster, (se_edges, nw_edges), (se_corners, nw_corners), outs, sems, act
        )


def slot_shapes(edges, corners):
    _, _, parts, shots, edge_width = edges.shape
    corner_width = corners.shape[-1]
    return [
        pltpu.VMEM((parts, shots, edge_width), edges.dtype),
        pltpu.VMEM((parts, shots, edge_width + corner_width), edges.dtype),
        pltpu.VMEM((parts, shots, corner_width), edges.dtype),
    ]


def select_initial(counts, stream, roster, states):
    return pl.pallas_call(
        functools.partial(select_kernel, counts, stream),
        out_shape=slot_shapes(states[0], states[2]),
        in_specs=[SMEM] + [HBM] * 4,
        out_specs=[VMEM] * 3,
        scratch_shapes=[pltpu.SemaphoreType.DMA((4,))],
        compiler_params=pltpu.CompilerParams(vmem_limit_bytes=VMEM_LIMIT),
        name="select_initial",
    )(roster, *map(in_hbm, states))


def load_kernel(
    counts, stream, roster, se_edges, nw_edges, se_corners, nw_corners, operators, sources, *refs
):
    outs = refs[:3]
    prepared, picked, select_sems, operator_sems, source_sems = refs[3:]
    count, edge_width, _ = operators.shape
    copies = [
        pltpu.make_async_copy(
            operators.at[i],
            prepared.at[0, pl.ds(i * edge_width, edge_width)],
            operator_sems.at[i],
        )
        for i in range(count)
    ]
    source_copies = []
    for direction in range(2):
        mine = chosen_at_start(roster, direction, counts)
        for late in range(2):
            source_copies.append(
                pltpu.make_async_copy(
                    sources.at[1 - mine if late else mine],
                    picked.at[direction, late],
                    source_sems.at[direction, late],
                )
            )
    edges, corners = (se_edges, nw_edges), (se_corners, nw_corners)
    for copy in copies:
        copy.start()
    select_slots(counts, stream, roster, edges, corners, outs, select_sems, start)
    for copy in source_copies:
        copy.start()
    for i in range(count):
        copies[i].wait()
        rows = pl.ds(i * edge_width, edge_width)
        prepared[1, rows, :] = prepared[0, rows, :].T
    select_slots(counts, stream, roster, edges, corners, outs, select_sems, wait)
    for copy in source_copies:
        copy.wait()


def load_operators(counts, stream, roster, states, operators, sources):
    count = operators.shape[0] * operators.shape[1]
    edge_width = operators.shape[-1]
    kind = operators.dtype
    operators = operators.reshape(count, edge_width, edge_width)
    return pl.pallas_call(
        functools.partial(load_kernel, counts, stream),
        out_shape=slot_shapes(states[0], states[2])
        + [
            pltpu.VMEM((2, count * edge_width, edge_width), kind),
            pltpu.VMEM((2,) + sources.shape, kind),
        ],
        in_specs=[SMEM] + [HBM] * 6,
        out_specs=[VMEM] * 5,
        scratch_shapes=[
            pltpu.SemaphoreType.DMA((4,)),
            pltpu.SemaphoreType.DMA((count,)),
            pltpu.SemaphoreType.DMA((2, 2)),
        ],
        compiler_params=pltpu.CompilerParams(vmem_limit_bytes=VMEM_LIMIT),
        cost_estimate=cost(False),
        name="load_operators",
    )(roster, *map(in_hbm, states), in_hbm(operators), in_hbm(sources))


def compute(
    tick, stream, corner_width, first_in, second_in, corner_in, sources, operators, outs, left, act
):
    first_out, second_out, *corner_out = outs
    parts, shots, edge_width = sources.shape[2:]
    rows = parts * shots
    direction = own_direction(tick, stream)
    edge_part = pl.ds(0, edge_width)
    corner_part = pl.ds(edge_width, corner_width)

    for place, ref in ((0, first_in), (2, second_in)):
        other_place = 2 - place
        real = ref[0, :, edge_part]
        imag = ref[1, :, edge_part]
        minus = -imag
        for slot, block in ((place, 0), (other_place, 1)):
            row = block * rows
            column = slot * edge_width
            left[pl.ds(row, shots), pl.ds(column, edge_width)] = real
            left[pl.ds(row + shots, shots), pl.ds(column, edge_width)] = imag
            left[pl.ds(row, shots), pl.ds(column + edge_width, edge_width)] = minus
            left[pl.ds(row + shots, shots), pl.ds(column + edge_width, edge_width)] = real

    corner = corner_in[...] if tick == 0 else first_in[:, :, corner_part]
    corner = corner.astype(jnp.float32).reshape(rows, corner_width)
    if first_out.shape[-1] > edge_width:
        first_out[:, :, corner_part] = second_in[:, :, corner_part]

    tile = edge_width // 3 if edge_width % 3 == 0 else edge_width
    steps = edge_width // tile
    for step in range(steps):
        at = pl.ds(step * tile, tile)
        value = jnp.dot(left[...], operators[direction, :, at], preferred_element_type=jnp.float32)
        source = sources[direction, tick % 2, :, :, at].astype(jnp.float32).reshape(rows, tile)
        first = value[:rows] + source
        second = value[rows:] + source
        for end in range(2):
            if step != (steps - 1 if end else 0):
                continue
            here = slice(tile - corner_width, tile) if end else slice(0, corner_width)
            added = jnp.where(direction == end, corner, 0.0)
            widths = ((0, 0), (tile - corner_width, 0) if end else (0, tile - corner_width))
            added = jnp.pad(added, widths)
            first = first + added
            second = second + added
            given = (0.5 * (first[:, here] + second[:, here])).astype(second_out.dtype)
            given = given.reshape(parts, shots, corner_width)

            @pl.when(direction != end)
            def _():
                for ref in corner_out:
                    ref[...] = given
                if second_out.shape[-1] > edge_width:
                    second_out[:, :, corner_part] = given

        first_out[:, :, at] = first.astype(first_out.dtype).reshape(parts, shots, tile)
        second_out[:, :, at] = second.astype(second_out.dtype).reshape(parts, shots, tile)
        act(step, at)


def middle_kernel(
    tick, stream, corner_width, first_in, second_in, corner_in, sources, operators, *refs
):
    outs, left = refs[:-1], refs[-1]
    compute(
        tick, stream, corner_width, first_in, second_in, corner_in, sources, operators, outs, left,
        lambda step, at: None,
    )


def last_kernel(
    counts, tick, stream, histories, corner_width, roster, first_in, second_in, sources, operators,
    *refs
):
    count = len(histories)
    older = [refs[3 * i : 3 * i + 3] for i in range(count)]
    refs = refs[3 * count :]
    if not count:
        refs = refs[4:]
    edges_out, corners_out, (left, *outs, old_sems, sems) = refs[0:2], refs[2:4], refs[4:]
    edge_width = sources.shape[-1]
    edge_part = pl.ds(0, edge_width)

    def each(at_tick, at_stream, act_on):
        for direction in range(2):

            @pl.when(own_direction(at_tick, at_stream) == direction)
            def _():
                batch = chosen_at_start(roster, direction, counts)
                if at_tick % 2:
                    batch = 1 - batch
                act_on(edges_out[direction], corners_out[direction], batch)

    def old_stores(index, act):
        first, second, corner = older[index]

        def act_on(edges, corners, batch):
            pairs = (
                (first.at[:, :, edge_part], edges.at[0, batch]),
                (second.at[:, :, edge_part], edges.at[1, batch]),
                (corner, corners.at[batch]),
            )
            for place, (source, target) in enumerate(pairs):
                act(pltpu.make_async_copy(source, target, old_sems.at[index, place]))

        each(tick - 1, histories[index], act_on)

    def tile_store(act, step, at):
        def act_on(edges, corners, batch):
            for slot in range(2):
                act(
                    pltpu.make_async_copy(
                        outs[slot].at[:, :, at], edges.at[slot, batch, :, :, at],
                        sems.at[slot, step],
                    )
                )

        each(tick, stream, act_on)

    def corner_store(act):
        each(
            tick, stream,
            lambda edges, corners, batch: act(
                pltpu.make_async_copy(outs[2], corners.at[batch], sems.at[2, 0])
            ),
        )

    for index in range(count):
        old_stores(index, start)
    tiles = []

    def stored(step, at):
        tiles.append((step, at))
        tile_store(start, step, at)

    compute(
        tick, stream, corner_width, first_in, second_in, None, sources, operators, outs, left,
        stored,
    )
    corner_store(start)
    for index in range(count):
        old_stores(index, wait)
    for step, at in tiles:
        tile_store(wait, step, at)
    corner_store(wait)


def tick_shapes(sources, corner_width, tick, ticks):
    _, _, parts, shots, edge_width = sources.shape
    kind = sources.dtype
    first_width = edge_width + (0 if tick == ticks - 1 else corner_width)
    second_width = edge_width + (0 if tick >= ticks - 2 else corner_width)
    shapes = [
        pltpu.VMEM((parts, shots, first_width), kind),
        pltpu.VMEM((parts, shots, second_width), kind),
    ]
    if tick >= ticks - 2:
        shapes.append(pltpu.VMEM((parts, shots, corner_width), kind))
    return shapes


def cost(heavy):
    return pl.CostEstimate(flops=10**10 if heavy else 0, bytes_accessed=1, transcendentals=0)


def left_side(sources):
    _, _, parts, shots, edge_width = sources.shape
    return pltpu.VMEM((2 * parts * shots, 4 * edge_width), sources.dtype)


def middle_tick(tick, ticks, stream, first_in, second_in, corner_in, sources, operators):
    shapes = tick_shapes(sources, corner_in.shape[-1], tick, ticks)
    return pl.pallas_call(
        functools.partial(middle_kernel, tick, stream, corner_in.shape[-1]),
        out_shape=shapes,
        in_specs=[VMEM] * 5,
        out_specs=[VMEM] * len(shapes),
        scratch_shapes=[left_side(sources)],
        compiler_params=pltpu.CompilerParams(vmem_limit_bytes=VMEM_LIMIT),
        cost_estimate=cost(tick == 0 and stream == 0),
        name="tick" + str(tick) + "_stream" + str(stream),
    )(first_in, second_in, corner_in, sources, operators)


def last_tick(
    counts, tick, ticks, stream, roster, first_in, second_in, sources, operators, history, so_far,
    corner_width,
):
    _, batches, parts, shots, edge_width = sources.shape
    kind = sources.dtype
    outs = [jax.ShapeDtypeStruct((2, batches, parts, shots, edge_width), kind)] * 2
    outs += [jax.ShapeDtypeStruct((batches, parts, shots, corner_width), kind)] * 2
    operands = [roster, first_in, second_in, sources, operators]
    in_specs = [SMEM] + [VMEM] * 4
    aliases = {}
    if so_far is None:
        for traces in history:
            operands += list(traces)
        in_specs += [VMEM] * 6
        histories = (0, 1)
    else:
        aliases = {len(operands) + i: i for i in range(4)}
        operands += list(so_far)
        in_specs += [HBM] * 4
        histories = ()
    return pl.pallas_call(
        functools.partial(last_kernel, counts, tick, stream, histories, corner_width),
        out_shape=outs,
        in_specs=in_specs,
        out_specs=[HBM] * 4,
        scratch_shapes=[left_side(sources)]
        + tick_shapes(sources, corner_width, tick, ticks)
        + [pltpu.SemaphoreType.DMA((2, 3)), pltpu.SemaphoreType.DMA((3, 3))],
        input_output_aliases=aliases,
        compiler_params=pltpu.CompilerParams(vmem_limit_bytes=VMEM_LIMIT),
        cost_estimate=cost(False),
        name="tick" + str(tick) + "_stream" + str(stream),
    )(*operands)


def move(array, counts, step_of_cell):
    row_count, col_count = counts
    pairs = []
    for row in range(row_count):
        for col in range(col_count):
            down, right = step_of_cell(row, col)
            to_row = (row + down) % row_count
            to_col = (col + right) % col_count
            pairs.append((row * col_count + col, to_row * col_count + to_col))
    return lax.ppermute(array, ("row", "col"), pairs)


def sense(row, col, tick, stream):
    return -1 if direction_at(row, col, tick, stream) else 1


def by_row(array, counts, tick, stream):
    return move(array, counts, lambda row, col: (sense(row, col, tick - 1, stream), 0))


def by_col(array, counts, tick, stream):
    return move(array, counts, lambda row, col: (0, sense(row, col, tick - 1, stream)))


def by_diagonal(array, counts, stream):
    return move(array, counts, lambda row, col: (sense(row, col, 0, stream),) * 2)


def shards(
    southeast_edges, northwest_edges, southeast_corners, northwest_corners, operators, sources,
    roster,
):
    counts = (lax.axis_size("row"), lax.axis_size("col"))
    ticks = roster.shape[1]
    corner_width = southeast_corners.shape[-1]
    roster = roster.transpose(0, 2, 1)
    states = (
        southeast_edges[0, 0], northwest_edges[0, 0], southeast_corners[0, 0],
        northwest_corners[0, 0],
    )
    slots = [select_initial(counts, 0, roster, states), None]
    *rest, prepared, picked = load_operators(
        counts, 1, roster, states, operators[0, 0], sources[0, 0]
    )
    slots[1] = rest
    corners = [None, None]
    firsts = [slots[stream][0] for stream in range(2)]
    seconds = [slots[stream][1] for stream in range(2)]
    outs = None
    for tick in range(ticks):
        done = []
        for stream in range(2):
            second_in = by_col(seconds[stream], counts, tick, stream)
            if tick == 0:
                corners[stream] = by_diagonal(slots[stream][2], counts, stream)
            first_in = by_row(firsts[stream], counts, tick, stream)
            if tick < ticks - 1:
                done.append(
                    middle_tick(
                        tick, ticks, stream, first_in, second_in, corners[stream], picked, prepared
                    )
                )
            else:
                outs = last_tick(
                    counts, tick, ticks, stream, roster, first_in, second_in, picked, prepared,
                    history, outs, corner_width,
                )
        if tick < ticks - 1:
            history = done
            firsts = [done[0][0], done[1][0]]
            seconds = [done[0][1], done[1][1]]
    return tuple(array[None, None] for array in outs)


def solution(mesh):
    edges = P("row", "col", None, None, None, None, None)
    corners = P("row", "col", None, None, None, None)
    return jax.shard_map(
        shards,
        mesh=mesh,
        in_specs=(edges, edges, corners, corners, corners, corners, P()),
        out_specs=(edges, edges, corners, corners),
        check_vma=False,
    )
```

time: 69 us -> 60.9 us (0.88)
  the two profiles are of different devices: /device:TPU:8 before, /device:TPU:0 now
where the time goes in v3:
time: 60.9 us; the launch traced here: 59.9 us
  Pallas kernels  21.8 us (36%)
  starting transfers between devices  18.6 us (31%)
  waiting for transfers between devices  17.9 us (29%)
  between operations  0.74 us (1%)
  local copies, waits for them, and re-layouts  0.68 us (1%)
    ppermute x14, starting transfers between devices, move(): return lax.ppermute(array, ('row', 'col'), pairs)  18.6 us
    ppermute x14, waiting for transfers between devices, move(): return lax.ppermute(array, ('row', 'col'), pairs)  17.9 us
    pallas_call x4, Pallas kernels, middle_tick(): pl.pallas_call(functools.partial(middle_kernel, tick, stream, corner_in.s...  9.02 us
    pallas_call x2, Pallas kernels, last_tick(): pl.pallas_call(functools.partial(last_kernel, counts, tick, stream, histo...  7.27 us
    pallas_call x1, Pallas kernels, load_operators(): pl.pallas_call(functools.partial(load_kernel, counts, stream), out_shape=...  3.86 us
    pallas_call x1, Pallas kernels, select_initial(): pl.pallas_call(functools.partial(select_kernel, counts, stream), out_shap...  1.7 us
  transfers between devices with their start and end apart: 14, of which 6 were waited for; matrix products, arithmetic and copies ran while one was open for 0% of the time, Pallas kernels for 28%

profile of v3, /device:TPU:0, one launch (start us, length us, event | category | flops | bytes accessed | tf_op | source)
XLA Modules:
  0.0 59.9 jit_solution(7624445081789971294)
XLA Ops:
  0.6 0.0 copy-start
  0.6 0.7 %copy-done = s32[2,3,2]{1,2,0:T(2,128)S(1)} copy-done((s32[2,3,2]{1,2,0:T(2,128)S(1)}, s32[2,3,2]{1,2,0:T(2,128)}, u32[]{:S(2)}) %copy-start) | copy-done | bytes 72
  1.3 1.7 %select_initial.1 = (bf16[2,96,768]{2,1,0:T(8,128)(2,1)S(1)}, bf16[2,96,896]{2,1,0:T(8,128)(2,1)S(1)}, bf16[2,96,128]{2,1,0:T(8,128)(2,1)S(1)}) custom-call(s32[2,2,3]{2,1,0:T(2,128)S(1)} %bitcast.11, bf16[2,2,2,96,768]{4,3,2,1,0:T(8,128)(2,1)} %bitcast.16, bf16[2,2,2,96,768]{4,3,2,1,0:T(8,128)(2,1)} %bitcast.18, bf16[2,2,96,128]{3,2,1,0:T(8,128)(2,1)} %bitcast.23, ...), custom_call_target="tpu_custom_call" | custom-call | tf_op jit(solution)/shard_map/select_initial/pallas_call | solution.py:86
  3.0 0.5 collective-permute-start.8
  3.5 3.4 %collective-permute-start.7 = (bf16[2,96,768]{2,1,0:T(8,128)(2,1)S(1)}, bf16[2,96,768]{2,1,0:T(8,128)(2,1)S(1)}, u32[]{:S(2)}, u32[]{:S(2)}) collective-permute-start(bf16[2,96,768]{2,1,0:T(8,128)(2,1)S(1)} %get-tuple-element.39), channel_id=1, source_target_pairs={{0,4},{1,29},{2,6},{3,31},{4,0},{5,9},{6,2},{7,11},{8,12},{9,5},{1... | collective-permute-start | bytes 884744 | tf_op jit(solution)/shard_map/ppermute | solution.py:391
  7.0 3.3 %collective-permute-start.9 = (bf16[2,96,128]{2,1,0:T(8,128)(2,1)S(1)}, bf16[2,96,128]{2,1,0:T(8,128)(2,1)S(1)}, u32[]{:S(2)}, u32[]{:S(2)}) collective-permute-start(bf16[2,96,128]{2,1,0:T(8,128)(2,1)S(1)} %get-tuple-element.41), channel_id=1, source_target_pairs={{0,31},{1,6},{2,29},{3,4},{4,9},{5,0},{6,11},{7,2},{8,7},{9,14},{1... | collective-permute-start | bytes 147464 | tf_op jit(solution)/shard_map/ppermute | solution.py:391
  10.2 3.9 %load_operators.1 = (bf16[2,96,768]{2,1,0:T(8,128)(2,1)S(1)}, bf16[2,96,896]{2,1,0:T(8,128)(2,1)S(1)}, bf16[2,96,128]{2,1,0:T(8,128)(2,1)S(1)}, bf16[2,3072,768]...) custom-call(s32[2,2,3]{2,1,0:T(2,128)S(1)} %bitcast.12, bf16[2,2,2,96,768]{4,3,2,1,0:T(8,128)(2,1)} %bitcast.17, ...), custom_call_target="tpu_custom_call" | custom-call | bytes 1 | tf_op jit(solution)/shard_map/load_operators/pallas_call | solution.py:142
  14.1 0.1 collective-permute-start.2
  14.2 4.6 %collective-permute-start = (bf16[2,96,768]{2,1,0:T(8,128)(2,1)S(1)}, bf16[2,96,768]{2,1,0:T(8,128)(2,1)S(1)}, u32[]{:S(2)}, u32[]{:S(2)}) collective-permute-start(bf16[2,96,768]{2,1,0:T(8,128)(2,1)S(1)} %get-tuple-element.30), channel_id=1, source_target_pairs={{0,28},{1,5},{2,30},{3,7},{4,8},{5,1},{6,10},{7,3},{8,4},{9,13},{1... | collective-permute-start | bytes 884744 | tf_op jit(solution)/shard_map/ppermute | solution.py:391
  18.8 0.0 collective-permute-done.9.corner_in
  18.8 0.2 collective-permute-start.1
  18.9 0.0 collective-permute-done.7.first_in
  18.9 2.3 %tick0_stream0.1 = (bf16[2,96,896]{2,1,0:T(8,128)(2,1)S(1)}, bf16[2,96,896]{2,1,0:T(8,128)(2,1)S(1)}) custom-call(bf16[2,96,768]{2,1,0:T(8,128)(2,1)S(1)} %collective-permute-done.7.first_in, bf16[2,96,896]{2,1,0:T(8,128)(2,1)S(1)} %collective-permute-done.8.second_in, bf16[2,96,128]{2,1,0:T(8,128)(2,1)S(1)} %collective-permute-done.9.corner_in, ...), custom_call_target="tpu_custom_call" | custom-call | flops 10000000000 | bytes 1 | tf_op jit(solution)/shard_map/tick0_stream0/pallas_call | solution.py:334
  21.2 2.1 %collective-permute-start.10 = (bf16[2,96,896]{2,1,0:T(8,128)(2,1)S(1)}, bf16[2,96,896]{2,1,0:T(8,128)(2,1)S(1)}, u32[]{:S(2)}, u32[]{:S(2)}) collective-permute-start(bf16[2,96,896]{2,1,0:T(8,128)(2,1)S(1)} %get-tuple-element.42), channel_id=1, source_target_pairs={{0,28},{1,5},{2,30},{3,7},{4,8},{5,1},{6,10},{7,3},{8,4},{9,13},{1... | collective-permute-start | bytes 1032200 | tf_op jit(solution)/shard_map/ppermute | solution.py:391
  23.3 1.0 %collective-permute-done.first_in = bf16[2,96,768]{2,1,0:T(8,128)(2,1)S(1)} collective-permute-done((bf16[2,96,768]{2,1,0:T(8,128)(2,1)S(1)}, bf16[2,96,768]{2,1,0:T(8,128)(2,1)S(1)}, u32[]{:S(2)}, u32[]{:S(2)}) %collective-permute-start) | collective-permute-done | bytes 294944 | tf_op jit(solution)/shard_map/ppermute | solution.py:391
  24.3 4.6 %collective-permute-done.1.second_in = bf16[2,96,896]{2,1,0:T(8,128)(2,1)S(1)} collective-permute-done((bf16[2,96,896]{2,1,0:T(8,128)(2,1)S(1)}, bf16[2,96,896]{2,1,0:T(8,128)(2,1)S(1)}, u32[]{:S(2)}, u32[]{:S(2)}) %collective-permute-start.1) | collective-permute-done | bytes 344096 | tf_op jit(solution)/shard_map/ppermute | solution.py:391
  28.9 2.3 %tick0_stream1.1 = (bf16[2,96,896]{2,1,0:T(8,128)(2,1)S(1)}, bf16[2,96,896]{2,1,0:T(8,128)(2,1)S(1)}) custom-call(bf16[2,96,768]{2,1,0:T(8,128)(2,1)S(1)} %collective-permute-done.first_in, bf16[2,96,896]{2,1,0:T(8,128)(2,1)S(1)} %collective-permute-done.1.second_in, bf16[2,96,128]{2,1,0:T(8,128)(2,1)S(1)} %collective-permute-done.2.corner_in, ...), custom_call_target="tpu_custom_call" | custom-call | bytes 1 | tf_op jit(solution)/shard_map/tick0_stream1/pallas_call | solution.py:334
  31.2 0.1 collective-permute-start.3
  31.3 1.1 %collective-permute-start.4 = (bf16[2,96,896]{2,1,0:T(8,128)(2,1)S(1)}, bf16[2,96,896]{2,1,0:T(8,128)(2,1)S(1)}, u32[]{:S(2)}, u32[]{:S(2)}) collective-permute-start(bf16[2,96,896]{2,1,0:T(8,128)(2,1)S(1)} %get-tuple-element.36), channel_id=1, source_target_pairs={{0,1},{1,0},{2,3},{3,2},{4,7},{5,6},{6,5},{7,4},{8,9},{9,8},{10,11... | collective-permute-start | bytes 1032200 | tf_op jit(solution)/shard_map/ppermute | solution.py:391
  32.4 3.9 %collective-permute-done.11.second_in = bf16[2,96,896]{2,1,0:T(8,128)(2,1)S(1)} collective-permute-done((bf16[2,96,896]{2,1,0:T(8,128)(2,1)S(1)}, bf16[2,96,896]{2,1,0:T(8,128)(2,1)S(1)}, u32[]{:S(2)}, u32[]{:S(2)}) %collective-permute-start.11) | collective-permute-done | bytes 344096 | tf_op jit(solution)/shard_map/ppermute | solution.py:391
  36.3 2.2 %tick1_stream0.1 = (bf16[2,96,896]{2,1,0:T(8,128)(2,1)S(1)}, bf16[2,96,768]{2,1,0:T(8,128)(2,1)S(1)}, bf16[2,96,128]{2,1,0:T(8,128)(2,1)S(1)}) custom-call(bf16[2,96,896]{2,1,0:T(8,128)(2,1)S(1)} %collective-permute-done.10.first_in, bf16[2,96,896]{2,1,0:T(8,128)(2,1)S(1)} %collective-permute-done.11.second_in, ...), custom_call_target="tpu_custom_call" | custom-call | bytes 1 | tf_op jit(solution)/shard_map/tick1_stream0/pallas_call | solution.py:334
  38.5 0.0 copy-start.1
  38.6 0.1 collective-permute-start.12
  38.6 3.5 %collective-permute-done.3.first_in = bf16[2,96,896]{2,1,0:T(8,128)(2,1)S(1)} collective-permute-done((bf16[2,96,896]{2,1,0:T(8,128)(2,1)S(1)}, bf16[2,96,896]{2,1,0:T(8,128)(2,1)S(1)}, u32[]{:S(2)}, u32[]{:S(2)}) %collective-permute-start.3) | collective-permute-done | bytes 344096 | tf_op jit(solution)/shard_map/ppermute | solution.py:391
  42.2 2.3 %tick1_stream1.1 = (bf16[2,96,896]{2,1,0:T(8,128)(2,1)S(1)}, bf16[2,96,768]{2,1,0:T(8,128)(2,1)S(1)}, bf16[2,96,128]{2,1,0:T(8,128)(2,1)S(1)}) custom-call(bf16[2,96,896]{2,1,0:T(8,128)(2,1)S(1)} %collective-permute-done.3.first_in, bf16[2,96,896]{2,1,0:T(8,128)(2,1)S(1)} %collective-permute-done.4.second_in, ...), custom_call_target="tpu_custom_call" | custom-call | bytes 1 | tf_op jit(solution)/shard_map/tick1_stream1/pallas_call | solution.py:334
  44.4 2.0 %collective-permute-start.5 = (bf16[2,96,896]{2,1,0:T(8,128)(2,1)S(1)}, bf16[2,96,896]{2,1,0:T(8,128)(2,1)S(1)}, u32[]{:S(2)}, u32[]{:S(2)}) collective-permute-start(bf16[2,96,896]{2,1,0:T(8,128)(2,1)S(1)} %get-tuple-element.37.refs_3_), channel_id=1, source_target_pairs={{0,28},{1,5},{2,30},{3,7},{4,8},{5,1},{6,10},{7,3},{8,4},{9,13},{1... | collective-permute-start | bytes 1032200 | tf_op jit(solution)/shard_map/ppermute | solution.py:391
  46.5 0.7 %collective-permute-start.13 = (bf16[2,96,768]{2,1,0:T(8,128)(2,1)S(1)}, bf16[2,96,768]{2,1,0:T(8,128)(2,1)S(1)}, u32[]{:S(2)}, u32[]{:S(2)}) collective-permute-start(bf16[2,96,768]{2,1,0:T(8,128)(2,1)S(1)} %get-tuple-element.45.refs_1_), channel_id=1, source_target_pairs={{0,1},{1,0},{2,3},{3,2},{4,7},{5,6},{6,5},{7,4},{8,9},{9,8},{10,11... | collective-permute-start | bytes 884744 | tf_op jit(solution)/shard_map/ppermute | solution.py:391
  47.2 0.5 collective-permute-start.6
  47.7 0.7 %collective-permute-done.13.second_in = bf16[2,96,768]{2,1,0:T(8,128)(2,1)S(1)} collective-permute-done((bf16[2,96,768]{2,1,0:T(8,128)(2,1)S(1)}, bf16[2,96,768]{2,1,0:T(8,128)(2,1)S(1)}, u32[]{:S(2)}, u32[]{:S(2)}) %collective-permute-start.13) | collective-permute-done | bytes 294944 | tf_op jit(solution)/shard_map/ppermute | solution.py:391
  48.4 3.7 %tick2_stream0.1 = (bf16[2,2,2,96,768]{4,3,2,1,0:T(8,128)(2,1)}, bf16[2,2,2,96,768]{4,3,2,1,0:T(8,128)(2,1)}, bf16[2,2,96,128]{3,2,1,0:T(8,128)(2,1)}, bf16[2,2,96,128]{3,2,1,0:T(8,128)(2,1)}) custom-call(s32[2,2,3]{2,1,0:T(2,128)S(1)} %bitcast.13, bf16[2,96,896]{2,1,0:T(8,128)(2,1)S(1)} %collective-permute-done.12.first_in, ...), custom_call_target="tpu_custom_call" | custom-call | bytes 1 | tf_op jit(solution)/shard_map/tick2_stream0/pallas_call | solution.py:367
  52.1 4.2 %collective-permute-done.6.second_in = bf16[2,96,768]{2,1,0:T(8,128)(2,1)S(1)} collective-permute-done((bf16[2,96,768]{2,1,0:T(8,128)(2,1)S(1)}, bf16[2,96,768]{2,1,0:T(8,128)(2,1)S(1)}, u32[]{:S(2)}, u32[]{:S(2)}) %collective-permute-start.6) | collective-permute-done | bytes 294944 | tf_op jit(solution)/shard_map/ppermute | solution.py:391
  56.2 3.6 %tick2_stream1.1 = (bf16[2,2,2,96,768]{4,3,2,1,0:T(8,128)(2,1)}, bf16[2,2,2,96,768]{4,3,2,1,0:T(8,128)(2,1)}, bf16[2,2,96,128]{3,2,1,0:T(8,128)(2,1)}, bf16[2,2,96,128]{3,2,1,0:T(8,128)(2,1)}) custom-call(s32[2,2,3]{2,1,0:T(2,128)S(1)} %bitcast.14, ...), custom_call_target="tpu_custom_call", output_to_operand_aliasing={{0}: (5, {}), {1}: (6, {}), {2}: (7, {}), {3}: (8, {})} | custom-call | bytes 1 | tf_op jit(solution)/shard_map/tick2_stream1/pallas_call | solution.py:367
  (8 shorter events, 0.0 us)
Async XLA Ops:
  0.6 0.7 %copy-start = (s32[2,3,2]{1,2,0:T(2,128)S(1)}, s32[2,3,2]{1,2,0:T(2,128)}, u32[]{:S(2)}) copy-start(s32[2,3,2]{1,2,0:T(2,128)} %param.13) | copy-start | bytes 148
  3.0 15.9 %collective-permute-start.8 = (bf16[2,96,896]{2,1,0:T(8,128)(2,1)S(1)}, bf16[2,96,896]{2,1,0:T(8,128)(2,1)S(1)}, u32[]{:S(2)}, u32[]{:S(2)}) collective-permute-start(bf16[2,96,896]{2,1,0:T(8,128)(2,1)S(1)} %get-tuple-element.40), channel_id=1, source_target_pairs={{0,1},{1,0},{2,3},{3,2},{4,7},{5,6},{6,5},{7,4},{8,9},{9,8},{10,11... | collective-permute-start | bytes 1032200 | tf_op jit(solution)/shard_map/ppermute | solution.py:391
  3.5 15.4 %collective-permute-start.7 = (bf16[2,96,768]{2,1,0:T(8,128)(2,1)S(1)}, bf16[2,96,768]{2,1,0:T(8,128)(2,1)S(1)}, u32[]{:S(2)}, u32[]{:S(2)}) collective-permute-start(bf16[2,96,768]{2,1,0:T(8,128)(2,1)S(1)} %get-tuple-element.39), channel_id=1, source_target_pairs={{0,4},{1,29},{2,6},{3,31},{4,0},{5,9},{6,2},{7,11},{8,12},{9,5},{1... | collective-permute-start | bytes 884744 | tf_op jit(solution)/shard_map/ppermute | solution.py:391
  7.0 11.8 %collective-permute-start.9 = (bf16[2,96,128]{2,1,0:T(8,128)(2,1)S(1)}, bf16[2,96,128]{2,1,0:T(8,128)(2,1)S(1)}, u32[]{:S(2)}, u32[]{:S(2)}) collective-permute-start(bf16[2,96,128]{2,1,0:T(8,128)(2,1)S(1)} %get-tuple-element.41), channel_id=1, source_target_pairs={{0,31},{1,6},{2,29},{3,4},{4,9},{5,0},{6,11},{7,2},{8,7},{9,14},{1... | collective-permute-start | bytes 147464 | tf_op jit(solution)/shard_map/ppermute | solution.py:391
  14.1 9.2 %collective-permute-start.2 = (bf16[2,96,128]{2,1,0:T(8,128)(2,1)S(1)}, bf16[2,96,128]{2,1,0:T(8,128)(2,1)S(1)}, u32[]{:S(2)}, u32[]{:S(2)}) collective-permute-start(bf16[2,96,128]{2,1,0:T(8,128)(2,1)S(1)} %get-tuple-element.32), channel_id=1, source_target_pairs={{0,5},{1,28},{2,7},{3,30},{4,3},{5,10},{6,1},{7,8},{8,13},{9,4},{1... | collective-permute-start | bytes 147464 | tf_op jit(solution)/shard_map/ppermute | solution.py:391
  14.2 10.1 %collective-permute-start = (bf16[2,96,768]{2,1,0:T(8,128)(2,1)S(1)}, bf16[2,96,768]{2,1,0:T(8,128)(2,1)S(1)}, u32[]{:S(2)}, u32[]{:S(2)}) collective-permute-start(bf16[2,96,768]{2,1,0:T(8,128)(2,1)S(1)} %get-tuple-element.30), channel_id=1, source_target_pairs={{0,28},{1,5},{2,30},{3,7},{4,8},{5,1},{6,10},{7,3},{8,4},{9,13},{1... | collective-permute-start | bytes 884744 | tf_op jit(solution)/shard_map/ppermute | solution.py:391
  18.8 10.1 %collective-permute-start.1 = (bf16[2,96,896]{2,1,0:T(8,128)(2,1)S(1)}, bf16[2,96,896]{2,1,0:T(8,128)(2,1)S(1)}, u32[]{:S(2)}, u32[]{:S(2)}) collective-permute-start(bf16[2,96,896]{2,1,0:T(8,128)(2,1)S(1)} %get-tuple-element.31), channel_id=1, source_target_pairs={{0,3},{1,2},{2,1},{3,0},{4,5},{5,4},{6,7},{7,6},{8,11},{9,10},{10,... | collective-permute-start | bytes 1032200 | tf_op jit(solution)/shard_map/ppermute | solution.py:391
  21.2 11.2 %collective-permute-start.10 = (bf16[2,96,896]{2,1,0:T(8,128)(2,1)S(1)}, bf16[2,96,896]{2,1,0:T(8,128)(2,1)S(1)}, u32[]{:S(2)}, u32[]{:S(2)}) collective-permute-start(bf16[2,96,896]{2,1,0:T(8,128)(2,1)S(1)} %get-tuple-element.42), channel_id=1, source_target_pairs={{0,28},{1,5},{2,30},{3,7},{4,8},{5,1},{6,10},{7,3},{8,4},{9,13},{1... | collective-permute-start | bytes 1032200 | tf_op jit(solution)/shard_map/ppermute | solution.py:391
  23.3 13.0 %collective-permute-start.11 = (bf16[2,96,896]{2,1,0:T(8,128)(2,1)S(1)}, bf16[2,96,896]{2,1,0:T(8,128)(2,1)S(1)}, u32[]{:S(2)}, u32[]{:S(2)}) collective-permute-start(bf16[2,96,896]{2,1,0:T(8,128)(2,1)S(1)} %get-tuple-element.43), channel_id=1, source_target_pairs={{0,3},{1,2},{2,1},{3,0},{4,5},{5,4},{6,7},{7,6},{8,11},{9,10},{10,... | collective-permute-start | bytes 1032200 | tf_op jit(solution)/shard_map/ppermute | solution.py:391
  31.2 11.0 %collective-permute-start.3 = (bf16[2,96,896]{2,1,0:T(8,128)(2,1)S(1)}, bf16[2,96,896]{2,1,0:T(8,128)(2,1)S(1)}, u32[]{:S(2)}, u32[]{:S(2)}) collective-permute-start(bf16[2,96,896]{2,1,0:T(8,128)(2,1)S(1)} %get-tuple-element.35), channel_id=1, source_target_pairs={{0,4},{1,29},{2,6},{3,31},{4,0},{5,9},{6,2},{7,11},{8,12},{9,5},{1... | collective-permute-start | bytes 1032200 | tf_op jit(solution)/shard_map/ppermute | solution.py:391
  31.3 10.9 %collective-permute-start.4 = (bf16[2,96,896]{2,1,0:T(8,128)(2,1)S(1)}, bf16[2,96,896]{2,1,0:T(8,128)(2,1)S(1)}, u32[]{:S(2)}, u32[]{:S(2)}) collective-permute-start(bf16[2,96,896]{2,1,0:T(8,128)(2,1)S(1)} %get-tuple-element.36), channel_id=1, source_target_pairs={{0,1},{1,0},{2,3},{3,2},{4,7},{5,6},{6,5},{7,4},{8,9},{9,8},{10,11... | collective-permute-start | bytes 1032200 | tf_op jit(solution)/shard_map/ppermute | solution.py:391
  38.5 9.9 %copy-start.1 = (s32[2,3,2]{1,2,0:T(2,128)S(1)}, s32[2,3,2]{1,2,0:T(2,128)}, u32[]{:S(2)}) copy-start(s32[2,3,2]{1,2,0:T(2,128)} %param.13) | copy-start | bytes 148
  38.6 9.8 %collective-permute-start.12 = (bf16[2,96,896]{2,1,0:T(8,128)(2,1)S(1)}, bf16[2,96,896]{2,1,0:T(8,128)(2,1)S(1)}, u32[]{:S(2)}, u32[]{:S(2)}) collective-permute-start(bf16[2,96,896]{2,1,0:T(8,128)(2,1)S(1)} %get-tuple-element.44.refs_0_), channel_id=1, source_target_pairs={{0,4},{1,29},{2,6},{3,31},{4,0},{5,9},{6,2},{7,11},{8,12},{9,5},{1... | collective-permute-start | bytes 1032200 | tf_op jit(solution)/shard_map/ppermute | solution.py:391
  44.4 11.8 %collective-permute-start.5 = (bf16[2,96,896]{2,1,0:T(8,128)(2,1)S(1)}, bf16[2,96,896]{2,1,0:T(8,128)(2,1)S(1)}, u32[]{:S(2)}, u32[]{:S(2)}) collective-permute-start(bf16[2,96,896]{2,1,0:T(8,128)(2,1)S(1)} %get-tuple-element.37.refs_3_), channel_id=1, source_target_pairs={{0,28},{1,5},{2,30},{3,7},{4,8},{5,1},{6,10},{7,3},{8,4},{9,13},{1... | collective-permute-start | bytes 1032200 | tf_op jit(solution)/shard_map/ppermute | solution.py:391
  46.5 1.9 %collective-permute-start.13 = (bf16[2,96,768]{2,1,0:T(8,128)(2,1)S(1)}, bf16[2,96,768]{2,1,0:T(8,128)(2,1)S(1)}, u32[]{:S(2)}, u32[]{:S(2)}) collective-permute-start(bf16[2,96,768]{2,1,0:T(8,128)(2,1)S(1)} %get-tuple-element.45.refs_1_), channel_id=1, source_target_pairs={{0,1},{1,0},{2,3},{3,2},{4,7},{5,6},{6,5},{7,4},{8,9},{9,8},{10,11... | collective-permute-start | bytes 884744 | tf_op jit(solution)/shard_map/ppermute | solution.py:391
  47.2 9.0 %collective-permute-start.6 = (bf16[2,96,768]{2,1,0:T(8,128)(2,1)S(1)}, bf16[2,96,768]{2,1,0:T(8,128)(2,1)S(1)}, u32[]{:S(2)}, u32[]{:S(2)}) collective-permute-start(bf16[2,96,768]{2,1,0:T(8,128)(2,1)S(1)} %get-tuple-element.38.refs_4_), channel_id=1, source_target_pairs={{0,3},{1,2},{2,1},{3,0},{4,5},{5,4},{6,7},{7,6},{8,11},{9,10},{10,... | collective-permute-start | bytes 884744 | tf_op jit(solution)/shard_map/ppermute | solution.py:391

commit v4 on v3

--- a/solution.py
+++ b/solution.py
@@ -64,12 +64,36 @@
                 act(pltpu.make_async_copy(source, target, sems.at[index]))
 
 
-def select_kernel(counts, stream, roster, se_edges, nw_edges, se_corners, nw_corners, *refs):
-    outs, sems = refs[:3], refs[3]
-    for act in (start, wait):
-        select_slots(
-            counts, stream, roster, (se_edges, nw_edges), (se_corners, nw_corners), outs, sems, act
-        )
+def select_kernel(
+    counts, stream, roster, se_edges, nw_edges, se_corners, nw_corners, by_row, by_col, by_diagonal,
+    numbers, all_edges, all_corners, sems
+):
+    edges, corners = (se_edges, nw_edges), (se_corners, nw_corners)
+    edge_width = by_row.shape[-1]
+    corner_width = by_diagonal.shape[-1]
+    roster_copy = pltpu.make_async_copy(roster, numbers, sems.at[0])
+    roster_copy.start()
+    own = 1 - own_direction(-1, stream)
+
+    def fetch(act):
+        for going in range(2):
+
+            @pl.when(own_direction(-1, stream) == going)
+            def _():
+                act(pltpu.make_async_copy(edges[going], all_edges, sems.at[1]))
+
+            act(pltpu.make_async_copy(corners[going], all_corners.at[going], sems.at[2 + going]))
+
+    fetch(start)
+    roster_copy.wait()
+    chosen = [chosen_at_start(numbers, direction, counts) for direction in range(2)]
+    other = 1 - jnp.where(own == 0, chosen[1], chosen[0])
+    mine = jnp.where(own == 0, chosen[0], chosen[1])
+    fetch(wait)
+    by_row[...] = all_edges[0, other]
+    by_col[:, :, pl.ds(0, edge_width)] = all_edges[1, other]
+    by_col[:, :, pl.ds(edge_width, corner_width)] = all_corners[1 - own, other]
+    by_diagonal[...] = all_corners[own, mine]
 
 
 def slot_shapes(edges, corners):
@@ -83,12 +107,18 @@
 
 
 def select_initial(counts, stream, roster, states):
+    edges, _, corners, _ = states
     return pl.pallas_call(
         functools.partial(select_kernel, counts, stream),
-        out_shape=slot_shapes(states[0], states[2]),
-        in_specs=[SMEM] + [HBM] * 4,
+        out_shape=slot_shapes(edges, corners),
+        in_specs=[HBM] * 5,
         out_specs=[VMEM] * 3,
-        scratch_shapes=[pltpu.SemaphoreType.DMA((4,))],
+        scratch_shapes=[
+            pltpu.SMEM(roster.shape, roster.dtype),
+            pltpu.VMEM(edges.shape, edges.dtype),
+            pltpu.VMEM((2,) + corners.shape, corners.dtype),
+            pltpu.SemaphoreType.DMA((4,)),
+        ],
         compiler_params=pltpu.CompilerParams(vmem_limit_bytes=VMEM_LIMIT),
         name="select_initial",
     )(roster, *map(in_hbm, states))
@@ -98,7 +128,7 @@
     counts, stream, roster, se_edges, nw_edges, se_corners, nw_corners, operators, sources, *refs
 ):
     outs = refs[:3]
-    prepared, picked, select_sems, operator_sems, source_sems = refs[3:]
+    prepared, picked, flags, select_sems, operator_sems, source_sems = refs[3:]
     count, edge_width, _ = operators.shape
     copies = [
         pltpu.make_async_copy(
@@ -111,6 +141,7 @@
     source_copies = []
     for direction in range(2):
         mine = chosen_at_start(roster, direction, counts)
+        flags[direction] = jnp.full(flags.shape[1:], mine.astype(jnp.float32))
         for late in range(2):
             source_copies.append(
                 pltpu.make_async_copy(
@@ -145,9 +176,10 @@
         + [
             pltpu.VMEM((2, count * edge_width, edge_width), kind),
             pltpu.VMEM((2,) + sources.shape, kind),
+            pltpu.VMEM((2, 8, 128), jnp.float32),
         ],
         in_specs=[SMEM] + [HBM] * 6,
-        out_specs=[VMEM] * 5,
+        out_specs=[VMEM] * 6,
         scratch_shapes=[
             pltpu.SemaphoreType.DMA((4,)),
             pltpu.SemaphoreType.DMA((count,)),
@@ -162,7 +194,7 @@
 def compute(
     tick, stream, corner_width, first_in, second_in, corner_in, sources, operators, outs, left, act
 ):
-    first_out, second_out, *corner_out = outs
+    first_out, second_out = outs
     parts, shots, edge_width = sources.shape[2:]
     rows = parts * shots
     direction = own_direction(tick, stream)
@@ -209,10 +241,7 @@
 
             @pl.when(direction != end)
             def _():
-                for ref in corner_out:
-                    ref[...] = given
-                if second_out.shape[-1] > edge_width:
-                    second_out[:, :, corner_part] = given
+                second_out[:, :, corner_part] = given
 
         first_out[:, :, at] = first.astype(first_out.dtype).reshape(parts, shots, tile)
         second_out[:, :, at] = second.astype(second_out.dtype).reshape(parts, shots, tile)
@@ -230,36 +259,42 @@
 
 
 def last_kernel(
-    counts, tick, stream, histories, corner_width, roster, first_in, second_in, sources, operators,
-    *refs
+    tick, stream, histories, corner_width, flags, first_in, second_in, sources, operators, *refs
 ):
     count = len(histories)
-    older = [refs[3 * i : 3 * i + 3] for i in range(count)]
-    refs = refs[3 * count :]
+    older = [refs[2 * i : 2 * i + 2] for i in range(count)]
+    refs = refs[2 * count :]
     if not count:
         refs = refs[4:]
     edges_out, corners_out, (left, *outs, old_sems, sems) = refs[0:2], refs[2:4], refs[4:]
     edge_width = sources.shape[-1]
     edge_part = pl.ds(0, edge_width)
+    corner_part = pl.ds(edge_width, corner_width)
+
+    batches = {}
+    for at_tick in (tick - 1, tick) if count else (tick,):
+        chosen = jnp.max(flags[own_direction(at_tick, stream), :1]).astype(jnp.int32)
+        batches[at_tick, stream] = 1 - chosen if at_tick % 2 else chosen
+    if count:
+        chosen = jnp.max(flags[own_direction(tick - 1, 1 - stream), :1]).astype(jnp.int32)
+        batches[tick - 1, 1 - stream] = 1 - chosen if (tick - 1) % 2 else chosen
 
     def each(at_tick, at_stream, act_on):
         for direction in range(2):
 
             @pl.when(own_direction(at_tick, at_stream) == direction)
             def _():
-                batch = chosen_at_start(roster, direction, counts)
-                if at_tick % 2:
-                    batch = 1 - batch
+                batch = batches[at_tick, at_stream]
                 act_on(edges_out[direction], corners_out[direction], batch)
 
     def old_stores(index, act):
-        first, second, corner = older[index]
+        first, second = older[index]
 
         def act_on(edges, corners, batch):
             pairs = (
                 (first.at[:, :, edge_part], edges.at[0, batch]),
                 (second.at[:, :, edge_part], edges.at[1, batch]),
-                (corner, corners.at[batch]),
+                (second.at[:, :, corner_part], corners.at[batch]),
             )
             for place, (source, target) in enumerate(pairs):
                 act(pltpu.make_async_copy(source, target, old_sems.at[index, place]))
@@ -282,7 +317,9 @@
         each(
             tick, stream,
             lambda edges, corners, batch: act(
-                pltpu.make_async_copy(outs[2], corners.at[batch], sems.at[2, 0])
+                pltpu.make_async_copy(
+                    outs[1].at[:, :, corner_part], corners.at[batch], sems.at[2, 0]
+                )
             ),
         )
 
@@ -310,14 +347,10 @@
     _, _, parts, shots, edge_width = sources.shape
     kind = sources.dtype
     first_width = edge_width + (0 if tick == ticks - 1 else corner_width)
-    second_width = edge_width + (0 if tick >= ticks - 2 else corner_width)
-    shapes = [
+    return [
         pltpu.VMEM((parts, shots, first_width), kind),
-        pltpu.VMEM((parts, shots, second_width), kind),
+        pltpu.VMEM((parts, shots, edge_width + corner_width), kind),
     ]
-    if tick >= ticks - 2:
-        shapes.append(pltpu.VMEM((parts, shots, corner_width), kind))
-    return shapes
 
 
 def cost(heavy):
@@ -344,20 +377,20 @@
 
 
 def last_tick(
-    counts, tick, ticks, stream, roster, first_in, second_in, sources, operators, history, so_far,
+    tick, ticks, stream, flags, first_in, second_in, sources, operators, history, so_far,
     corner_width,
 ):
     _, batches, parts, shots, edge_width = sources.shape
     kind = sources.dtype
     outs = [jax.ShapeDtypeStruct((2, batches, parts, shots, edge_width), kind)] * 2
     outs += [jax.ShapeDtypeStruct((batches, parts, shots, corner_width), kind)] * 2
-    operands = [roster, first_in, second_in, sources, operators]
-    in_specs = [SMEM] + [VMEM] * 4
+    operands = [flags, first_in, second_in, sources, operators]
+    in_specs = [VMEM] * 5
     aliases = {}
     if so_far is None:
         for traces in history:
             operands += list(traces)
-        in_specs += [VMEM] * 6
+        in_specs += [VMEM] * 4
         histories = (0, 1)
     else:
         aliases = {len(operands) + i: i for i in range(4)}
@@ -365,7 +398,7 @@
         in_specs += [HBM] * 4
         histories = ()
     return pl.pallas_call(
-        functools.partial(last_kernel, counts, tick, stream, histories, corner_width),
+        functools.partial(last_kernel, tick, stream, histories, corner_width),
         out_shape=outs,
         in_specs=in_specs,
         out_specs=[HBM] * 4,
@@ -414,13 +447,13 @@
     counts = (lax.axis_size("row"), lax.axis_size("col"))
     ticks = roster.shape[1]
     corner_width = southeast_corners.shape[-1]
-    roster = roster.transpose(0, 2, 1)
+    roster = in_hbm(roster.transpose(0, 2, 1))
     states = (
         southeast_edges[0, 0], northwest_edges[0, 0], southeast_corners[0, 0],
         northwest_corners[0, 0],
     )
     slots = [select_initial(counts, 0, roster, states), None]
-    *rest, prepared, picked = load_operators(
+    *rest, prepared, picked, flags = load_operators(
         counts, 1, roster, states, operators[0, 0], sources[0, 0]
     )
     slots[1] = rest
@@ -443,8 +476,8 @@
                 )
             else:
                 outs = last_tick(
-                    counts, tick, ticks, stream, roster, first_in, second_in, picked, prepared,
-                    history, outs, corner_width,
+                    tick, ticks, stream, flags, first_in, second_in, picked, prepared, history, outs,
+                    corner_width,
                 )
         if tick < ticks - 1:
             history = done

time: 60.9 us -> 59.6 us (0.979); the launches traced: 59.9 us -> 59.4 us
  starting transfers between devices: 18.6 us -> 21.5 us
  waiting for transfers between devices: 17.9 us -> 16.5 us
  Pallas kernels: 21.8 us -> 20.7 us
  local copies, waits for them, and re-layouts: 0.68 us -> 0 us
    ppermute x14, starting transfers between devices: 18.6 us -> 21.5 us  [move(): return lax.ppermute(array, ('row', 'col'), pairs)]
    ppermute x14, waiting for transfers between devices: 17.9 us -> 16.5 us  [move(): return lax.ppermute(array, ('row', 'col'), pairs)]
    pallas_call x2, Pallas kernels: 7.27 us -> 6.19 us  [last_tick(): pl.pallas_call(functools.partial(last_kernel, tick, stream, histories, co...]
    unnamed x4 -> x0, local copies, waits for them, and re-layouts: 0.68 us -> none
  transfers between devices with their start and end apart: 14 -> 14, of which waited for: 6 -> 5; matrix products, arithmetic and copies ran while one was open for 0% -> 0% of each run, Pallas kernels for 28% -> 27%
where the time goes in v4:
time: 59.6 us; the launch traced here: 59.4 us
  starting transfers between devices  21.5 us (36%)
  Pallas kernels  20.7 us (35%)
  waiting for transfers between devices  16.5 us (28%)
  between operations  0.75 us (1%)
    ppermute x14, starting transfers between devices, move(): return lax.ppermute(array, ('row', 'col'), pairs)  21.5 us
    ppermute x14, waiting for transfers between devices, move(): return lax.ppermute(array, ('row', 'col'), pairs)  16.5 us
    pallas_call x4, Pallas kernels, middle_tick(): pl.pallas_call(functools.partial(middle_kernel, tick, stream, corner_in.s...  9.12 us
    pallas_call x2, Pallas kernels, last_tick(): pl.pallas_call(functools.partial(last_kernel, tick, stream, histories, co...  6.19 us
    pallas_call x1, Pallas kernels, load_operators(): pl.pallas_call(functools.partial(load_kernel, counts, stream), out_shape=...  3.98 us
    pallas_call x1, Pallas kernels, select_initial(): pl.pallas_call(functools.partial(select_kernel, counts, stream), out_shap...  1.38 us
  transfers between devices with their start and end apart: 14, of which 5 were waited for; matrix products, arithmetic and copies ran while one was open for 0% of the time, Pallas kernels for 27%

profile of v4, /device:TPU:0, one launch (start us, length us, event | category | flops | bytes accessed | tf_op | source)
XLA Modules:
  0.0 59.4 jit_solution(5690688335110090008)
XLA Ops:
  0.6 1.4 %select_initial.1 = (bf16[2,96,768]{2,1,0:T(8,128)(2,1)S(1)}, bf16[2,96,896]{2,1,0:T(8,128)(2,1)S(1)}, bf16[2,96,128]{2,1,0:T(8,128)(2,1)S(1)}) custom-call(s32[2,2,3]{2,1,0:T(2,128)} %bitcast.25, bf16[2,2,2,96,768]{4,3,2,1,0:T(8,128)(2,1)} %bitcast.12, bf16[2,2,2,96,768]{4,3,2,1,0:T(8,128)(2,1)} %bitcast.14, bf16[2,2,96,128]{3,2,1,0:T(8,128)(2,1)} %bitcast.19, ...), custom_call_target="tpu_custom_call" | custom-call | tf_op jit(solution)/shard_map/select_initial/pallas_call | solution.py:111
  2.0 0.6 collective-permute-start.8
  2.6 3.4 %collective-permute-start.7 = (bf16[2,96,768]{2,1,0:T(8,128)(2,1)S(1)}, bf16[2,96,768]{2,1,0:T(8,128)(2,1)S(1)}, u32[]{:S(2)}, u32[]{:S(2)}) collective-permute-start(bf16[2,96,768]{2,1,0:T(8,128)(2,1)S(1)} %get-tuple-element.39), channel_id=1, source_target_pairs={{0,4},{1,29},{2,6},{3,31},{4,0},{5,9},{6,2},{7,11},{8,12},{9,5},{1... | collective-permute-start | bytes 884744 | tf_op jit(solution)/shard_map/ppermute | solution.py:424
  6.0 3.3 %collective-permute-start.9 = (bf16[2,96,128]{2,1,0:T(8,128)(2,1)S(1)}, bf16[2,96,128]{2,1,0:T(8,128)(2,1)S(1)}, u32[]{:S(2)}, u32[]{:S(2)}) collective-permute-start(bf16[2,96,128]{2,1,0:T(8,128)(2,1)S(1)} %get-tuple-element.41), channel_id=1, source_target_pairs={{0,31},{1,6},{2,29},{3,4},{4,9},{5,0},{6,11},{7,2},{8,7},{9,14},{1... | collective-permute-start | bytes 147464 | tf_op jit(solution)/shard_map/ppermute | solution.py:424
  9.3 4.0 %load_operators.1 = (bf16[2,96,768]{2,1,0:T(8,128)(2,1)S(1)}, bf16[2,96,896]{2,1,0:T(8,128)(2,1)S(1)}, bf16[2,96,128]{2,1,0:T(8,128)(2,1)S(1)}, bf16[2,3072,768]...) custom-call(s32[2,2,3]{2,1,0:T(2,128)} %bitcast.26, ...), custom_call_target="tpu_custom_call" | custom-call | bytes 1 | tf_op jit(solution)/shard_map/load_operators/pallas_call | solution.py:173
  13.3 0.1 collective-permute-start.2
  13.4 4.6 %collective-permute-start = (bf16[2,96,768]{2,1,0:T(8,128)(2,1)S(1)}, bf16[2,96,768]{2,1,0:T(8,128)(2,1)S(1)}, u32[]{:S(2)}, u32[]{:S(2)}) collective-permute-start(bf16[2,96,768]{2,1,0:T(8,128)(2,1)S(1)} %get-tuple-element.30), channel_id=1, source_target_pairs={{0,28},{1,5},{2,30},{3,7},{4,8},{5,1},{6,10},{7,3},{8,4},{9,13},{1... | collective-permute-start | bytes 884744 | tf_op jit(solution)/shard_map/ppermute | solution.py:424
  17.9 0.0 collective-permute-done.9.corner_in
  18.0 0.2 collective-permute-start.1
  18.1 0.0 collective-permute-done.7.first_in
  18.1 0.0 collective-permute-done.8.second_in
  18.1 2.3 %tick0_stream0.1 = (bf16[2,96,896]{2,1,0:T(8,128)(2,1)S(1)}, bf16[2,96,896]{2,1,0:T(8,128)(2,1)S(1)}) custom-call(bf16[2,96,768]{2,1,0:T(8,128)(2,1)S(1)} %collective-permute-done.7.first_in, bf16[2,96,896]{2,1,0:T(8,128)(2,1)S(1)} %collective-permute-done.8.second_in, bf16[2,96,128]{2,1,0:T(8,128)(2,1)S(1)} %collective-permute-done.9.corner_in, ...), custom_call_target="tpu_custom_call" | custom-call | flops 10000000000 | bytes 1 | tf_op jit(solution)/shard_map/tick0_stream0/pallas_call | solution.py:367
  20.4 1.9 %collective-permute-start.10 = (bf16[2,96,896]{2,1,0:T(8,128)(2,1)S(1)}, bf16[2,96,896]{2,1,0:T(8,128)(2,1)S(1)}, u32[]{:S(2)}, u32[]{:S(2)}) collective-permute-start(bf16[2,96,896]{2,1,0:T(8,128)(2,1)S(1)} %get-tuple-element.42), channel_id=1, source_target_pairs={{0,28},{1,5},{2,30},{3,7},{4,8},{5,1},{6,10},{7,3},{8,4},{9,13},{1... | collective-permute-start | bytes 1032200 | tf_op jit(solution)/shard_map/ppermute | solution.py:424
  22.3 1.1 %collective-permute-done.first_in = bf16[2,96,768]{2,1,0:T(8,128)(2,1)S(1)} collective-permute-done((bf16[2,96,768]{2,1,0:T(8,128)(2,1)S(1)}, bf16[2,96,768]{2,1,0:T(8,128)(2,1)S(1)}, u32[]{:S(2)}, u32[]{:S(2)}) %collective-permute-start) | collective-permute-done | bytes 294944 | tf_op jit(solution)/shard_map/ppermute | solution.py:424
  23.5 4.6 %collective-permute-done.1.second_in = bf16[2,96,896]{2,1,0:T(8,128)(2,1)S(1)} collective-permute-done((bf16[2,96,896]{2,1,0:T(8,128)(2,1)S(1)}, bf16[2,96,896]{2,1,0:T(8,128)(2,1)S(1)}, u32[]{:S(2)}, u32[]{:S(2)}) %collective-permute-start.1) | collective-permute-done | bytes 344096 | tf_op jit(solution)/shard_map/ppermute | solution.py:424
  28.1 2.3 %tick0_stream1.1 = (bf16[2,96,896]{2,1,0:T(8,128)(2,1)S(1)}, bf16[2,96,896]{2,1,0:T(8,128)(2,1)S(1)}) custom-call(bf16[2,96,768]{2,1,0:T(8,128)(2,1)S(1)} %collective-permute-done.first_in, bf16[2,96,896]{2,1,0:T(8,128)(2,1)S(1)} %collective-permute-done.1.second_in, bf16[2,96,128]{2,1,0:T(8,128)(2,1)S(1)} %collective-permute-done.2.corner_in, ...), custom_call_target="tpu_custom_call" | custom-call | bytes 1 | tf_op jit(solution)/shard_map/tick0_stream1/pallas_call | solution.py:367
  30.4 0.1 collective-permute-start.3
  30.5 1.1 %collective-permute-start.4 = (bf16[2,96,896]{2,1,0:T(8,128)(2,1)S(1)}, bf16[2,96,896]{2,1,0:T(8,128)(2,1)S(1)}, u32[]{:S(2)}, u32[]{:S(2)}) collective-permute-start(bf16[2,96,896]{2,1,0:T(8,128)(2,1)S(1)} %get-tuple-element.36), channel_id=1, source_target_pairs={{0,1},{1,0},{2,3},{3,2},{4,7},{5,6},{6,5},{7,4},{8,9},{9,8},{10,11... | collective-permute-start | bytes 1032200 | tf_op jit(solution)/shard_map/ppermute | solution.py:424
  31.5 0.0 collective-permute-done.10.first_in
  31.6 3.9 %collective-permute-done.11.second_in = bf16[2,96,896]{2,1,0:T(8,128)(2,1)S(1)} collective-permute-done((bf16[2,96,896]{2,1,0:T(8,128)(2,1)S(1)}, bf16[2,96,896]{2,1,0:T(8,128)(2,1)S(1)}, u32[]{:S(2)}, u32[]{:S(2)}) %collective-permute-start.11) | collective-permute-done | bytes 344096 | tf_op jit(solution)/shard_map/ppermute | solution.py:424
  35.5 2.3 %tick1_stream0.1 = (bf16[2,96,896]{2,1,0:T(8,128)(2,1)S(1)}, bf16[2,96,896]{2,1,0:T(8,128)(2,1)S(1)}) custom-call(bf16[2,96,896]{2,1,0:T(8,128)(2,1)S(1)} %collective-permute-done.10.first_in, bf16[2,96,896]{2,1,0:T(8,128)(2,1)S(1)} %collective-permute-done.11.second_in, bf16[2,96,128]{2,1,0:T(8,128)(2,1)S(1)} %collective-permute-done.9.corner_in, ...), custom_call_target="tpu_custom_call" | custom-call | bytes 1 | tf_op jit(solution)/shard_map/tick1_stream0/pallas_call | solution.py:367
  37.7 0.1 collective-permute-start.12
  37.8 6.1 %collective-permute-start.13 = (bf16[2,96,896]{2,1,0:T(8,128)(2,1)S(1)}, bf16[2,96,896]{2,1,0:T(8,128)(2,1)S(1)}, u32[]{:S(2)}, u32[]{:S(2)}) collective-permute-start(bf16[2,96,896]{2,1,0:T(8,128)(2,1)S(1)} %get-tuple-element.45.refs_1_), channel_id=1, source_target_pairs={{0,1},{1,0},{2,3},{3,2},{4,7},{5,6},{6,5},{7,4},{8,9},{9,8},{10,11... | collective-permute-start | bytes 1032200 | tf_op jit(solution)/shard_map/ppermute | solution.py:424
  43.9 0.0 collective-permute-done.3.first_in
  43.9 0.0 collective-permute-done.4.second_in
  44.0 2.3 %tick1_stream1.1 = (bf16[2,96,896]{2,1,0:T(8,128)(2,1)S(1)}, bf16[2,96,896]{2,1,0:T(8,128)(2,1)S(1)}) custom-call(bf16[2,96,896]{2,1,0:T(8,128)(2,1)S(1)} %collective-permute-done.3.first_in, bf16[2,96,896]{2,1,0:T(8,128)(2,1)S(1)} %collective-permute-done.4.second_in, bf16[2,96,128]{2,1,0:T(8,128)(2,1)S(1)} %collective-permute-done.2.corner_in, ...), custom_call_target="tpu_custom_call" | custom-call | bytes 1 | tf_op jit(solution)/shard_map/tick1_stream1/pallas_call | solution.py:367
  46.2 0.1 collective-permute-start.5
  46.3 0.1 collective-permute-start.6
  46.4 3.1 %tick2_stream0.1 = (bf16[2,2,2,96,768]{4,3,2,1,0:T(8,128)(2,1)}, bf16[2,2,2,96,768]{4,3,2,1,0:T(8,128)(2,1)}, bf16[2,2,96,128]{3,2,1,0:T(8,128)(2,1)}, bf16[2,2,96,128]{3,2,1,0:T(8,128)(2,1)}) custom-call(f32[2,8,128]{2,1,0:T(8,128)S(1)} %get-tuple-element.29.flags, bf16[2,96,896]{2,1,0:T(8,128)(2,1)S(1)} %collective-permute-done.12.first_in, ...), custom_call_target="tpu_custom_call" | custom-call | bytes 1 | tf_op jit(solution)/shard_map/tick2_stream0/pallas_call | solution.py:400
  49.5 6.7 %collective-permute-done.5.first_in = bf16[2,96,896]{2,1,0:T(8,128)(2,1)S(1)} collective-permute-done((bf16[2,96,896]{2,1,0:T(8,128)(2,1)S(1)}, bf16[2,96,896]{2,1,0:T(8,128)(2,1)S(1)}, u32[]{:S(2)}, u32[]{:S(2)}) %collective-permute-start.5) | collective-permute-done | bytes 344096 | tf_op jit(solution)/shard_map/ppermute | solution.py:424
  56.3 0.1 collective-permute-done.6.second_in
  56.3 3.1 %tick2_stream1.1 = (bf16[2,2,2,96,768]{4,3,2,1,0:T(8,128)(2,1)}, bf16[2,2,2,96,768]{4,3,2,1,0:T(8,128)(2,1)}, bf16[2,2,96,128]{3,2,1,0:T(8,128)(2,1)}, bf16[2,2,96,128]{3,2,1,0:T(8,128)(2,1)}) custom-call(f32[2,8,128]{2,1,0:T(8,128)S(1)} %get-tuple-element.29.flags, ...), custom_call_target="tpu_custom_call", output_to_operand_aliasing={{0}: (5, {}), {1}: (6, {}), {2}: (7, {}), {3}: (8, {})} | custom-call | bytes 1 | tf_op jit(solution)/shard_map/tick2_stream1/pallas_call | solution.py:400
  (4 shorter events, 0.0 us)
Async XLA Ops:
  2.0 16.1 %collective-permute-start.8 = (bf16[2,96,896]{2,1,0:T(8,128)(2,1)S(1)}, bf16[2,96,896]{2,1,0:T(8,128)(2,1)S(1)}, u32[]{:S(2)}, u32[]{:S(2)}) collective-permute-start(bf16[2,96,896]{2,1,0:T(8,128)(2,1)S(1)} %get-tuple-element.40), channel_id=1, source_target_pairs={{0,1},{1,0},{2,3},{3,2},{4,7},{5,6},{6,5},{7,4},{8,9},{9,8},{10,11... | collective-permute-start | bytes 1032200 | tf_op jit(solution)/shard_map/ppermute | solution.py:424
  2.6 15.5 %collective-permute-start.7 = (bf16[2,96,768]{2,1,0:T(8,128)(2,1)S(1)}, bf16[2,96,768]{2,1,0:T(8,128)(2,1)S(1)}, u32[]{:S(2)}, u32[]{:S(2)}) collective-permute-start(bf16[2,96,768]{2,1,0:T(8,128)(2,1)S(1)} %get-tuple-element.39), channel_id=1, source_target_pairs={{0,4},{1,29},{2,6},{3,31},{4,0},{5,9},{6,2},{7,11},{8,12},{9,5},{1... | collective-permute-start | bytes 884744 | tf_op jit(solution)/shard_map/ppermute | solution.py:424
  6.0 12.0 %collective-permute-start.9 = (bf16[2,96,128]{2,1,0:T(8,128)(2,1)S(1)}, bf16[2,96,128]{2,1,0:T(8,128)(2,1)S(1)}, u32[]{:S(2)}, u32[]{:S(2)}) collective-permute-start(bf16[2,96,128]{2,1,0:T(8,128)(2,1)S(1)} %get-tuple-element.41), channel_id=1, source_target_pairs={{0,31},{1,6},{2,29},{3,4},{4,9},{5,0},{6,11},{7,2},{8,7},{9,14},{1... | collective-permute-start | bytes 147464 | tf_op jit(solution)/shard_map/ppermute | solution.py:424
  13.3 9.0 %collective-permute-start.2 = (bf16[2,96,128]{2,1,0:T(8,128)(2,1)S(1)}, bf16[2,96,128]{2,1,0:T(8,128)(2,1)S(1)}, u32[]{:S(2)}, u32[]{:S(2)}) collective-permute-start(bf16[2,96,128]{2,1,0:T(8,128)(2,1)S(1)} %get-tuple-element.32), channel_id=1, source_target_pairs={{0,5},{1,28},{2,7},{3,30},{4,3},{5,10},{6,1},{7,8},{8,13},{9,4},{1... | collective-permute-start | bytes 147464 | tf_op jit(solution)/shard_map/ppermute | solution.py:424
  13.4 10.1 %collective-permute-start = (bf16[2,96,768]{2,1,0:T(8,128)(2,1)S(1)}, bf16[2,96,768]{2,1,0:T(8,128)(2,1)S(1)}, u32[]{:S(2)}, u32[]{:S(2)}) collective-permute-start(bf16[2,96,768]{2,1,0:T(8,128)(2,1)S(1)} %get-tuple-element.30), channel_id=1, source_target_pairs={{0,28},{1,5},{2,30},{3,7},{4,8},{5,1},{6,10},{7,3},{8,4},{9,13},{1... | collective-permute-start | bytes 884744 | tf_op jit(solution)/shard_map/ppermute | solution.py:424
  18.0 10.1 %collective-permute-start.1 = (bf16[2,96,896]{2,1,0:T(8,128)(2,1)S(1)}, bf16[2,96,896]{2,1,0:T(8,128)(2,1)S(1)}, u32[]{:S(2)}, u32[]{:S(2)}) collective-permute-start(bf16[2,96,896]{2,1,0:T(8,128)(2,1)S(1)} %get-tuple-element.31), channel_id=1, source_target_pairs={{0,3},{1,2},{2,1},{3,0},{4,5},{5,4},{6,7},{7,6},{8,11},{9,10},{10,... | collective-permute-start | bytes 1032200 | tf_op jit(solution)/shard_map/ppermute | solution.py:424
  20.4 11.2 %collective-permute-start.10 = (bf16[2,96,896]{2,1,0:T(8,128)(2,1)S(1)}, bf16[2,96,896]{2,1,0:T(8,128)(2,1)S(1)}, u32[]{:S(2)}, u32[]{:S(2)}) collective-permute-start(bf16[2,96,896]{2,1,0:T(8,128)(2,1)S(1)} %get-tuple-element.42), channel_id=1, source_target_pairs={{0,28},{1,5},{2,30},{3,7},{4,8},{5,1},{6,10},{7,3},{8,4},{9,13},{1... | collective-permute-start | bytes 1032200 | tf_op jit(solution)/shard_map/ppermute | solution.py:424
  22.3 13.1 %collective-permute-start.11 = (bf16[2,96,896]{2,1,0:T(8,128)(2,1)S(1)}, bf16[2,96,896]{2,1,0:T(8,128)(2,1)S(1)}, u32[]{:S(2)}, u32[]{:S(2)}) collective-permute-start(bf16[2,96,896]{2,1,0:T(8,128)(2,1)S(1)} %get-tuple-element.43), channel_id=1, source_target_pairs={{0,3},{1,2},{2,1},{3,0},{4,5},{5,4},{6,7},{7,6},{8,11},{9,10},{10,... | collective-permute-start | bytes 1032200 | tf_op jit(solution)/shard_map/ppermute | solution.py:424
  30.4 13.6 %collective-permute-start.3 = (bf16[2,96,896]{2,1,0:T(8,128)(2,1)S(1)}, bf16[2,96,896]{2,1,0:T(8,128)(2,1)S(1)}, u32[]{:S(2)}, u32[]{:S(2)}) collective-permute-start(bf16[2,96,896]{2,1,0:T(8,128)(2,1)S(1)} %get-tuple-element.35), channel_id=1, source_target_pairs={{0,4},{1,29},{2,6},{3,31},{4,0},{5,9},{6,2},{7,11},{8,12},{9,5},{1... | collective-permute-start | bytes 1032200 | tf_op jit(solution)/shard_map/ppermute | solution.py:424
  30.5 13.5 %collective-permute-start.4 = (bf16[2,96,896]{2,1,0:T(8,128)(2,1)S(1)}, bf16[2,96,896]{2,1,0:T(8,128)(2,1)S(1)}, u32[]{:S(2)}, u32[]{:S(2)}) collective-permute-start(bf16[2,96,896]{2,1,0:T(8,128)(2,1)S(1)} %get-tuple-element.36), channel_id=1, source_target_pairs={{0,1},{1,0},{2,3},{3,2},{4,7},{5,6},{6,5},{7,4},{8,9},{9,8},{10,11... | collective-permute-start | bytes 1032200 | tf_op jit(solution)/shard_map/ppermute | solution.py:424
  37.7 8.6 %collective-permute-start.12 = (bf16[2,96,896]{2,1,0:T(8,128)(2,1)S(1)}, bf16[2,96,896]{2,1,0:T(8,128)(2,1)S(1)}, u32[]{:S(2)}, u32[]{:S(2)}) collective-permute-start(bf16[2,96,896]{2,1,0:T(8,128)(2,1)S(1)} %get-tuple-element.44.refs_0_), channel_id=1, source_target_pairs={{0,4},{1,29},{2,6},{3,31},{4,0},{5,9},{6,2},{7,11},{8,12},{9,5},{1... | collective-permute-start | bytes 1032200 | tf_op jit(solution)/shard_map/ppermute | solution.py:424
  37.8 8.6 %collective-permute-start.13 = (bf16[2,96,896]{2,1,0:T(8,128)(2,1)S(1)}, bf16[2,96,896]{2,1,0:T(8,128)(2,1)S(1)}, u32[]{:S(2)}, u32[]{:S(2)}) collective-permute-start(bf16[2,96,896]{2,1,0:T(8,128)(2,1)S(1)} %get-tuple-element.45.refs_1_), channel_id=1, source_target_pairs={{0,1},{1,0},{2,3},{3,2},{4,7},{5,6},{6,5},{7,4},{8,9},{9,8},{10,11... | collective-permute-start | bytes 1032200 | tf_op jit(solution)/shard_map/ppermute | solution.py:424
  46.2 10.0 %collective-permute-start.5 = (bf16[2,96,896]{2,1,0:T(8,128)(2,1)S(1)}, bf16[2,96,896]{2,1,0:T(8,128)(2,1)S(1)}, u32[]{:S(2)}, u32[]{:S(2)}) collective-permute-start(bf16[2,96,896]{2,1,0:T(8,128)(2,1)S(1)} %get-tuple-element.37.refs_2_), channel_id=1, source_target_pairs={{0,28},{1,5},{2,30},{3,7},{4,8},{5,1},{6,10},{7,3},{8,4},{9,13},{1... | collective-permute-start | bytes 1032200 | tf_op jit(solution)/shard_map/ppermute | solution.py:424
  46.3 10.0 %collective-permute-start.6 = (bf16[2,96,896]{2,1,0:T(8,128)(2,1)S(1)}, bf16[2,96,896]{2,1,0:T(8,128)(2,1)S(1)}, u32[]{:S(2)}, u32[]{:S(2)}) collective-permute-start(bf16[2,96,896]{2,1,0:T(8,128)(2,1)S(1)} %get-tuple-element.38.refs_3_), channel_id=1, source_target_pairs={{0,3},{1,2},{2,1},{3,0},{4,5},{5,4},{6,7},{7,6},{8,11},{9,10},{10,... | collective-permute-start | bytes 1032200 | tf_op jit(solution)/shard_map/ppermute | solution.py:424

commit v5 on v4

--- a/solution.py
+++ b/solution.py
@@ -11,6 +11,8 @@
 SMEM = pl.BlockSpec(memory_space=pltpu.SMEM)
 HBM = pl.BlockSpec(memory_space=pltpu.HBM)
 VMEM_LIMIT = 40 * 1024 * 1024
+FIRST = 10**10
+MIDDLE = 8 * 10**8
 
 
 def direction_at(row, col, tick, stream):
@@ -56,7 +58,8 @@
             mine = chosen_at_start(roster, own, counts)
             pairs = (
                 (edges[going].at[0, other], by_row),
-                (corners[own].at[mine], by_diagonal),
+                (corners[own].at[mine], by_diagonal.at[0]),
+                (corners[own].at[1 - mine], by_diagonal.at[1]),
                 (edges[going].at[1, other], by_col.at[:, :, pl.ds(0, edge_width)]),
                 (corners[going].at[other], by_col.at[:, :, pl.ds(edge_width, corner_width)]),
             )
@@ -69,8 +72,6 @@
     numbers, all_edges, all_corners, sems
 ):
     edges, corners = (se_edges, nw_edges), (se_corners, nw_corners)
-    edge_width = by_row.shape[-1]
-    corner_width = by_diagonal.shape[-1]
     roster_copy = pltpu.make_async_copy(roster, numbers, sems.at[0])
     roster_copy.start()
     own = 1 - own_direction(-1, stream)
@@ -81,8 +82,7 @@
             @pl.when(own_direction(-1, stream) == going)
             def _():
                 act(pltpu.make_async_copy(edges[going], all_edges, sems.at[1]))
-
-            act(pltpu.make_async_copy(corners[going], all_corners.at[going], sems.at[2 + going]))
+                act(pltpu.make_async_copy(corners[1 - going], all_corners, sems.at[2]))
 
     fetch(start)
     roster_copy.wait()
@@ -91,18 +91,18 @@
     mine = jnp.where(own == 0, chosen[0], chosen[1])
     fetch(wait)
     by_row[...] = all_edges[0, other]
-    by_col[:, :, pl.ds(0, edge_width)] = all_edges[1, other]
-    by_col[:, :, pl.ds(edge_width, corner_width)] = all_corners[1 - own, other]
-    by_diagonal[...] = all_corners[own, mine]
-
-
-def slot_shapes(edges, corners):
+    by_col[...] = all_edges[1, other]
+    by_diagonal[...] = all_corners[mine]
+
+
+def slot_shapes(edges, corners, late):
     _, _, parts, shots, edge_width = edges.shape
     corner_width = corners.shape[-1]
+    kind = edges.dtype
     return [
-        pltpu.VMEM((parts, shots, edge_width), edges.dtype),
-        pltpu.VMEM((parts, shots, edge_width + corner_width), edges.dtype),
-        pltpu.VMEM((parts, shots, corner_width), edges.dtype),
+        pltpu.VMEM((parts, shots, edge_width), kind),
+        pltpu.VMEM((parts, shots, edge_width + (corner_width if late else 0)), kind),
+        pltpu.VMEM(((2,) if late else ()) + (parts, shots, corner_width), kind),
     ]
 
 
@@ -110,14 +110,14 @@
     edges, _, corners, _ = states
     return pl.pallas_call(
         functools.partial(select_kernel, counts, stream),
-        out_shape=slot_shapes(edges, corners),
+        out_shape=slot_shapes(edges, corners, False),
         in_specs=[HBM] * 5,
         out_specs=[VMEM] * 3,
         scratch_shapes=[
             pltpu.SMEM(roster.shape, roster.dtype),
             pltpu.VMEM(edges.shape, edges.dtype),
-            pltpu.VMEM((2,) + corners.shape, corners.dtype),
-            pltpu.SemaphoreType.DMA((4,)),
+            pltpu.VMEM(corners.shape, corners.dtype),
+            pltpu.SemaphoreType.DMA((3,)),
         ],
         compiler_params=pltpu.CompilerParams(vmem_limit_bytes=VMEM_LIMIT),
         name="select_initial",
@@ -172,7 +172,7 @@
     operators = operators.reshape(count, edge_width, edge_width)
     return pl.pallas_call(
         functools.partial(load_kernel, counts, stream),
-        out_shape=slot_shapes(states[0], states[2])
+        out_shape=slot_shapes(states[0], states[2], True)
         + [
             pltpu.VMEM((2, count * edge_width, edge_width), kind),
             pltpu.VMEM((2,) + sources.shape, kind),
@@ -181,12 +181,12 @@
         in_specs=[SMEM] + [HBM] * 6,
         out_specs=[VMEM] * 6,
         scratch_shapes=[
-            pltpu.SemaphoreType.DMA((4,)),
+            pltpu.SemaphoreType.DMA((5,)),
             pltpu.SemaphoreType.DMA((count,)),
             pltpu.SemaphoreType.DMA((2, 2)),
         ],
         compiler_params=pltpu.CompilerParams(vmem_limit_bytes=VMEM_LIMIT),
-        cost_estimate=cost(False),
+        cost_estimate=cost(0),
         name="load_operators",
     )(roster, *map(in_hbm, states), in_hbm(operators), in_hbm(sources))
 
@@ -214,7 +214,10 @@
             left[pl.ds(row, shots), pl.ds(column + edge_width, edge_width)] = minus
             left[pl.ds(row + shots, shots), pl.ds(column + edge_width, edge_width)] = real
 
-    corner = corner_in[...] if tick == 0 else first_in[:, :, corner_part]
+    if corner_in is None:
+        corner = first_in[:, :, corner_part]
+    else:
+        corner = corner_in[...] if len(corner_in.shape) == 3 else corner_in[tick]
     corner = corner.astype(jnp.float32).reshape(rows, corner_width)
     if first_out.shape[-1] > edge_width:
         first_out[:, :, corner_part] = second_in[:, :, corner_part]
@@ -249,9 +252,11 @@
 
 
 def middle_kernel(
-    tick, stream, corner_width, first_in, second_in, corner_in, sources, operators, *refs
-):
-    outs, left = refs[:-1], refs[-1]
+    tick, stream, corner_width, first_in, second_in, sources, operators, *refs
+):
+    *corner_in, first_out, second_out, left = refs
+    outs = (first_out, second_out)
+    corner_in = corner_in[0] if corner_in else None
     compute(
         tick, stream, corner_width, first_in, second_in, corner_in, sources, operators, outs, left,
         lambda step, at: None,
@@ -343,18 +348,18 @@
     corner_store(wait)
 
 
-def tick_shapes(sources, corner_width, tick, ticks):
+def tick_shapes(sources, corner_width, tick, ticks, stream):
     _, _, parts, shots, edge_width = sources.shape
     kind = sources.dtype
-    first_width = edge_width + (0 if tick == ticks - 1 else corner_width)
+    first_width = edge_width + (0 if tick == ticks - 1 or tick + stream == 0 else corner_width)
     return [
         pltpu.VMEM((parts, shots, first_width), kind),
         pltpu.VMEM((parts, shots, edge_width + corner_width), kind),
     ]
 
 
-def cost(heavy):
-    return pl.CostEstimate(flops=10**10 if heavy else 0, bytes_accessed=1, transcendentals=0)
+def cost(flops):
+    return pl.CostEstimate(flops=flops, bytes_accessed=1, transcendentals=0)
 
 
 def left_side(sources):
@@ -362,18 +367,23 @@
     return pltpu.VMEM((2 * parts * shots, 4 * edge_width), sources.dtype)
 
 
-def middle_tick(tick, ticks, stream, first_in, second_in, corner_in, sources, operators):
-    shapes = tick_shapes(sources, corner_in.shape[-1], tick, ticks)
+def middle_tick(
+    tick, ticks, stream, first_in, second_in, sources, operators, corner_width, corner_in
+):
+    shapes = tick_shapes(sources, corner_width, tick, ticks, stream)
+    operands = [first_in, second_in, sources, operators]
+    if corner_in is not None:
+        operands.append(corner_in)
     return pl.pallas_call(
-        functools.partial(middle_kernel, tick, stream, corner_in.shape[-1]),
+        functools.partial(middle_kernel, tick, stream, corner_width),
         out_shape=shapes,
-        in_specs=[VMEM] * 5,
+        in_specs=[VMEM] * len(operands),
         out_specs=[VMEM] * len(shapes),
         scratch_shapes=[left_side(sources)],
         compiler_params=pltpu.CompilerParams(vmem_limit_bytes=VMEM_LIMIT),
-        cost_estimate=cost(tick == 0 and stream == 0),
+        cost_estimate=cost(0 if stream else FIRST if tick == 0 else MIDDLE),
         name="tick" + str(tick) + "_stream" + str(stream),
-    )(first_in, second_in, corner_in, sources, operators)
+    )(*operands)
 
 
 def last_tick(
@@ -403,11 +413,11 @@
         in_specs=in_specs,
         out_specs=[HBM] * 4,
         scratch_shapes=[left_side(sources)]
-        + tick_shapes(sources, corner_width, tick, ticks)
+        + tick_shapes(sources, corner_width, tick, ticks, stream)
         + [pltpu.SemaphoreType.DMA((2, 3)), pltpu.SemaphoreType.DMA((3, 3))],
         input_output_aliases=aliases,
         compiler_params=pltpu.CompilerParams(vmem_limit_bytes=VMEM_LIMIT),
-        cost_estimate=cost(False),
+        cost_estimate=cost(0),
         name="tick" + str(tick) + "_stream" + str(stream),
     )(*operands)
 
@@ -469,9 +479,13 @@
                 corners[stream] = by_diagonal(slots[stream][2], counts, stream)
             first_in = by_row(firsts[stream], counts, tick, stream)
             if tick < ticks - 1:
+                corner_in = corners[stream] if tick == 0 else None
+                if tick == 1 and stream == 0:
+                    corner_in = corners[1]
                 done.append(
                     middle_tick(
-                        tick, ticks, stream, first_in, second_in, corners[stream], picked, prepared
+                        tick, ticks, stream, first_in, second_in, picked, prepared, corner_width,
+                        corner_in,
                     )
                 )
             else:

time: 59.6 us -> 59 us (0.990)
  the two profiles are of different devices: /device:TPU:0 before, /device:TPU:1 now
where the time goes in v5:
time: 59 us; the launch traced here: 58.8 us
  starting transfers between devices  25.5 us (43%)
  Pallas kernels  20.7 us (35%)
  waiting for transfers between devices  11.9 us (20%)
  between operations  0.7 us (1%)
    ppermute x14, starting transfers between devices, move(): return lax.ppermute(array, ('row', 'col'), pairs)  25.5 us
    ppermute x14, waiting for transfers between devices, move(): return lax.ppermute(array, ('row', 'col'), pairs)  11.9 us
    pallas_call x4, Pallas kernels, middle_tick(): pl.pallas_call(functools.partial(middle_kernel, tick, stream, corner_widt...  9.11 us
    pallas_call x2, Pallas kernels, last_tick(): pl.pallas_call(functools.partial(last_kernel, tick, stream, histories, co...  6.19 us
    pallas_call x1, Pallas kernels, load_operators(): pl.pallas_call(functools.partial(load_kernel, counts, stream), out_shape=...  4.06 us
    pallas_call x1, Pallas kernels, select_initial(): pl.pallas_call(functools.partial(select_kernel, counts, stream), out_shap...  1.36 us
  transfers between devices with their start and end apart: 14, of which 6 were waited for; matrix products, arithmetic and copies ran while one was open for 0% of the time, Pallas kernels for 28%

profile of v5, /device:TPU:1, one launch (start us, length us, event | category | flops | bytes accessed | tf_op | source)
XLA Modules:
  0.0 58.8 jit_solution(16293020113718783036)
XLA Ops:
  0.6 1.4 %select_initial.1 = (bf16[2,96,768]{2,1,0:T(8,128)(2,1)S(1)}, bf16[2,96,768]{2,1,0:T(8,128)(2,1)S(1)}, bf16[2,96,128]{2,1,0:T(8,128)(2,1)S(1)}) custom-call(s32[2,2,3]{2,1,0:T(2,128)} %bitcast.25, bf16[2,2,2,96,768]{4,3,2,1,0:T(8,128)(2,1)} %bitcast.12, bf16[2,2,2,96,768]{4,3,2,1,0:T(8,128)(2,1)} %bitcast.14, bf16[2,2,96,128]{3,2,1,0:T(8,128)(2,1)} %bitcast.19, ...), custom_call_target="tpu_custom_call" | custom-call | tf_op jit(solution)/shard_map/select_initial/pallas_call | solution.py:111
  2.0 5.1 %collective-permute-start.7 = (bf16[2,96,768]{2,1,0:T(8,128)(2,1)S(1)}, bf16[2,96,768]{2,1,0:T(8,128)(2,1)S(1)}, u32[]{:S(2)}, u32[]{:S(2)}) collective-permute-start(bf16[2,96,768]{2,1,0:T(8,128)(2,1)S(1)} %get-tuple-element.39), channel_id=1, source_target_pairs={{0,4},{1,29},{2,6},{3,31},{4,0},{5,9},{6,2},{7,11},{8,12},{9,5},{1... | collective-permute-start | bytes 884744 | tf_op jit(solution)/shard_map/ppermute | solution.py:434
  7.1 0.0 collective-permute-start.8
  7.1 0.0 collective-permute-start.9
  7.1 4.1 %load_operators.1 = (bf16[2,96,768]{2,1,0:T(8,128)(2,1)S(1)}, bf16[2,96,896]{2,1,0:T(8,128)(2,1)S(1)}, bf16[2,2,96,128]{3,2,1,0:T(8,128)(2,1)S(1)}, bf16[2,3072,...) custom-call(s32[2,2,3]{2,1,0:T(2,128)} %bitcast.26, ...), custom_call_target="tpu_custom_call" | custom-call | bytes 1 | tf_op jit(solution)/shard_map/load_operators/pallas_call | solution.py:173
  11.2 4.5 %collective-permute-start.2 = (bf16[2,2,96,128]{3,2,1,0:T(8,128)(2,1)S(1)}, bf16[2,2,96,128]{3,2,1,0:T(8,128)(2,1)S(1)}, u32[]{:S(2)}, u32[]{:S(2)}) collective-permute-start(bf16[2,2,96,128]{3,2,1,0:T(8,128)(2,1)S(1)} %get-tuple-element.34), channel_id=1, source_target_pairs={{0,5},{1,28},{2,7},{3,30},{4,3},{5,10},{6,1},{7,8},{8,13},{9,4},{1... | collective-permute-start | bytes 294920 | tf_op jit(solution)/shard_map/ppermute | solution.py:434
  15.7 0.0 collective-permute-start
  15.7 0.0 collective-permute-done.9.refs_0_
  15.7 1.6 %collective-permute-start.1 = (bf16[2,96,896]{2,1,0:T(8,128)(2,1)S(1)}, bf16[2,96,896]{2,1,0:T(8,128)(2,1)S(1)}, u32[]{:S(2)}, u32[]{:S(2)}) collective-permute-start(bf16[2,96,896]{2,1,0:T(8,128)(2,1)S(1)} %get-tuple-element.31), channel_id=1, source_target_pairs={{0,3},{1,2},{2,1},{3,0},{4,5},{5,4},{6,7},{7,6},{8,11},{9,10},{10,... | collective-permute-start | bytes 1032200 | tf_op jit(solution)/shard_map/ppermute | solution.py:434
  17.3 2.3 %tick0_stream0.1 = (bf16[2,96,768]{2,1,0:T(8,128)(2,1)S(1)}, bf16[2,96,896]{2,1,0:T(8,128)(2,1)S(1)}) custom-call(bf16[2,96,768]{2,1,0:T(8,128)(2,1)S(1)} %collective-permute-done.7.first_in, bf16[2,96,768]{2,1,0:T(8,128)(2,1)S(1)} %collective-permute-done.8.second_in, bf16[2,2,2,96,768]{4,3,2,1,0:T(8,128)(2,1)S(1)} %get-tuple-element.32.sources, ...), custom_call_target="tpu_custom_call" | custom-call | flops 10000000000 | bytes 1 | tf_op jit(solution)/shard_map/tick0_stream0/pallas_call | solution.py:377
  19.6 0.2 collective-permute-start.11
  19.8 0.2 collective-permute-start.10
  20.1 0.0 collective-permute-done.2.refs_0_
  20.1 5.7 %collective-permute-done.first_in = bf16[2,96,768]{2,1,0:T(8,128)(2,1)S(1)} collective-permute-done((bf16[2,96,768]{2,1,0:T(8,128)(2,1)S(1)}, bf16[2,96,768]{2,1,0:T(8,128)(2,1)S(1)}, u32[]{:S(2)}, u32[]{:S(2)}) %collective-permute-start) | collective-permute-done | bytes 294944 | tf_op jit(solution)/shard_map/ppermute | solution.py:434
  25.8 1.6 %collective-permute-done.1.second_in = bf16[2,96,896]{2,1,0:T(8,128)(2,1)S(1)} collective-permute-done((bf16[2,96,896]{2,1,0:T(8,128)(2,1)S(1)}, bf16[2,96,896]{2,1,0:T(8,128)(2,1)S(1)}, u32[]{:S(2)}, u32[]{:S(2)}) %collective-permute-start.1) | collective-permute-done | bytes 344096 | tf_op jit(solution)/shard_map/ppermute | solution.py:434
  27.4 2.3 %tick0_stream1.1 = (bf16[2,96,896]{2,1,0:T(8,128)(2,1)S(1)}, bf16[2,96,896]{2,1,0:T(8,128)(2,1)S(1)}) custom-call(bf16[2,96,768]{2,1,0:T(8,128)(2,1)S(1)} %collective-permute-done.first_in, bf16[2,96,896]{2,1,0:T(8,128)(2,1)S(1)} %collective-permute-done.1.second_in, bf16[2,2,2,96,768]{4,3,2,1,0:T(8,128)(2,1)S(1)} %get-tuple-element.32.sources, ...), custom_call_target="tpu_custom_call" | custom-call | bytes 1 | tf_op jit(solution)/shard_map/tick0_stream1/pallas_call | solution.py:377
  29.7 4.0 %collective-permute-start.3 = (bf16[2,96,896]{2,1,0:T(8,128)(2,1)S(1)}, bf16[2,96,896]{2,1,0:T(8,128)(2,1)S(1)}, u32[]{:S(2)}, u32[]{:S(2)}) collective-permute-start(bf16[2,96,896]{2,1,0:T(8,128)(2,1)S(1)} %get-tuple-element.35), channel_id=1, source_target_pairs={{0,4},{1,29},{2,6},{3,31},{4,0},{5,9},{6,2},{7,11},{8,12},{9,5},{1... | collective-permute-start | bytes 1032200 | tf_op jit(solution)/shard_map/ppermute | solution.py:434
  33.7 0.0 collective-permute-start.4
  33.7 0.0 collective-permute-done.10.first_in
  33.7 0.9 %collective-permute-done.11.second_in = bf16[2,96,896]{2,1,0:T(8,128)(2,1)S(1)} collective-permute-done((bf16[2,96,896]{2,1,0:T(8,128)(2,1)S(1)}, bf16[2,96,896]{2,1,0:T(8,128)(2,1)S(1)}, u32[]{:S(2)}, u32[]{:S(2)}) %collective-permute-start.11) | collective-permute-done | bytes 344096 | tf_op jit(solution)/shard_map/ppermute | solution.py:434
  34.6 2.3 %tick1_stream0.1 = (bf16[2,96,896]{2,1,0:T(8,128)(2,1)S(1)}, bf16[2,96,896]{2,1,0:T(8,128)(2,1)S(1)}) custom-call(bf16[2,96,768]{2,1,0:T(8,128)(2,1)S(1)} %collective-permute-done.10.first_in, bf16[2,96,896]{2,1,0:T(8,128)(2,1)S(1)} %collective-permute-done.11.second_in, bf16[2,2,2,96,768]{4,3,2,1,0:T(8,128)(2,1)S(1)} %get-tuple-element.32.sources, ...), custom_call_target="tpu_custom_call" | custom-call | flops 800000000 | bytes 1 | tf_op jit(solution)/shard_map/tick1_stream0/pallas_call | solution.py:377
  36.9 1.7 %collective-permute-start.12 = (bf16[2,96,896]{2,1,0:T(8,128)(2,1)S(1)}, bf16[2,96,896]{2,1,0:T(8,128)(2,1)S(1)}, u32[]{:S(2)}, u32[]{:S(2)}) collective-permute-start(bf16[2,96,896]{2,1,0:T(8,128)(2,1)S(1)} %get-tuple-element.44.refs_0_), channel_id=1, source_target_pairs={{0,4},{1,29},{2,6},{3,31},{4,0},{5,9},{6,2},{7,11},{8,12},{9,5},{1... | collective-permute-start | bytes 1032200 | tf_op jit(solution)/shard_map/ppermute | solution.py:434
  38.6 0.0 collective-permute-start.13
  38.6 0.1 collective-permute-done.3.first_in
  38.7 0.0 collective-permute-done.4.second_in
  38.7 2.3 %tick1_stream1.1 = (bf16[2,96,896]{2,1,0:T(8,128)(2,1)S(1)}, bf16[2,96,896]{2,1,0:T(8,128)(2,1)S(1)}) custom-call(bf16[2,96,896]{2,1,0:T(8,128)(2,1)S(1)} %collective-permute-done.3.first_in, bf16[2,96,896]{2,1,0:T(8,128)(2,1)S(1)} %collective-permute-done.4.second_in, bf16[2,2,2,96,768]{4,3,2,1,0:T(8,128)(2,1)S(1)} %get-tuple-element.32.sources, ...), custom_call_target="tpu_custom_call" | custom-call | bytes 1 | tf_op jit(solution)/shard_map/tick1_stream1/pallas_call | solution.py:377
  41.0 2.8 %collective-permute-start.5 = (bf16[2,96,896]{2,1,0:T(8,128)(2,1)S(1)}, bf16[2,96,896]{2,1,0:T(8,128)(2,1)S(1)}, u32[]{:S(2)}, u32[]{:S(2)}) collective-permute-start(bf16[2,96,896]{2,1,0:T(8,128)(2,1)S(1)} %get-tuple-element.37.refs_2_), channel_id=1, source_target_pairs={{0,28},{1,5},{2,30},{3,7},{4,8},{5,1},{6,10},{7,3},{8,4},{9,13},{1... | collective-permute-start | bytes 1032200 | tf_op jit(solution)/shard_map/ppermute | solution.py:434
  43.8 5.2 %collective-permute-start.6 = (bf16[2,96,896]{2,1,0:T(8,128)(2,1)S(1)}, bf16[2,96,896]{2,1,0:T(8,128)(2,1)S(1)}, u32[]{:S(2)}, u32[]{:S(2)}) collective-permute-start(bf16[2,96,896]{2,1,0:T(8,128)(2,1)S(1)} %get-tuple-element.38.refs_3_), channel_id=1, source_target_pairs={{0,3},{1,2},{2,1},{3,0},{4,5},{5,4},{6,7},{7,6},{8,11},{9,10},{10,... | collective-permute-start | bytes 1032200 | tf_op jit(solution)/shard_map/ppermute | solution.py:434
  49.0 3.1 %tick2_stream0.1 = (bf16[2,2,2,96,768]{4,3,2,1,0:T(8,128)(2,1)}, bf16[2,2,2,96,768]{4,3,2,1,0:T(8,128)(2,1)}, bf16[2,2,96,128]{3,2,1,0:T(8,128)(2,1)}, bf16[2,2,96,128]{3,2,1,0:T(8,128)(2,1)}) custom-call(f32[2,8,128]{2,1,0:T(8,128)S(1)} %get-tuple-element.29.flags, bf16[2,96,896]{2,1,0:T(8,128)(2,1)S(1)} %collective-permute-done.12.first_in, ...), custom_call_target="tpu_custom_call" | custom-call | bytes 1 | tf_op jit(solution)/shard_map/tick2_stream0/pallas_call | solution.py:410
  52.1 2.6 %collective-permute-done.5.first_in = bf16[2,96,896]{2,1,0:T(8,128)(2,1)S(1)} collective-permute-done((bf16[2,96,896]{2,1,0:T(8,128)(2,1)S(1)}, bf16[2,96,896]{2,1,0:T(8,128)(2,1)S(1)}, u32[]{:S(2)}, u32[]{:S(2)}) %collective-permute-start.5) | collective-permute-done | bytes 344096 | tf_op jit(solution)/shard_map/ppermute | solution.py:434
  54.7 1.0 %collective-permute-done.6.second_in = bf16[2,96,896]{2,1,0:T(8,128)(2,1)S(1)} collective-permute-done((bf16[2,96,896]{2,1,0:T(8,128)(2,1)S(1)}, bf16[2,96,896]{2,1,0:T(8,128)(2,1)S(1)}, u32[]{:S(2)}, u32[]{:S(2)}) %collective-permute-start.6) | collective-permute-done | bytes 344096 | tf_op jit(solution)/shard_map/ppermute | solution.py:434
  55.7 3.1 %tick2_stream1.1 = (bf16[2,2,2,96,768]{4,3,2,1,0:T(8,128)(2,1)}, bf16[2,2,2,96,768]{4,3,2,1,0:T(8,128)(2,1)}, bf16[2,2,96,128]{3,2,1,0:T(8,128)(2,1)}, bf16[2,2,96,128]{3,2,1,0:T(8,128)(2,1)}) custom-call(f32[2,8,128]{2,1,0:T(8,128)S(1)} %get-tuple-element.29.flags, ...), custom_call_target="tpu_custom_call", output_to_operand_aliasing={{0}: (5, {}), {1}: (6, {}), {2}: (7, {}), {3}: (8, {})} | custom-call | bytes 1 | tf_op jit(solution)/shard_map/tick2_stream1/pallas_call | solution.py:410
  (4 shorter events, 0.0 us)
Async XLA Ops:
  2.0 15.3 %collective-permute-start.7 = (bf16[2,96,768]{2,1,0:T(8,128)(2,1)S(1)}, bf16[2,96,768]{2,1,0:T(8,128)(2,1)S(1)}, u32[]{:S(2)}, u32[]{:S(2)}) collective-permute-start(bf16[2,96,768]{2,1,0:T(8,128)(2,1)S(1)} %get-tuple-element.39), channel_id=1, source_target_pairs={{0,4},{1,29},{2,6},{3,31},{4,0},{5,9},{6,2},{7,11},{8,12},{9,5},{1... | collective-permute-start | bytes 884744 | tf_op jit(solution)/shard_map/ppermute | solution.py:434
  7.1 10.2 %collective-permute-start.8 = (bf16[2,96,768]{2,1,0:T(8,128)(2,1)S(1)}, bf16[2,96,768]{2,1,0:T(8,128)(2,1)S(1)}, u32[]{:S(2)}, u32[]{:S(2)}) collective-permute-start(bf16[2,96,768]{2,1,0:T(8,128)(2,1)S(1)} %get-tuple-element.40), channel_id=1, source_target_pairs={{0,1},{1,0},{2,3},{3,2},{4,7},{5,6},{6,5},{7,4},{8,9},{9,8},{10,11... | collective-permute-start | bytes 884744 | tf_op jit(solution)/shard_map/ppermute | solution.py:434
  7.1 8.6 %collective-permute-start.9 = (bf16[2,96,128]{2,1,0:T(8,128)(2,1)S(1)}, bf16[2,96,128]{2,1,0:T(8,128)(2,1)S(1)}, u32[]{:S(2)}, u32[]{:S(2)}) collective-permute-start(bf16[2,96,128]{2,1,0:T(8,128)(2,1)S(1)} %get-tuple-element.41), channel_id=1, source_target_pairs={{0,31},{1,6},{2,29},{3,4},{4,9},{5,0},{6,11},{7,2},{8,7},{9,14},{1... | collective-permute-start | bytes 147464 | tf_op jit(solution)/shard_map/ppermute | solution.py:434
  11.2 8.8 %collective-permute-start.2 = (bf16[2,2,96,128]{3,2,1,0:T(8,128)(2,1)S(1)}, bf16[2,2,96,128]{3,2,1,0:T(8,128)(2,1)S(1)}, u32[]{:S(2)}, u32[]{:S(2)}) collective-permute-start(bf16[2,2,96,128]{3,2,1,0:T(8,128)(2,1)S(1)} %get-tuple-element.34), channel_id=1, source_target_pairs={{0,5},{1,28},{2,7},{3,30},{4,3},{5,10},{6,1},{7,8},{8,13},{9,4},{1... | collective-permute-start | bytes 294920 | tf_op jit(solution)/shard_map/ppermute | solution.py:434
  15.7 10.1 %collective-permute-start = (bf16[2,96,768]{2,1,0:T(8,128)(2,1)S(1)}, bf16[2,96,768]{2,1,0:T(8,128)(2,1)S(1)}, u32[]{:S(2)}, u32[]{:S(2)}) collective-permute-start(bf16[2,96,768]{2,1,0:T(8,128)(2,1)S(1)} %get-tuple-element.30), channel_id=1, source_target_pairs={{0,28},{1,5},{2,30},{3,7},{4,8},{5,1},{6,10},{7,3},{8,4},{9,13},{1... | collective-permute-start | bytes 884744 | tf_op jit(solution)/shard_map/ppermute | solution.py:434
  15.7 11.7 %collective-permute-start.1 = (bf16[2,96,896]{2,1,0:T(8,128)(2,1)S(1)}, bf16[2,96,896]{2,1,0:T(8,128)(2,1)S(1)}, u32[]{:S(2)}, u32[]{:S(2)}) collective-permute-start(bf16[2,96,896]{2,1,0:T(8,128)(2,1)S(1)} %get-tuple-element.31), channel_id=1, source_target_pairs={{0,3},{1,2},{2,1},{3,0},{4,5},{5,4},{6,7},{7,6},{8,11},{9,10},{10,... | collective-permute-start | bytes 1032200 | tf_op jit(solution)/shard_map/ppermute | solution.py:434
  19.6 15.0 %collective-permute-start.11 = (bf16[2,96,896]{2,1,0:T(8,128)(2,1)S(1)}, bf16[2,96,896]{2,1,0:T(8,128)(2,1)S(1)}, u32[]{:S(2)}, u32[]{:S(2)}) collective-permute-start(bf16[2,96,896]{2,1,0:T(8,128)(2,1)S(1)} %get-tuple-element.43), channel_id=1, source_target_pairs={{0,3},{1,2},{2,1},{3,0},{4,5},{5,4},{6,7},{7,6},{8,11},{9,10},{10,... | collective-permute-start | bytes 1032200 | tf_op jit(solution)/shard_map/ppermute | solution.py:434
  19.8 13.9 %collective-permute-start.10 = (bf16[2,96,768]{2,1,0:T(8,128)(2,1)S(1)}, bf16[2,96,768]{2,1,0:T(8,128)(2,1)S(1)}, u32[]{:S(2)}, u32[]{:S(2)}) collective-permute-start(bf16[2,96,768]{2,1,0:T(8,128)(2,1)S(1)} %get-tuple-element.42), channel_id=1, source_target_pairs={{0,28},{1,5},{2,30},{3,7},{4,8},{5,1},{6,10},{7,3},{8,4},{9,13},{1... | collective-permute-start | bytes 884744 | tf_op jit(solution)/shard_map/ppermute | solution.py:434
  29.7 9.0 %collective-permute-start.3 = (bf16[2,96,896]{2,1,0:T(8,128)(2,1)S(1)}, bf16[2,96,896]{2,1,0:T(8,128)(2,1)S(1)}, u32[]{:S(2)}, u32[]{:S(2)}) collective-permute-start(bf16[2,96,896]{2,1,0:T(8,128)(2,1)S(1)} %get-tuple-element.35), channel_id=1, source_target_pairs={{0,4},{1,29},{2,6},{3,31},{4,0},{5,9},{6,2},{7,11},{8,12},{9,5},{1... | collective-permute-start | bytes 1032200 | tf_op jit(solution)/shard_map/ppermute | solution.py:434
  33.7 5.0 %collective-permute-start.4 = (bf16[2,96,896]{2,1,0:T(8,128)(2,1)S(1)}, bf16[2,96,896]{2,1,0:T(8,128)(2,1)S(1)}, u32[]{:S(2)}, u32[]{:S(2)}) collective-permute-start(bf16[2,96,896]{2,1,0:T(8,128)(2,1)S(1)} %get-tuple-element.36), channel_id=1, source_target_pairs={{0,1},{1,0},{2,3},{3,2},{4,7},{5,6},{6,5},{7,4},{8,9},{9,8},{10,11... | collective-permute-start | bytes 1032200 | tf_op jit(solution)/shard_map/ppermute | solution.py:434
  36.9 12.2 %collective-permute-start.12 = (bf16[2,96,896]{2,1,0:T(8,128)(2,1)S(1)}, bf16[2,96,896]{2,1,0:T(8,128)(2,1)S(1)}, u32[]{:S(2)}, u32[]{:S(2)}) collective-permute-start(bf16[2,96,896]{2,1,0:T(8,128)(2,1)S(1)} %get-tuple-element.44.refs_0_), channel_id=1, source_target_pairs={{0,4},{1,29},{2,6},{3,31},{4,0},{5,9},{6,2},{7,11},{8,12},{9,5},{1... | collective-permute-start | bytes 1032200 | tf_op jit(solution)/shard_map/ppermute | solution.py:434
  38.6 10.4 %collective-permute-start.13 = (bf16[2,96,896]{2,1,0:T(8,128)(2,1)S(1)}, bf16[2,96,896]{2,1,0:T(8,128)(2,1)S(1)}, u32[]{:S(2)}, u32[]{:S(2)}) collective-permute-start(bf16[2,96,896]{2,1,0:T(8,128)(2,1)S(1)} %get-tuple-element.45.refs_1_), channel_id=1, source_target_pairs={{0,1},{1,0},{2,3},{3,2},{4,7},{5,6},{6,5},{7,4},{8,9},{9,8},{10,11... | collective-permute-start | bytes 1032200 | tf_op jit(solution)/shard_map/ppermute | solution.py:434
  41.0 13.8 %collective-permute-start.5 = (bf16[2,96,896]{2,1,0:T(8,128)(2,1)S(1)}, bf16[2,96,896]{2,1,0:T(8,128)(2,1)S(1)}, u32[]{:S(2)}, u32[]{:S(2)}) collective-permute-start(bf16[2,96,896]{2,1,0:T(8,128)(2,1)S(1)} %get-tuple-element.37.refs_2_), channel_id=1, source_target_pairs={{0,28},{1,5},{2,30},{3,7},{4,8},{5,1},{6,10},{7,3},{8,4},{9,13},{1... | collective-permute-start | bytes 1032200 | tf_op jit(solution)/shard_map/ppermute | solution.py:434
  43.8 11.9 %collective-permute-start.6 = (bf16[2,96,896]{2,1,0:T(8,128)(2,1)S(1)}, bf16[2,96,896]{2,1,0:T(8,128)(2,1)S(1)}, u32[]{:S(2)}, u32[]{:S(2)}) collective-permute-start(bf16[2,96,896]{2,1,0:T(8,128)(2,1)S(1)} %get-tuple-element.38.refs_3_), channel_id=1, source_target_pairs={{0,3},{1,2},{2,1},{3,0},{4,5},{5,4},{6,7},{7,6},{8,11},{9,10},{10,... | collective-permute-start | bytes 1032200 | tf_op jit(solution)/shard_map/ppermute | solution.py:434

commit v6 on v5

--- a/solution.py
+++ b/solution.py
@@ -11,7 +11,7 @@
 SMEM = pl.BlockSpec(memory_space=pltpu.SMEM)
 HBM = pl.BlockSpec(memory_space=pltpu.HBM)
 VMEM_LIMIT = 40 * 1024 * 1024
-FIRST = 10**10
+FIRST = 2000 * 10**6
 MIDDLE = 8 * 10**8
 
 

time: 59 us -> 58.7 us (level)
  the two profiles are of different devices: /device:TPU:1 before, /device:TPU:0 now
where the time goes in v6:
time: 58.7 us; the launch traced here: 58.6 us
  starting transfers between devices  30.2 us (51%)
  Pallas kernels  20.7 us (35%)
  waiting for transfers between devices  6.96 us (12%)
  between operations  0.73 us (1%)
    ppermute x14, starting transfers between devices, move(): return lax.ppermute(array, ('row', 'col'), pairs)  30.2 us
    pallas_call x4, Pallas kernels, middle_tick(): pl.pallas_call(functools.partial(middle_kernel, tick, stream, corner_widt...  9.11 us
    ppermute x14, waiting for transfers between devices, move(): return lax.ppermute(array, ('row', 'col'), pairs)  6.96 us
    pallas_call x2, Pallas kernels, last_tick(): pl.pallas_call(functools.partial(last_kernel, tick, stream, histories, co...  6.19 us
    pallas_call x1, Pallas kernels, load_operators(): pl.pallas_call(functools.partial(load_kernel, counts, stream), out_shape=...  4.04 us
    pallas_call x1, Pallas kernels, select_initial(): pl.pallas_call(functools.partial(select_kernel, counts, stream), out_shap...  1.36 us
  transfers between devices with their start and end apart: 14, of which 3 were waited for; matrix products, arithmetic and copies ran while one was open for 0% of the time, Pallas kernels for 28%

profile of v6, /device:TPU:0, one launch (start us, length us, event | category | flops | bytes accessed | tf_op | source)
XLA Modules:
  0.0 58.6 jit_solution(14582902220736478627)
XLA Ops:
  0.6 1.4 %select_initial.1 = (bf16[2,96,768]{2,1,0:T(8,128)(2,1)S(1)}, bf16[2,96,768]{2,1,0:T(8,128)(2,1)S(1)}, bf16[2,96,128]{2,1,0:T(8,128)(2,1)S(1)}) custom-call(s32[2,2,3]{2,1,0:T(2,128)} %bitcast.25, bf16[2,2,2,96,768]{4,3,2,1,0:T(8,128)(2,1)} %bitcast.12, bf16[2,2,2,96,768]{4,3,2,1,0:T(8,128)(2,1)} %bitcast.14, bf16[2,2,96,128]{3,2,1,0:T(8,128)(2,1)} %bitcast.19, ...), custom_call_target="tpu_custom_call" | custom-call | tf_op jit(solution)/shard_map/select_initial/pallas_call | solution.py:111
  2.0 3.0 %collective-permute-start.7 = (bf16[2,96,768]{2,1,0:T(8,128)(2,1)S(1)}, bf16[2,96,768]{2,1,0:T(8,128)(2,1)S(1)}, u32[]{:S(2)}, u32[]{:S(2)}) collective-permute-start(bf16[2,96,768]{2,1,0:T(8,128)(2,1)S(1)} %get-tuple-element.39), channel_id=1, source_target_pairs={{0,4},{1,29},{2,6},{3,31},{4,0},{5,9},{6,2},{7,11},{8,12},{9,5},{1... | collective-permute-start | bytes 884744 | tf_op jit(solution)/shard_map/ppermute | solution.py:434
  5.0 2.6 %collective-permute-start.8 = (bf16[2,96,768]{2,1,0:T(8,128)(2,1)S(1)}, bf16[2,96,768]{2,1,0:T(8,128)(2,1)S(1)}, u32[]{:S(2)}, u32[]{:S(2)}) collective-permute-start(bf16[2,96,768]{2,1,0:T(8,128)(2,1)S(1)} %get-tuple-element.40), channel_id=1, source_target_pairs={{0,1},{1,0},{2,3},{3,2},{4,7},{5,6},{6,5},{7,4},{8,9},{9,8},{10,11... | collective-permute-start | bytes 884744 | tf_op jit(solution)/shard_map/ppermute | solution.py:434
  7.6 4.0 %load_operators.1 = (bf16[2,96,768]{2,1,0:T(8,128)(2,1)S(1)}, bf16[2,96,896]{2,1,0:T(8,128)(2,1)S(1)}, bf16[2,2,96,128]{3,2,1,0:T(8,128)(2,1)S(1)}, bf16[2,3072,...) custom-call(s32[2,2,3]{2,1,0:T(2,128)} %bitcast.26, ...), custom_call_target="tpu_custom_call" | custom-call | bytes 1 | tf_op jit(solution)/shard_map/load_operators/pallas_call | solution.py:173
  11.6 1.2 %collective-permute-start.1 = (bf16[2,96,896]{2,1,0:T(8,128)(2,1)S(1)}, bf16[2,96,896]{2,1,0:T(8,128)(2,1)S(1)}, u32[]{:S(2)}, u32[]{:S(2)}) collective-permute-start(bf16[2,96,896]{2,1,0:T(8,128)(2,1)S(1)} %get-tuple-element.31), channel_id=1, source_target_pairs={{0,3},{1,2},{2,1},{3,0},{4,5},{5,4},{6,7},{7,6},{8,11},{9,10},{10,... | collective-permute-start | bytes 1032200 | tf_op jit(solution)/shard_map/ppermute | solution.py:434
  12.9 1.1 %collective-permute-start.9 = (bf16[2,96,128]{2,1,0:T(8,128)(2,1)S(1)}, bf16[2,96,128]{2,1,0:T(8,128)(2,1)S(1)}, u32[]{:S(2)}, u32[]{:S(2)}) collective-permute-start(bf16[2,96,128]{2,1,0:T(8,128)(2,1)S(1)} %get-tuple-element.41), channel_id=1, source_target_pairs={{0,31},{1,6},{2,29},{3,4},{4,9},{5,0},{6,11},{7,2},{8,7},{9,14},{1... | collective-permute-start | bytes 147464 | tf_op jit(solution)/shard_map/ppermute | solution.py:434
  13.9 3.7 %collective-permute-start = (bf16[2,96,768]{2,1,0:T(8,128)(2,1)S(1)}, bf16[2,96,768]{2,1,0:T(8,128)(2,1)S(1)}, u32[]{:S(2)}, u32[]{:S(2)}) collective-permute-start(bf16[2,96,768]{2,1,0:T(8,128)(2,1)S(1)} %get-tuple-element.30), channel_id=1, source_target_pairs={{0,28},{1,5},{2,30},{3,7},{4,8},{5,1},{6,10},{7,3},{8,4},{9,13},{1... | collective-permute-start | bytes 884744 | tf_op jit(solution)/shard_map/ppermute | solution.py:434
  17.7 0.0 collective-permute-done.9.refs_0_
  17.7 0.0 collective-permute-start.2
  17.7 0.0 collective-permute-done.7.first_in
  17.7 0.0 collective-permute-done.8.second_in
  17.7 2.3 %tick0_stream0.1 = (bf16[2,96,768]{2,1,0:T(8,128)(2,1)S(1)}, bf16[2,96,896]{2,1,0:T(8,128)(2,1)S(1)}) custom-call(bf16[2,96,768]{2,1,0:T(8,128)(2,1)S(1)} %collective-permute-done.7.first_in, bf16[2,96,768]{2,1,0:T(8,128)(2,1)S(1)} %collective-permute-done.8.second_in, bf16[2,2,2,96,768]{4,3,2,1,0:T(8,128)(2,1)S(1)} %get-tuple-element.32.sources, ...), custom_call_target="tpu_custom_call" | custom-call | flops 2000000000 | bytes 1 | tf_op jit(solution)/shard_map/tick0_stream0/pallas_call | solution.py:377
  20.0 2.3 %collective-permute-start.11 = (bf16[2,96,896]{2,1,0:T(8,128)(2,1)S(1)}, bf16[2,96,896]{2,1,0:T(8,128)(2,1)S(1)}, u32[]{:S(2)}, u32[]{:S(2)}) collective-permute-start(bf16[2,96,896]{2,1,0:T(8,128)(2,1)S(1)} %get-tuple-element.43), channel_id=1, source_target_pairs={{0,3},{1,2},{2,1},{3,0},{4,5},{5,4},{6,7},{7,6},{8,11},{9,10},{10,... | collective-permute-start | bytes 1032200 | tf_op jit(solution)/shard_map/ppermute | solution.py:434
  22.3 2.5 %collective-permute-start.10 = (bf16[2,96,768]{2,1,0:T(8,128)(2,1)S(1)}, bf16[2,96,768]{2,1,0:T(8,128)(2,1)S(1)}, u32[]{:S(2)}, u32[]{:S(2)}) collective-permute-start(bf16[2,96,768]{2,1,0:T(8,128)(2,1)S(1)} %get-tuple-element.42), channel_id=1, source_target_pairs={{0,28},{1,5},{2,30},{3,7},{4,8},{5,1},{6,10},{7,3},{8,4},{9,13},{1... | collective-permute-start | bytes 884744 | tf_op jit(solution)/shard_map/ppermute | solution.py:434
  24.8 0.8 %collective-permute-done.2.refs_0_ = bf16[2,2,96,128]{3,2,1,0:T(8,128)(2,1)S(1)} collective-permute-done((bf16[2,2,96,128]{3,2,1,0:T(8,128)(2,1)S(1)}, bf16[2,2,96,128]{3,2,1,0:T(8,128)(2,1)S(1)}, u32[]{:S(2)}, u32[]{:S(2)}) %collective-permute-start.2) | collective-permute-done | bytes 98336 | tf_op jit(solution)/shard_map/ppermute | solution.py:434
  25.6 0.0 collective-permute-done.first_in
  25.6 2.3 %tick0_stream1.1 = (bf16[2,96,896]{2,1,0:T(8,128)(2,1)S(1)}, bf16[2,96,896]{2,1,0:T(8,128)(2,1)S(1)}) custom-call(bf16[2,96,768]{2,1,0:T(8,128)(2,1)S(1)} %collective-permute-done.first_in, bf16[2,96,896]{2,1,0:T(8,128)(2,1)S(1)} %collective-permute-done.1.second_in, bf16[2,2,2,96,768]{4,3,2,1,0:T(8,128)(2,1)S(1)} %get-tuple-element.32.sources, ...), custom_call_target="tpu_custom_call" | custom-call | bytes 1 | tf_op jit(solution)/shard_map/tick0_stream1/pallas_call | solution.py:377
  27.9 0.1 collective-permute-start.3
  27.9 4.1 %collective-permute-start.4 = (bf16[2,96,896]{2,1,0:T(8,128)(2,1)S(1)}, bf16[2,96,896]{2,1,0:T(8,128)(2,1)S(1)}, u32[]{:S(2)}, u32[]{:S(2)}) collective-permute-start(bf16[2,96,896]{2,1,0:T(8,128)(2,1)S(1)} %get-tuple-element.36), channel_id=1, source_target_pairs={{0,1},{1,0},{2,3},{3,2},{4,7},{5,6},{6,5},{7,4},{8,9},{9,8},{10,11... | collective-permute-start | bytes 1032200 | tf_op jit(solution)/shard_map/ppermute | solution.py:434
  32.1 2.3 %tick1_stream0.1 = (bf16[2,96,896]{2,1,0:T(8,128)(2,1)S(1)}, bf16[2,96,896]{2,1,0:T(8,128)(2,1)S(1)}) custom-call(bf16[2,96,768]{2,1,0:T(8,128)(2,1)S(1)} %collective-permute-done.10.first_in, bf16[2,96,896]{2,1,0:T(8,128)(2,1)S(1)} %collective-permute-done.11.second_in, bf16[2,2,2,96,768]{4,3,2,1,0:T(8,128)(2,1)S(1)} %get-tuple-element.32.sources, ...), custom_call_target="tpu_custom_call" | custom-call | flops 800000000 | bytes 1 | tf_op jit(solution)/shard_map/tick1_stream0/pallas_call | solution.py:377
  34.4 0.1 collective-permute-start.12
  34.4 5.1 %collective-permute-start.13 = (bf16[2,96,896]{2,1,0:T(8,128)(2,1)S(1)}, bf16[2,96,896]{2,1,0:T(8,128)(2,1)S(1)}, u32[]{:S(2)}, u32[]{:S(2)}) collective-permute-start(bf16[2,96,896]{2,1,0:T(8,128)(2,1)S(1)} %get-tuple-element.45.refs_1_), channel_id=1, source_target_pairs={{0,1},{1,0},{2,3},{3,2},{4,7},{5,6},{6,5},{7,4},{8,9},{9,8},{10,11... | collective-permute-start | bytes 1032200 | tf_op jit(solution)/shard_map/ppermute | solution.py:434
  39.5 0.0 collective-permute-done.4.second_in
  39.5 2.3 %tick1_stream1.1 = (bf16[2,96,896]{2,1,0:T(8,128)(2,1)S(1)}, bf16[2,96,896]{2,1,0:T(8,128)(2,1)S(1)}) custom-call(bf16[2,96,896]{2,1,0:T(8,128)(2,1)S(1)} %collective-permute-done.3.first_in, bf16[2,96,896]{2,1,0:T(8,128)(2,1)S(1)} %collective-permute-done.4.second_in, bf16[2,2,2,96,768]{4,3,2,1,0:T(8,128)(2,1)S(1)} %get-tuple-element.32.sources, ...), custom_call_target="tpu_custom_call" | custom-call | bytes 1 | tf_op jit(solution)/shard_map/tick1_stream1/pallas_call | solution.py:377
  41.8 4.4 %collective-permute-start.5 = (bf16[2,96,896]{2,1,0:T(8,128)(2,1)S(1)}, bf16[2,96,896]{2,1,0:T(8,128)(2,1)S(1)}, u32[]{:S(2)}, u32[]{:S(2)}) collective-permute-start(bf16[2,96,896]{2,1,0:T(8,128)(2,1)S(1)} %get-tuple-element.37.refs_2_), channel_id=1, source_target_pairs={{0,28},{1,5},{2,30},{3,7},{4,8},{5,1},{6,10},{7,3},{8,4},{9,13},{1... | collective-permute-start | bytes 1032200 | tf_op jit(solution)/shard_map/ppermute | solution.py:434
  46.2 0.0 collective-permute-start.6
  46.2 0.0 collective-permute-done.12.first_in
  46.2 0.0 collective-permute-done.13.second_in
  46.2 3.1 %tick2_stream0.1 = (bf16[2,2,2,96,768]{4,3,2,1,0:T(8,128)(2,1)}, bf16[2,2,2,96,768]{4,3,2,1,0:T(8,128)(2,1)}, bf16[2,2,96,128]{3,2,1,0:T(8,128)(2,1)}, bf16[2,2,96,128]{3,2,1,0:T(8,128)(2,1)}) custom-call(f32[2,8,128]{2,1,0:T(8,128)S(1)} %get-tuple-element.29.flags, bf16[2,96,896]{2,1,0:T(8,128)(2,1)S(1)} %collective-permute-done.12.first_in, ...), custom_call_target="tpu_custom_call" | custom-call | bytes 1 | tf_op jit(solution)/shard_map/tick2_stream0/pallas_call | solution.py:410
  49.3 2.6 %collective-permute-done.5.first_in = bf16[2,96,896]{2,1,0:T(8,128)(2,1)S(1)} collective-permute-done((bf16[2,96,896]{2,1,0:T(8,128)(2,1)S(1)}, bf16[2,96,896]{2,1,0:T(8,128)(2,1)S(1)}, u32[]{:S(2)}, u32[]{:S(2)}) %collective-permute-start.5) | collective-permute-done | bytes 344096 | tf_op jit(solution)/shard_map/ppermute | solution.py:434
  51.9 3.6 %collective-permute-done.6.second_in = bf16[2,96,896]{2,1,0:T(8,128)(2,1)S(1)} collective-permute-done((bf16[2,96,896]{2,1,0:T(8,128)(2,1)S(1)}, bf16[2,96,896]{2,1,0:T(8,128)(2,1)S(1)}, u32[]{:S(2)}, u32[]{:S(2)}) %collective-permute-start.6) | collective-permute-done | bytes 344096 | tf_op jit(solution)/shard_map/ppermute | solution.py:434
  55.5 3.1 %tick2_stream1.1 = (bf16[2,2,2,96,768]{4,3,2,1,0:T(8,128)(2,1)}, bf16[2,2,2,96,768]{4,3,2,1,0:T(8,128)(2,1)}, bf16[2,2,96,128]{3,2,1,0:T(8,128)(2,1)}, bf16[2,2,96,128]{3,2,1,0:T(8,128)(2,1)}) custom-call(f32[2,8,128]{2,1,0:T(8,128)S(1)} %get-tuple-element.29.flags, ...), custom_call_target="tpu_custom_call", output_to_operand_aliasing={{0}: (5, {}), {1}: (6, {}), {2}: (7, {}), {3}: (8, {})} | custom-call | bytes 1 | tf_op jit(solution)/shard_map/tick2_stream1/pallas_call | solution.py:410
  (4 shorter events, 0.0 us)
Async XLA Ops:
  2.0 15.7 %collective-permute-start.7 = (bf16[2,96,768]{2,1,0:T(8,128)(2,1)S(1)}, bf16[2,96,768]{2,1,0:T(8,128)(2,1)S(1)}, u32[]{:S(2)}, u32[]{:S(2)}) collective-permute-start(bf16[2,96,768]{2,1,0:T(8,128)(2,1)S(1)} %get-tuple-element.39), channel_id=1, source_target_pairs={{0,4},{1,29},{2,6},{3,31},{4,0},{5,9},{6,2},{7,11},{8,12},{9,5},{1... | collective-permute-start | bytes 884744 | tf_op jit(solution)/shard_map/ppermute | solution.py:434
  5.0 12.7 %collective-permute-start.8 = (bf16[2,96,768]{2,1,0:T(8,128)(2,1)S(1)}, bf16[2,96,768]{2,1,0:T(8,128)(2,1)S(1)}, u32[]{:S(2)}, u32[]{:S(2)}) collective-permute-start(bf16[2,96,768]{2,1,0:T(8,128)(2,1)S(1)} %get-tuple-element.40), channel_id=1, source_target_pairs={{0,1},{1,0},{2,3},{3,2},{4,7},{5,6},{6,5},{7,4},{8,9},{9,8},{10,11... | collective-permute-start | bytes 884744 | tf_op jit(solution)/shard_map/ppermute | solution.py:434
  11.6 13.9 %collective-permute-start.1 = (bf16[2,96,896]{2,1,0:T(8,128)(2,1)S(1)}, bf16[2,96,896]{2,1,0:T(8,128)(2,1)S(1)}, u32[]{:S(2)}, u32[]{:S(2)}) collective-permute-start(bf16[2,96,896]{2,1,0:T(8,128)(2,1)S(1)} %get-tuple-element.31), channel_id=1, source_target_pairs={{0,3},{1,2},{2,1},{3,0},{4,5},{5,4},{6,7},{7,6},{8,11},{9,10},{10,... | collective-permute-start | bytes 1032200 | tf_op jit(solution)/shard_map/ppermute | solution.py:434
  12.9 4.8 %collective-permute-start.9 = (bf16[2,96,128]{2,1,0:T(8,128)(2,1)S(1)}, bf16[2,96,128]{2,1,0:T(8,128)(2,1)S(1)}, u32[]{:S(2)}, u32[]{:S(2)}) collective-permute-start(bf16[2,96,128]{2,1,0:T(8,128)(2,1)S(1)} %get-tuple-element.41), channel_id=1, source_target_pairs={{0,31},{1,6},{2,29},{3,4},{4,9},{5,0},{6,11},{7,2},{8,7},{9,14},{1... | collective-permute-start | bytes 147464 | tf_op jit(solution)/shard_map/ppermute | solution.py:434
  13.9 11.6 %collective-permute-start = (bf16[2,96,768]{2,1,0:T(8,128)(2,1)S(1)}, bf16[2,96,768]{2,1,0:T(8,128)(2,1)S(1)}, u32[]{:S(2)}, u32[]{:S(2)}) collective-permute-start(bf16[2,96,768]{2,1,0:T(8,128)(2,1)S(1)} %get-tuple-element.30), channel_id=1, source_target_pairs={{0,28},{1,5},{2,30},{3,7},{4,8},{5,1},{6,10},{7,3},{8,4},{9,13},{1... | collective-permute-start | bytes 884744 | tf_op jit(solution)/shard_map/ppermute | solution.py:434
  17.7 7.9 %collective-permute-start.2 = (bf16[2,2,96,128]{3,2,1,0:T(8,128)(2,1)S(1)}, bf16[2,2,96,128]{3,2,1,0:T(8,128)(2,1)S(1)}, u32[]{:S(2)}, u32[]{:S(2)}) collective-permute-start(bf16[2,2,96,128]{3,2,1,0:T(8,128)(2,1)S(1)} %get-tuple-element.34), channel_id=1, source_target_pairs={{0,5},{1,28},{2,7},{3,30},{4,3},{5,10},{6,1},{7,8},{8,13},{9,4},{1... | collective-permute-start | bytes 294920 | tf_op jit(solution)/shard_map/ppermute | solution.py:434
  20.0 12.1 %collective-permute-start.11 = (bf16[2,96,896]{2,1,0:T(8,128)(2,1)S(1)}, bf16[2,96,896]{2,1,0:T(8,128)(2,1)S(1)}, u32[]{:S(2)}, u32[]{:S(2)}) collective-permute-start(bf16[2,96,896]{2,1,0:T(8,128)(2,1)S(1)} %get-tuple-element.43), channel_id=1, source_target_pairs={{0,3},{1,2},{2,1},{3,0},{4,5},{5,4},{6,7},{7,6},{8,11},{9,10},{10,... | collective-permute-start | bytes 1032200 | tf_op jit(solution)/shard_map/ppermute | solution.py:434
  22.3 9.8 %collective-permute-start.10 = (bf16[2,96,768]{2,1,0:T(8,128)(2,1)S(1)}, bf16[2,96,768]{2,1,0:T(8,128)(2,1)S(1)}, u32[]{:S(2)}, u32[]{:S(2)}) collective-permute-start(bf16[2,96,768]{2,1,0:T(8,128)(2,1)S(1)} %get-tuple-element.42), channel_id=1, source_target_pairs={{0,28},{1,5},{2,30},{3,7},{4,8},{5,1},{6,10},{7,3},{8,4},{9,13},{1... | collective-permute-start | bytes 884744 | tf_op jit(solution)/shard_map/ppermute | solution.py:434
  27.9 11.7 %collective-permute-start.3 = (bf16[2,96,896]{2,1,0:T(8,128)(2,1)S(1)}, bf16[2,96,896]{2,1,0:T(8,128)(2,1)S(1)}, u32[]{:S(2)}, u32[]{:S(2)}) collective-permute-start(bf16[2,96,896]{2,1,0:T(8,128)(2,1)S(1)} %get-tuple-element.35), channel_id=1, source_target_pairs={{0,4},{1,29},{2,6},{3,31},{4,0},{5,9},{6,2},{7,11},{8,12},{9,5},{1... | collective-permute-start | bytes 1032200 | tf_op jit(solution)/shard_map/ppermute | solution.py:434
  27.9 11.6 %collective-permute-start.4 = (bf16[2,96,896]{2,1,0:T(8,128)(2,1)S(1)}, bf16[2,96,896]{2,1,0:T(8,128)(2,1)S(1)}, u32[]{:S(2)}, u32[]{:S(2)}) collective-permute-start(bf16[2,96,896]{2,1,0:T(8,128)(2,1)S(1)} %get-tuple-element.36), channel_id=1, source_target_pairs={{0,1},{1,0},{2,3},{3,2},{4,7},{5,6},{6,5},{7,4},{8,9},{9,8},{10,11... | collective-permute-start | bytes 1032200 | tf_op jit(solution)/shard_map/ppermute | solution.py:434
  34.4 11.8 %collective-permute-start.12 = (bf16[2,96,896]{2,1,0:T(8,128)(2,1)S(1)}, bf16[2,96,896]{2,1,0:T(8,128)(2,1)S(1)}, u32[]{:S(2)}, u32[]{:S(2)}) collective-permute-start(bf16[2,96,896]{2,1,0:T(8,128)(2,1)S(1)} %get-tuple-element.44.refs_0_), channel_id=1, source_target_pairs={{0,4},{1,29},{2,6},{3,31},{4,0},{5,9},{6,2},{7,11},{8,12},{9,5},{1... | collective-permute-start | bytes 1032200 | tf_op jit(solution)/shard_map/ppermute | solution.py:434
  34.4 11.8 %collective-permute-start.13 = (bf16[2,96,896]{2,1,0:T(8,128)(2,1)S(1)}, bf16[2,96,896]{2,1,0:T(8,128)(2,1)S(1)}, u32[]{:S(2)}, u32[]{:S(2)}) collective-permute-start(bf16[2,96,896]{2,1,0:T(8,128)(2,1)S(1)} %get-tuple-element.45.refs_1_), channel_id=1, source_target_pairs={{0,1},{1,0},{2,3},{3,2},{4,7},{5,6},{6,5},{7,4},{8,9},{9,8},{10,11... | collective-permute-start | bytes 1032200 | tf_op jit(solution)/shard_map/ppermute | solution.py:434
  41.8 10.1 %collective-permute-start.5 = (bf16[2,96,896]{2,1,0:T(8,128)(2,1)S(1)}, bf16[2,96,896]{2,1,0:T(8,128)(2,1)S(1)}, u32[]{:S(2)}, u32[]{:S(2)}) collective-permute-start(bf16[2,96,896]{2,1,0:T(8,128)(2,1)S(1)} %get-tuple-element.37.refs_2_), channel_id=1, source_target_pairs={{0,28},{1,5},{2,30},{3,7},{4,8},{5,1},{6,10},{7,3},{8,4},{9,13},{1... | collective-permute-start | bytes 1032200 | tf_op jit(solution)/shard_map/ppermute | solution.py:434
  46.2 9.3 %collective-permute-start.6 = (bf16[2,96,896]{2,1,0:T(8,128)(2,1)S(1)}, bf16[2,96,896]{2,1,0:T(8,128)(2,1)S(1)}, u32[]{:S(2)}, u32[]{:S(2)}) collective-permute-start(bf16[2,96,896]{2,1,0:T(8,128)(2,1)S(1)} %get-tuple-element.38.refs_3_), channel_id=1, source_target_pairs={{0,3},{1,2},{2,1},{3,0},{4,5},{5,4},{6,7},{7,6},{8,11},{9,10},{10,... | collective-permute-start | bytes 1032200 | tf_op jit(solution)/shard_map/ppermute | solution.py:434

commit v7 on v6

--- a/solution.py
+++ b/solution.py
@@ -251,6 +251,10 @@
         act(step, at)
 
 
+def in_order(stream, first, second):
+    return (second, first) if stream else (first, second)
+
+
 def middle_kernel(
     tick, stream, corner_width, first_in, second_in, sources, operators, *refs
 ):
@@ -264,8 +268,9 @@
 
 
 def last_kernel(
-    tick, stream, histories, corner_width, flags, first_in, second_in, sources, operators, *refs
-):
+    tick, stream, histories, corner_width, flags, one_in, two_in, sources, operators, *refs
+):
+    first_in, second_in = in_order(stream, one_in, two_in)
     count = len(histories)
     older = [refs[2 * i : 2 * i + 2] for i in range(count)]
     refs = refs[2 * count :]
@@ -394,7 +399,7 @@
     kind = sources.dtype
     outs = [jax.ShapeDtypeStruct((2, batches, parts, shots, edge_width), kind)] * 2
     outs += [jax.ShapeDtypeStruct((batches, parts, shots, corner_width), kind)] * 2
-    operands = [flags, first_in, second_in, sources, operators]
+    operands = [flags, *in_order(stream, first_in, second_in), sources, operators]
     in_specs = [VMEM] * 5
     aliases = {}
     if so_far is None:

time: 58.7 us -> 57.2 us (0.974); the launches traced: 58.6 us -> 56.3 us
  waiting for transfers between devices: 6.96 us -> 4.64 us
    ppermute x14, waiting for transfers between devices: 6.96 us -> 4.64 us  [move(): return lax.ppermute(array, ('row', 'col'), pairs)]
  transfers between devices with their start and end apart: 14 -> 14, of which waited for: 3 -> 3; matrix products, arithmetic and copies ran while one was open for 0% -> 0% of each run, Pallas kernels for 28% -> 29%
where the time goes in v7:
time: 57.2 us; the launch traced here: 56.3 us
  starting transfers between devices  30.2 us (53%)
  Pallas kernels  20.7 us (36%)
  waiting for transfers between devices  4.64 us (8%)
  between operations  0.72 us (1%)
    ppermute x14, starting transfers between devices, move(): return lax.ppermute(array, ('row', 'col'), pairs)  30.2 us
    pallas_call x4, Pallas kernels, middle_tick(): pl.pallas_call(functools.partial(middle_kernel, tick, stream, corner_widt...  9.11 us
    pallas_call x2, Pallas kernels, last_tick(): pl.pallas_call(functools.partial(last_kernel, tick, stream, histories, co...  6.19 us
    ppermute x14, waiting for transfers between devices, move(): return lax.ppermute(array, ('row', 'col'), pairs)  4.64 us
    pallas_call x1, Pallas kernels, load_operators(): pl.pallas_call(functools.partial(load_kernel, counts, stream), out_shape=...  4.04 us
    pallas_call x1, Pallas kernels, select_initial(): pl.pallas_call(functools.partial(select_kernel, counts, stream), out_shap...  1.36 us
  transfers between devices with their start and end apart: 14, of which 3 were waited for; matrix products, arithmetic and copies ran while one was open for 0% of the time, Pallas kernels for 29%

profile of v7, /device:TPU:0, one launch (start us, length us, event | category | flops | bytes accessed | tf_op | source)
XLA Modules:
  0.0 56.3 jit_solution(8597789098445738724)
XLA Ops:
  0.6 1.4 %select_initial.1 = (bf16[2,96,768]{2,1,0:T(8,128)(2,1)S(1)}, bf16[2,96,768]{2,1,0:T(8,128)(2,1)S(1)}, bf16[2,96,128]{2,1,0:T(8,128)(2,1)S(1)}) custom-call(s32[2,2,3]{2,1,0:T(2,128)} %bitcast.25, bf16[2,2,2,96,768]{4,3,2,1,0:T(8,128)(2,1)} %bitcast.12, bf16[2,2,2,96,768]{4,3,2,1,0:T(8,128)(2,1)} %bitcast.14, bf16[2,2,96,128]{3,2,1,0:T(8,128)(2,1)} %bitcast.19, ...), custom_call_target="tpu_custom_call" | custom-call | tf_op jit(solution)/shard_map/select_initial/pallas_call | solution.py:111
  2.0 3.0 %collective-permute-start.7 = (bf16[2,96,768]{2,1,0:T(8,128)(2,1)S(1)}, bf16[2,96,768]{2,1,0:T(8,128)(2,1)S(1)}, u32[]{:S(2)}, u32[]{:S(2)}) collective-permute-start(bf16[2,96,768]{2,1,0:T(8,128)(2,1)S(1)} %get-tuple-element.39), channel_id=1, source_target_pairs={{0,4},{1,29},{2,6},{3,31},{4,0},{5,9},{6,2},{7,11},{8,12},{9,5},{1... | collective-permute-start | bytes 884744 | tf_op jit(solution)/shard_map/ppermute | solution.py:439
  5.0 2.6 %collective-permute-start.8 = (bf16[2,96,768]{2,1,0:T(8,128)(2,1)S(1)}, bf16[2,96,768]{2,1,0:T(8,128)(2,1)S(1)}, u32[]{:S(2)}, u32[]{:S(2)}) collective-permute-start(bf16[2,96,768]{2,1,0:T(8,128)(2,1)S(1)} %get-tuple-element.40), channel_id=1, source_target_pairs={{0,1},{1,0},{2,3},{3,2},{4,7},{5,6},{6,5},{7,4},{8,9},{9,8},{10,11... | collective-permute-start | bytes 884744 | tf_op jit(solution)/shard_map/ppermute | solution.py:439
  7.6 4.0 %load_operators.1 = (bf16[2,96,768]{2,1,0:T(8,128)(2,1)S(1)}, bf16[2,96,896]{2,1,0:T(8,128)(2,1)S(1)}, bf16[2,2,96,128]{3,2,1,0:T(8,128)(2,1)S(1)}, bf16[2,3072,...) custom-call(s32[2,2,3]{2,1,0:T(2,128)} %bitcast.26, ...), custom_call_target="tpu_custom_call" | custom-call | bytes 1 | tf_op jit(solution)/shard_map/load_operators/pallas_call | solution.py:173
  11.6 1.2 %collective-permute-start.1 = (bf16[2,96,896]{2,1,0:T(8,128)(2,1)S(1)}, bf16[2,96,896]{2,1,0:T(8,128)(2,1)S(1)}, u32[]{:S(2)}, u32[]{:S(2)}) collective-permute-start(bf16[2,96,896]{2,1,0:T(8,128)(2,1)S(1)} %get-tuple-element.31), channel_id=1, source_target_pairs={{0,3},{1,2},{2,1},{3,0},{4,5},{5,4},{6,7},{7,6},{8,11},{9,10},{10,... | collective-permute-start | bytes 1032200 | tf_op jit(solution)/shard_map/ppermute | solution.py:439
  12.9 1.1 %collective-permute-start.9 = (bf16[2,96,128]{2,1,0:T(8,128)(2,1)S(1)}, bf16[2,96,128]{2,1,0:T(8,128)(2,1)S(1)}, u32[]{:S(2)}, u32[]{:S(2)}) collective-permute-start(bf16[2,96,128]{2,1,0:T(8,128)(2,1)S(1)} %get-tuple-element.41), channel_id=1, source_target_pairs={{0,31},{1,6},{2,29},{3,4},{4,9},{5,0},{6,11},{7,2},{8,7},{9,14},{1... | collective-permute-start | bytes 147464 | tf_op jit(solution)/shard_map/ppermute | solution.py:439
  13.9 3.7 %collective-permute-start = (bf16[2,96,768]{2,1,0:T(8,128)(2,1)S(1)}, bf16[2,96,768]{2,1,0:T(8,128)(2,1)S(1)}, u32[]{:S(2)}, u32[]{:S(2)}) collective-permute-start(bf16[2,96,768]{2,1,0:T(8,128)(2,1)S(1)} %get-tuple-element.30), channel_id=1, source_target_pairs={{0,28},{1,5},{2,30},{3,7},{4,8},{5,1},{6,10},{7,3},{8,4},{9,13},{1... | collective-permute-start | bytes 884744 | tf_op jit(solution)/shard_map/ppermute | solution.py:439
  17.7 0.0 collective-permute-done.9.refs_0_
  17.7 0.0 collective-permute-start.2
  17.7 0.0 collective-permute-done.7.first_in
  17.7 2.3 %tick0_stream0.1 = (bf16[2,96,768]{2,1,0:T(8,128)(2,1)S(1)}, bf16[2,96,896]{2,1,0:T(8,128)(2,1)S(1)}) custom-call(bf16[2,96,768]{2,1,0:T(8,128)(2,1)S(1)} %collective-permute-done.7.first_in, bf16[2,96,768]{2,1,0:T(8,128)(2,1)S(1)} %collective-permute-done.8.second_in, bf16[2,2,2,96,768]{4,3,2,1,0:T(8,128)(2,1)S(1)} %get-tuple-element.32.sources, ...), custom_call_target="tpu_custom_call" | custom-call | flops 2000000000 | bytes 1 | tf_op jit(solution)/shard_map/tick0_stream0/pallas_call | solution.py:382
  20.0 2.3 %collective-permute-start.11 = (bf16[2,96,896]{2,1,0:T(8,128)(2,1)S(1)}, bf16[2,96,896]{2,1,0:T(8,128)(2,1)S(1)}, u32[]{:S(2)}, u32[]{:S(2)}) collective-permute-start(bf16[2,96,896]{2,1,0:T(8,128)(2,1)S(1)} %get-tuple-element.43), channel_id=1, source_target_pairs={{0,3},{1,2},{2,1},{3,0},{4,5},{5,4},{6,7},{7,6},{8,11},{9,10},{10,... | collective-permute-start | bytes 1032200 | tf_op jit(solution)/shard_map/ppermute | solution.py:439
  22.3 2.5 %collective-permute-start.10 = (bf16[2,96,768]{2,1,0:T(8,128)(2,1)S(1)}, bf16[2,96,768]{2,1,0:T(8,128)(2,1)S(1)}, u32[]{:S(2)}, u32[]{:S(2)}) collective-permute-start(bf16[2,96,768]{2,1,0:T(8,128)(2,1)S(1)} %get-tuple-element.42), channel_id=1, source_target_pairs={{0,28},{1,5},{2,30},{3,7},{4,8},{5,1},{6,10},{7,3},{8,4},{9,13},{1... | collective-permute-start | bytes 884744 | tf_op jit(solution)/shard_map/ppermute | solution.py:439
  24.8 0.8 %collective-permute-done.2.refs_0_ = bf16[2,2,96,128]{3,2,1,0:T(8,128)(2,1)S(1)} collective-permute-done((bf16[2,2,96,128]{3,2,1,0:T(8,128)(2,1)S(1)}, bf16[2,2,96,128]{3,2,1,0:T(8,128)(2,1)S(1)}, u32[]{:S(2)}, u32[]{:S(2)}) %collective-permute-start.2) | collective-permute-done | bytes 98336 | tf_op jit(solution)/shard_map/ppermute | solution.py:439
  25.6 0.0 collective-permute-done.first_in
  25.6 0.0 collective-permute-done.1.second_in
  25.6 2.3 %tick0_stream1.1 = (bf16[2,96,896]{2,1,0:T(8,128)(2,1)S(1)}, bf16[2,96,896]{2,1,0:T(8,128)(2,1)S(1)}) custom-call(bf16[2,96,768]{2,1,0:T(8,128)(2,1)S(1)} %collective-permute-done.first_in, bf16[2,96,896]{2,1,0:T(8,128)(2,1)S(1)} %collective-permute-done.1.second_in, bf16[2,2,2,96,768]{4,3,2,1,0:T(8,128)(2,1)S(1)} %get-tuple-element.32.sources, ...), custom_call_target="tpu_custom_call" | custom-call | bytes 1 | tf_op jit(solution)/shard_map/tick0_stream1/pallas_call | solution.py:382
  27.9 0.1 collective-permute-start.3
  27.9 4.1 %collective-permute-start.4 = (bf16[2,96,896]{2,1,0:T(8,128)(2,1)S(1)}, bf16[2,96,896]{2,1,0:T(8,128)(2,1)S(1)}, u32[]{:S(2)}, u32[]{:S(2)}) collective-permute-start(bf16[2,96,896]{2,1,0:T(8,128)(2,1)S(1)} %get-tuple-element.36), channel_id=1, source_target_pairs={{0,1},{1,0},{2,3},{3,2},{4,7},{5,6},{6,5},{7,4},{8,9},{9,8},{10,11... | collective-permute-start | bytes 1032200 | tf_op jit(solution)/shard_map/ppermute | solution.py:439
  32.1 0.0 collective-permute-done.10.first_in
  32.1 0.0 collective-permute-done.11.second_in
  32.1 2.3 %tick1_stream0.1 = (bf16[2,96,896]{2,1,0:T(8,128)(2,1)S(1)}, bf16[2,96,896]{2,1,0:T(8,128)(2,1)S(1)}) custom-call(bf16[2,96,768]{2,1,0:T(8,128)(2,1)S(1)} %collective-permute-done.10.first_in, bf16[2,96,896]{2,1,0:T(8,128)(2,1)S(1)} %collective-permute-done.11.second_in, bf16[2,2,2,96,768]{4,3,2,1,0:T(8,128)(2,1)S(1)} %get-tuple-element.32.sources, ...), custom_call_target="tpu_custom_call" | custom-call | flops 800000000 | bytes 1 | tf_op jit(solution)/shard_map/tick1_stream0/pallas_call | solution.py:382
  34.4 0.1 collective-permute-start.12
  34.4 5.1 %collective-permute-start.13 = (bf16[2,96,896]{2,1,0:T(8,128)(2,1)S(1)}, bf16[2,96,896]{2,1,0:T(8,128)(2,1)S(1)}, u32[]{:S(2)}, u32[]{:S(2)}) collective-permute-start(bf16[2,96,896]{2,1,0:T(8,128)(2,1)S(1)} %get-tuple-element.45.refs_1_), channel_id=1, source_target_pairs={{0,1},{1,0},{2,3},{3,2},{4,7},{5,6},{6,5},{7,4},{8,9},{9,8},{10,11... | collective-permute-start | bytes 1032200 | tf_op jit(solution)/shard_map/ppermute | solution.py:439
  39.5 0.0 collective-permute-done.3.first_in
  39.5 2.3 %tick1_stream1.1 = (bf16[2,96,896]{2,1,0:T(8,128)(2,1)S(1)}, bf16[2,96,896]{2,1,0:T(8,128)(2,1)S(1)}) custom-call(bf16[2,96,896]{2,1,0:T(8,128)(2,1)S(1)} %collective-permute-done.3.first_in, bf16[2,96,896]{2,1,0:T(8,128)(2,1)S(1)} %collective-permute-done.4.second_in, bf16[2,2,2,96,768]{4,3,2,1,0:T(8,128)(2,1)S(1)} %get-tuple-element.32.sources, ...), custom_call_target="tpu_custom_call" | custom-call | bytes 1 | tf_op jit(solution)/shard_map/tick1_stream1/pallas_call | solution.py:382
  41.8 1.4 %collective-permute-start.5 = (bf16[2,96,896]{2,1,0:T(8,128)(2,1)S(1)}, bf16[2,96,896]{2,1,0:T(8,128)(2,1)S(1)}, u32[]{:S(2)}, u32[]{:S(2)}) collective-permute-start(bf16[2,96,896]{2,1,0:T(8,128)(2,1)S(1)} %get-tuple-element.37.refs_3_), channel_id=1, source_target_pairs={{0,3},{1,2},{2,1},{3,0},{4,5},{5,4},{6,7},{7,6},{8,11},{9,10},{10,... | collective-permute-start | bytes 1032200 | tf_op jit(solution)/shard_map/ppermute | solution.py:439
  43.2 3.1 %collective-permute-start.6 = (bf16[2,96,896]{2,1,0:T(8,128)(2,1)S(1)}, bf16[2,96,896]{2,1,0:T(8,128)(2,1)S(1)}, u32[]{:S(2)}, u32[]{:S(2)}) collective-permute-start(bf16[2,96,896]{2,1,0:T(8,128)(2,1)S(1)} %get-tuple-element.38.refs_2_), channel_id=1, source_target_pairs={{0,28},{1,5},{2,30},{3,7},{4,8},{5,1},{6,10},{7,3},{8,4},{9,13},{1... | collective-permute-start | bytes 1032200 | tf_op jit(solution)/shard_map/ppermute | solution.py:439
  46.3 3.1 %tick2_stream0.1 = (bf16[2,2,2,96,768]{4,3,2,1,0:T(8,128)(2,1)}, bf16[2,2,2,96,768]{4,3,2,1,0:T(8,128)(2,1)}, bf16[2,2,96,128]{3,2,1,0:T(8,128)(2,1)}, bf16[2,2,96,128]{3,2,1,0:T(8,128)(2,1)}) custom-call(f32[2,8,128]{2,1,0:T(8,128)S(1)} %get-tuple-element.29.flags, bf16[2,96,896]{2,1,0:T(8,128)(2,1)S(1)} %collective-permute-done.12.one_in, ...), custom_call_target="tpu_custom_call" | custom-call | bytes 1 | tf_op jit(solution)/shard_map/tick2_stream0/pallas_call | solution.py:415
  49.4 2.6 %collective-permute-done.5.one_in = bf16[2,96,896]{2,1,0:T(8,128)(2,1)S(1)} collective-permute-done((bf16[2,96,896]{2,1,0:T(8,128)(2,1)S(1)}, bf16[2,96,896]{2,1,0:T(8,128)(2,1)S(1)}, u32[]{:S(2)}, u32[]{:S(2)}) %collective-permute-start.5) | collective-permute-done | bytes 344096 | tf_op jit(solution)/shard_map/ppermute | solution.py:439
  52.0 1.3 %collective-permute-done.6.two_in = bf16[2,96,896]{2,1,0:T(8,128)(2,1)S(1)} collective-permute-done((bf16[2,96,896]{2,1,0:T(8,128)(2,1)S(1)}, bf16[2,96,896]{2,1,0:T(8,128)(2,1)S(1)}, u32[]{:S(2)}, u32[]{:S(2)}) %collective-permute-start.6) | collective-permute-done | bytes 344096 | tf_op jit(solution)/shard_map/ppermute | solution.py:439
  53.2 3.1 %tick2_stream1.1 = (bf16[2,2,2,96,768]{4,3,2,1,0:T(8,128)(2,1)}, bf16[2,2,2,96,768]{4,3,2,1,0:T(8,128)(2,1)}, bf16[2,2,96,128]{3,2,1,0:T(8,128)(2,1)}, bf16[2,2,96,128]{3,2,1,0:T(8,128)(2,1)}) custom-call(f32[2,8,128]{2,1,0:T(8,128)S(1)} %get-tuple-element.29.flags, ...), custom_call_target="tpu_custom_call", output_to_operand_aliasing={{0}: (5, {}), {1}: (6, {}), {2}: (7, {}), {3}: (8, {})} | custom-call | bytes 1 | tf_op jit(solution)/shard_map/tick2_stream1/pallas_call | solution.py:415
  (4 shorter events, 0.0 us)
Async XLA Ops:
  2.0 15.7 %collective-permute-start.7 = (bf16[2,96,768]{2,1,0:T(8,128)(2,1)S(1)}, bf16[2,96,768]{2,1,0:T(8,128)(2,1)S(1)}, u32[]{:S(2)}, u32[]{:S(2)}) collective-permute-start(bf16[2,96,768]{2,1,0:T(8,128)(2,1)S(1)} %get-tuple-element.39), channel_id=1, source_target_pairs={{0,4},{1,29},{2,6},{3,31},{4,0},{5,9},{6,2},{7,11},{8,12},{9,5},{1... | collective-permute-start | bytes 884744 | tf_op jit(solution)/shard_map/ppermute | solution.py:439
  5.0 12.7 %collective-permute-start.8 = (bf16[2,96,768]{2,1,0:T(8,128)(2,1)S(1)}, bf16[2,96,768]{2,1,0:T(8,128)(2,1)S(1)}, u32[]{:S(2)}, u32[]{:S(2)}) collective-permute-start(bf16[2,96,768]{2,1,0:T(8,128)(2,1)S(1)} %get-tuple-element.40), channel_id=1, source_target_pairs={{0,1},{1,0},{2,3},{3,2},{4,7},{5,6},{6,5},{7,4},{8,9},{9,8},{10,11... | collective-permute-start | bytes 884744 | tf_op jit(solution)/shard_map/ppermute | solution.py:439
  11.6 13.9 %collective-permute-start.1 = (bf16[2,96,896]{2,1,0:T(8,128)(2,1)S(1)}, bf16[2,96,896]{2,1,0:T(8,128)(2,1)S(1)}, u32[]{:S(2)}, u32[]{:S(2)}) collective-permute-start(bf16[2,96,896]{2,1,0:T(8,128)(2,1)S(1)} %get-tuple-element.31), channel_id=1, source_target_pairs={{0,3},{1,2},{2,1},{3,0},{4,5},{5,4},{6,7},{7,6},{8,11},{9,10},{10,... | collective-permute-start | bytes 1032200 | tf_op jit(solution)/shard_map/ppermute | solution.py:439
  12.9 4.8 %collective-permute-start.9 = (bf16[2,96,128]{2,1,0:T(8,128)(2,1)S(1)}, bf16[2,96,128]{2,1,0:T(8,128)(2,1)S(1)}, u32[]{:S(2)}, u32[]{:S(2)}) collective-permute-start(bf16[2,96,128]{2,1,0:T(8,128)(2,1)S(1)} %get-tuple-element.41), channel_id=1, source_target_pairs={{0,31},{1,6},{2,29},{3,4},{4,9},{5,0},{6,11},{7,2},{8,7},{9,14},{1... | collective-permute-start | bytes 147464 | tf_op jit(solution)/shard_map/ppermute | solution.py:439
  13.9 11.6 %collective-permute-start = (bf16[2,96,768]{2,1,0:T(8,128)(2,1)S(1)}, bf16[2,96,768]{2,1,0:T(8,128)(2,1)S(1)}, u32[]{:S(2)}, u32[]{:S(2)}) collective-permute-start(bf16[2,96,768]{2,1,0:T(8,128)(2,1)S(1)} %get-tuple-element.30), channel_id=1, source_target_pairs={{0,28},{1,5},{2,30},{3,7},{4,8},{5,1},{6,10},{7,3},{8,4},{9,13},{1... | collective-permute-start | bytes 884744 | tf_op jit(solution)/shard_map/ppermute | solution.py:439
  17.7 7.9 %collective-permute-start.2 = (bf16[2,2,96,128]{3,2,1,0:T(8,128)(2,1)S(1)}, bf16[2,2,96,128]{3,2,1,0:T(8,128)(2,1)S(1)}, u32[]{:S(2)}, u32[]{:S(2)}) collective-permute-start(bf16[2,2,96,128]{3,2,1,0:T(8,128)(2,1)S(1)} %get-tuple-element.34), channel_id=1, source_target_pairs={{0,5},{1,28},{2,7},{3,30},{4,3},{5,10},{6,1},{7,8},{8,13},{9,4},{1... | collective-permute-start | bytes 294920 | tf_op jit(solution)/shard_map/ppermute | solution.py:439
  20.0 12.1 %collective-permute-start.11 = (bf16[2,96,896]{2,1,0:T(8,128)(2,1)S(1)}, bf16[2,96,896]{2,1,0:T(8,128)(2,1)S(1)}, u32[]{:S(2)}, u32[]{:S(2)}) collective-permute-start(bf16[2,96,896]{2,1,0:T(8,128)(2,1)S(1)} %get-tuple-element.43), channel_id=1, source_target_pairs={{0,3},{1,2},{2,1},{3,0},{4,5},{5,4},{6,7},{7,6},{8,11},{9,10},{10,... | collective-permute-start | bytes 1032200 | tf_op jit(solution)/shard_map/ppermute | solution.py:439
  22.3 9.8 %collective-permute-start.10 = (bf16[2,96,768]{2,1,0:T(8,128)(2,1)S(1)}, bf16[2,96,768]{2,1,0:T(8,128)(2,1)S(1)}, u32[]{:S(2)}, u32[]{:S(2)}) collective-permute-start(bf16[2,96,768]{2,1,0:T(8,128)(2,1)S(1)} %get-tuple-element.42), channel_id=1, source_target_pairs={{0,28},{1,5},{2,30},{3,7},{4,8},{5,1},{6,10},{7,3},{8,4},{9,13},{1... | collective-permute-start | bytes 884744 | tf_op jit(solution)/shard_map/ppermute | solution.py:439
  27.9 11.7 %collective-permute-start.3 = (bf16[2,96,896]{2,1,0:T(8,128)(2,1)S(1)}, bf16[2,96,896]{2,1,0:T(8,128)(2,1)S(1)}, u32[]{:S(2)}, u32[]{:S(2)}) collective-permute-start(bf16[2,96,896]{2,1,0:T(8,128)(2,1)S(1)} %get-tuple-element.35), channel_id=1, source_target_pairs={{0,4},{1,29},{2,6},{3,31},{4,0},{5,9},{6,2},{7,11},{8,12},{9,5},{1... | collective-permute-start | bytes 1032200 | tf_op jit(solution)/shard_map/ppermute | solution.py:439
  27.9 11.6 %collective-permute-start.4 = (bf16[2,96,896]{2,1,0:T(8,128)(2,1)S(1)}, bf16[2,96,896]{2,1,0:T(8,128)(2,1)S(1)}, u32[]{:S(2)}, u32[]{:S(2)}) collective-permute-start(bf16[2,96,896]{2,1,0:T(8,128)(2,1)S(1)} %get-tuple-element.36), channel_id=1, source_target_pairs={{0,1},{1,0},{2,3},{3,2},{4,7},{5,6},{6,5},{7,4},{8,9},{9,8},{10,11... | collective-permute-start | bytes 1032200 | tf_op jit(solution)/shard_map/ppermute | solution.py:439
  34.4 11.9 %collective-permute-start.12 = (bf16[2,96,896]{2,1,0:T(8,128)(2,1)S(1)}, bf16[2,96,896]{2,1,0:T(8,128)(2,1)S(1)}, u32[]{:S(2)}, u32[]{:S(2)}) collective-permute-start(bf16[2,96,896]{2,1,0:T(8,128)(2,1)S(1)} %get-tuple-element.44.refs_0_), channel_id=1, source_target_pairs={{0,4},{1,29},{2,6},{3,31},{4,0},{5,9},{6,2},{7,11},{8,12},{9,5},{1... | collective-permute-start | bytes 1032200 | tf_op jit(solution)/shard_map/ppermute | solution.py:439
  34.4 11.8 %collective-permute-start.13 = (bf16[2,96,896]{2,1,0:T(8,128)(2,1)S(1)}, bf16[2,96,896]{2,1,0:T(8,128)(2,1)S(1)}, u32[]{:S(2)}, u32[]{:S(2)}) collective-permute-start(bf16[2,96,896]{2,1,0:T(8,128)(2,1)S(1)} %get-tuple-element.45.refs_1_), channel_id=1, source_target_pairs={{0,1},{1,0},{2,3},{3,2},{4,7},{5,6},{6,5},{7,4},{8,9},{9,8},{10,11... | collective-permute-start | bytes 1032200 | tf_op jit(solution)/shard_map/ppermute | solution.py:439
  41.8 10.2 %collective-permute-start.5 = (bf16[2,96,896]{2,1,0:T(8,128)(2,1)S(1)}, bf16[2,96,896]{2,1,0:T(8,128)(2,1)S(1)}, u32[]{:S(2)}, u32[]{:S(2)}) collective-permute-start(bf16[2,96,896]{2,1,0:T(8,128)(2,1)S(1)} %get-tuple-element.37.refs_3_), channel_id=1, source_target_pairs={{0,3},{1,2},{2,1},{3,0},{4,5},{5,4},{6,7},{7,6},{8,11},{9,10},{10,... | collective-permute-start | bytes 1032200 | tf_op jit(solution)/shard_map/ppermute | solution.py:439
  43.2 10.1 %collective-permute-start.6 = (bf16[2,96,896]{2,1,0:T(8,128)(2,1)S(1)}, bf16[2,96,896]{2,1,0:T(8,128)(2,1)S(1)}, u32[]{:S(2)}, u32[]{:S(2)}) collective-permute-start(bf16[2,96,896]{2,1,0:T(8,128)(2,1)S(1)} %get-tuple-element.38.refs_2_), channel_id=1, source_target_pairs={{0,28},{1,5},{2,30},{3,7},{4,8},{5,1},{6,10},{7,3},{8,4},{9,13},{1... | collective-permute-start | bytes 1032200 | tf_op jit(solution)/shard_map/ppermute | solution.py:439

commit v8 on v7

--- a/solution.py
+++ b/solution.py
@@ -256,8 +256,9 @@
 
 
 def middle_kernel(
-    tick, stream, corner_width, first_in, second_in, sources, operators, *refs
-):
+    tick, stream, corner_width, one_in, two_in, sources, operators, *refs
+):
+    first_in, second_in = in_order(tick * stream, one_in, two_in)
     *corner_in, first_out, second_out, left = refs
     outs = (first_out, second_out)
     corner_in = corner_in[0] if corner_in else None
@@ -376,7 +377,7 @@
     tick, ticks, stream, first_in, second_in, sources, operators, corner_width, corner_in
 ):
     shapes = tick_shapes(sources, corner_width, tick, ticks, stream)
-    operands = [first_in, second_in, sources, operators]
+    operands = [*in_order(tick * stream, first_in, second_in), sources, operators]
     if corner_in is not None:
         operands.append(corner_in)
     return pl.pallas_call(

time: 57.2 us -> 59.1 us (1.033); the launches traced: 56.3 us -> 59 us
  waiting for transfers between devices: 4.64 us -> 12.1 us
  starting transfers between devices: 30.2 us -> 25.5 us
    ppermute x14, waiting for transfers between devices: 4.64 us -> 12.1 us  [move(): return lax.ppermute(array, ('row', 'col'), pairs)]
    ppermute x14, starting transfers between devices: 30.2 us -> 25.5 us  [move(): return lax.ppermute(array, ('row', 'col'), pairs)]
  transfers between devices with their start and end apart: 14 -> 14, of which waited for: 3 -> 5; matrix products, arithmetic and copies ran while one was open for 0% -> 0% of each run, Pallas kernels for 29% -> 28%
where the time goes in v8:
time: 59.1 us; the launch traced here: 59 us
  starting transfers between devices  25.5 us (43%)
  Pallas kernels  20.7 us (35%)
  waiting for transfers between devices  12.1 us (20%)
  between operations  0.74 us (1%)
    ppermute x14, starting transfers between devices, move(): return lax.ppermute(array, ('row', 'col'), pairs)  25.5 us
    ppermute x14, waiting for transfers between devices, move(): return lax.ppermute(array, ('row', 'col'), pairs)  12.1 us
    pallas_call x4, Pallas kernels, middle_tick(): pl.pallas_call(functools.partial(middle_kernel, tick, stream, corner_widt...  9.12 us
    pallas_call x2, Pallas kernels, last_tick(): pl.pallas_call(functools.partial(last_kernel, tick, stream, histories, co...  6.19 us
    pallas_call x1, Pallas kernels, load_operators(): pl.pallas_call(functools.partial(load_kernel, counts, stream), out_shape=...  4.04 us
    pallas_call x1, Pallas kernels, select_initial(): pl.pallas_call(functools.partial(select_kernel, counts, stream), out_shap...  1.36 us
  transfers between devices with their start and end apart: 14, of which 5 were waited for; matrix products, arithmetic and copies ran while one was open for 0% of the time, Pallas kernels for 28%

profile of v8, /device:TPU:0, one launch (start us, length us, event | category | flops | bytes accessed | tf_op | source)
XLA Modules:
  0.0 59.0 jit_solution(5285653327607009248)
XLA Ops:
  0.6 1.4 %select_initial.1 = (bf16[2,96,768]{2,1,0:T(8,128)(2,1)S(1)}, bf16[2,96,768]{2,1,0:T(8,128)(2,1)S(1)}, bf16[2,96,128]{2,1,0:T(8,128)(2,1)S(1)}) custom-call(s32[2,2,3]{2,1,0:T(2,128)} %bitcast.25, bf16[2,2,2,96,768]{4,3,2,1,0:T(8,128)(2,1)} %bitcast.12, bf16[2,2,2,96,768]{4,3,2,1,0:T(8,128)(2,1)} %bitcast.14, bf16[2,2,96,128]{3,2,1,0:T(8,128)(2,1)} %bitcast.19, ...), custom_call_target="tpu_custom_call" | custom-call | tf_op jit(solution)/shard_map/select_initial/pallas_call | solution.py:111
  2.0 3.0 %collective-permute-start.7 = (bf16[2,96,768]{2,1,0:T(8,128)(2,1)S(1)}, bf16[2,96,768]{2,1,0:T(8,128)(2,1)S(1)}, u32[]{:S(2)}, u32[]{:S(2)}) collective-permute-start(bf16[2,96,768]{2,1,0:T(8,128)(2,1)S(1)} %get-tuple-element.39), channel_id=1, source_target_pairs={{0,4},{1,29},{2,6},{3,31},{4,0},{5,9},{6,2},{7,11},{8,12},{9,5},{1... | collective-permute-start | bytes 884744 | tf_op jit(solution)/shard_map/ppermute | solution.py:440
  5.0 2.6 %collective-permute-start.8 = (bf16[2,96,768]{2,1,0:T(8,128)(2,1)S(1)}, bf16[2,96,768]{2,1,0:T(8,128)(2,1)S(1)}, u32[]{:S(2)}, u32[]{:S(2)}) collective-permute-start(bf16[2,96,768]{2,1,0:T(8,128)(2,1)S(1)} %get-tuple-element.40), channel_id=1, source_target_pairs={{0,1},{1,0},{2,3},{3,2},{4,7},{5,6},{6,5},{7,4},{8,9},{9,8},{10,11... | collective-permute-start | bytes 884744 | tf_op jit(solution)/shard_map/ppermute | solution.py:440
  7.6 4.0 %load_operators.1 = (bf16[2,96,768]{2,1,0:T(8,128)(2,1)S(1)}, bf16[2,96,896]{2,1,0:T(8,128)(2,1)S(1)}, bf16[2,2,96,128]{3,2,1,0:T(8,128)(2,1)S(1)}, bf16[2,3072,...) custom-call(s32[2,2,3]{2,1,0:T(2,128)} %bitcast.26, ...), custom_call_target="tpu_custom_call" | custom-call | bytes 1 | tf_op jit(solution)/shard_map/load_operators/pallas_call | solution.py:173
  11.6 1.2 %collective-permute-start.1 = (bf16[2,96,896]{2,1,0:T(8,128)(2,1)S(1)}, bf16[2,96,896]{2,1,0:T(8,128)(2,1)S(1)}, u32[]{:S(2)}, u32[]{:S(2)}) collective-permute-start(bf16[2,96,896]{2,1,0:T(8,128)(2,1)S(1)} %get-tuple-element.31), channel_id=1, source_target_pairs={{0,3},{1,2},{2,1},{3,0},{4,5},{5,4},{6,7},{7,6},{8,11},{9,10},{10,... | collective-permute-start | bytes 1032200 | tf_op jit(solution)/shard_map/ppermute | solution.py:440
  12.9 1.1 %collective-permute-start.9 = (bf16[2,96,128]{2,1,0:T(8,128)(2,1)S(1)}, bf16[2,96,128]{2,1,0:T(8,128)(2,1)S(1)}, u32[]{:S(2)}, u32[]{:S(2)}) collective-permute-start(bf16[2,96,128]{2,1,0:T(8,128)(2,1)S(1)} %get-tuple-element.41), channel_id=1, source_target_pairs={{0,31},{1,6},{2,29},{3,4},{4,9},{5,0},{6,11},{7,2},{8,7},{9,14},{1... | collective-permute-start | bytes 147464 | tf_op jit(solution)/shard_map/ppermute | solution.py:440
  13.9 3.7 %collective-permute-start = (bf16[2,96,768]{2,1,0:T(8,128)(2,1)S(1)}, bf16[2,96,768]{2,1,0:T(8,128)(2,1)S(1)}, u32[]{:S(2)}, u32[]{:S(2)}) collective-permute-start(bf16[2,96,768]{2,1,0:T(8,128)(2,1)S(1)} %get-tuple-element.30), channel_id=1, source_target_pairs={{0,28},{1,5},{2,30},{3,7},{4,8},{5,1},{6,10},{7,3},{8,4},{9,13},{1... | collective-permute-start | bytes 884744 | tf_op jit(solution)/shard_map/ppermute | solution.py:440
  17.7 0.0 collective-permute-done.9.refs_0_
  17.7 0.0 collective-permute-start.2
  17.7 0.0 collective-permute-done.7.one_in
  17.7 2.3 %tick0_stream0.1 = (bf16[2,96,768]{2,1,0:T(8,128)(2,1)S(1)}, bf16[2,96,896]{2,1,0:T(8,128)(2,1)S(1)}) custom-call(bf16[2,96,768]{2,1,0:T(8,128)(2,1)S(1)} %collective-permute-done.7.one_in, bf16[2,96,768]{2,1,0:T(8,128)(2,1)S(1)} %collective-permute-done.8.two_in, bf16[2,2,2,96,768]{4,3,2,1,0:T(8,128)(2,1)S(1)} %get-tuple-element.32.sources, ...), custom_call_target="tpu_custom_call" | custom-call | flops 2000000000 | bytes 1 | tf_op jit(solution)/shard_map/tick0_stream0/pallas_call | solution.py:383
  20.0 2.3 %collective-permute-start.11 = (bf16[2,96,896]{2,1,0:T(8,128)(2,1)S(1)}, bf16[2,96,896]{2,1,0:T(8,128)(2,1)S(1)}, u32[]{:S(2)}, u32[]{:S(2)}) collective-permute-start(bf16[2,96,896]{2,1,0:T(8,128)(2,1)S(1)} %get-tuple-element.43), channel_id=1, source_target_pairs={{0,3},{1,2},{2,1},{3,0},{4,5},{5,4},{6,7},{7,6},{8,11},{9,10},{10,... | collective-permute-start | bytes 1032200 | tf_op jit(solution)/shard_map/ppermute | solution.py:440
  22.3 2.5 %collective-permute-start.10 = (bf16[2,96,768]{2,1,0:T(8,128)(2,1)S(1)}, bf16[2,96,768]{2,1,0:T(8,128)(2,1)S(1)}, u32[]{:S(2)}, u32[]{:S(2)}) collective-permute-start(bf16[2,96,768]{2,1,0:T(8,128)(2,1)S(1)} %get-tuple-element.42), channel_id=1, source_target_pairs={{0,28},{1,5},{2,30},{3,7},{4,8},{5,1},{6,10},{7,3},{8,4},{9,13},{1... | collective-permute-start | bytes 884744 | tf_op jit(solution)/shard_map/ppermute | solution.py:440
  24.8 0.8 %collective-permute-done.2.refs_0_ = bf16[2,2,96,128]{3,2,1,0:T(8,128)(2,1)S(1)} collective-permute-done((bf16[2,2,96,128]{3,2,1,0:T(8,128)(2,1)S(1)}, bf16[2,2,96,128]{3,2,1,0:T(8,128)(2,1)S(1)}, u32[]{:S(2)}, u32[]{:S(2)}) %collective-permute-start.2) | collective-permute-done | bytes 98336 | tf_op jit(solution)/shard_map/ppermute | solution.py:440
  25.6 0.0 collective-permute-done.one_in
  25.6 0.0 collective-permute-done.1.two_in
  25.6 2.3 %tick0_stream1.1 = (bf16[2,96,896]{2,1,0:T(8,128)(2,1)S(1)}, bf16[2,96,896]{2,1,0:T(8,128)(2,1)S(1)}) custom-call(bf16[2,96,768]{2,1,0:T(8,128)(2,1)S(1)} %collective-permute-done.one_in, bf16[2,96,896]{2,1,0:T(8,128)(2,1)S(1)} %collective-permute-done.1.two_in, bf16[2,2,2,96,768]{4,3,2,1,0:T(8,128)(2,1)S(1)} %get-tuple-element.32.sources, ...), custom_call_target="tpu_custom_call" | custom-call | bytes 1 | tf_op jit(solution)/shard_map/tick0_stream1/pallas_call | solution.py:383
  27.9 1.3 %collective-permute-start.3 = (bf16[2,96,896]{2,1,0:T(8,128)(2,1)S(1)}, bf16[2,96,896]{2,1,0:T(8,128)(2,1)S(1)}, u32[]{:S(2)}, u32[]{:S(2)}) collective-permute-start(bf16[2,96,896]{2,1,0:T(8,128)(2,1)S(1)} %get-tuple-element.35), channel_id=1, source_target_pairs={{0,1},{1,0},{2,3},{3,2},{4,7},{5,6},{6,5},{7,4},{8,9},{9,8},{10,11... | collective-permute-start | bytes 1032200 | tf_op jit(solution)/shard_map/ppermute | solution.py:440
  29.1 0.0 collective-permute-start.4
  29.1 2.6 %collective-permute-done.10.one_in = bf16[2,96,768]{2,1,0:T(8,128)(2,1)S(1)} collective-permute-done((bf16[2,96,768]{2,1,0:T(8,128)(2,1)S(1)}, bf16[2,96,768]{2,1,0:T(8,128)(2,1)S(1)}, u32[]{:S(2)}, u32[]{:S(2)}) %collective-permute-start.10) | collective-permute-done | bytes 294944 | tf_op jit(solution)/shard_map/ppermute | solution.py:440
  31.8 0.2 collective-permute-done.11.two_in
  32.0 2.3 %tick1_stream0.1 = (bf16[2,96,896]{2,1,0:T(8,128)(2,1)S(1)}, bf16[2,96,896]{2,1,0:T(8,128)(2,1)S(1)}) custom-call(bf16[2,96,768]{2,1,0:T(8,128)(2,1)S(1)} %collective-permute-done.10.one_in, bf16[2,96,896]{2,1,0:T(8,128)(2,1)S(1)} %collective-permute-done.11.two_in, bf16[2,2,2,96,768]{4,3,2,1,0:T(8,128)(2,1)S(1)} %get-tuple-element.32.sources, ...), custom_call_target="tpu_custom_call" | custom-call | flops 800000000 | bytes 1 | tf_op jit(solution)/shard_map/tick1_stream0/pallas_call | solution.py:383
  34.3 0.1 collective-permute-start.12
  34.4 3.3 %collective-permute-start.13 = (bf16[2,96,896]{2,1,0:T(8,128)(2,1)S(1)}, bf16[2,96,896]{2,1,0:T(8,128)(2,1)S(1)}, u32[]{:S(2)}, u32[]{:S(2)}) collective-permute-start(bf16[2,96,896]{2,1,0:T(8,128)(2,1)S(1)} %get-tuple-element.45.refs_1_), channel_id=1, source_target_pairs={{0,1},{1,0},{2,3},{3,2},{4,7},{5,6},{6,5},{7,4},{8,9},{9,8},{10,11... | collective-permute-start | bytes 1032200 | tf_op jit(solution)/shard_map/ppermute | solution.py:440
  37.7 0.0 collective-permute-done.3.one_in
  37.7 2.4 %collective-permute-done.4.two_in = bf16[2,96,896]{2,1,0:T(8,128)(2,1)S(1)} collective-permute-done((bf16[2,96,896]{2,1,0:T(8,128)(2,1)S(1)}, bf16[2,96,896]{2,1,0:T(8,128)(2,1)S(1)}, u32[]{:S(2)}, u32[]{:S(2)}) %collective-permute-start.4) | collective-permute-done | bytes 344096 | tf_op jit(solution)/shard_map/ppermute | solution.py:440
  40.1 2.3 %tick1_stream1.1 = (bf16[2,96,896]{2,1,0:T(8,128)(2,1)S(1)}, bf16[2,96,896]{2,1,0:T(8,128)(2,1)S(1)}) custom-call(bf16[2,96,896]{2,1,0:T(8,128)(2,1)S(1)} %collective-permute-done.3.one_in, bf16[2,96,896]{2,1,0:T(8,128)(2,1)S(1)} %collective-permute-done.4.two_in, bf16[2,2,2,96,768]{4,3,2,1,0:T(8,128)(2,1)S(1)} %get-tuple-element.32.sources, ...), custom_call_target="tpu_custom_call" | custom-call | bytes 1 | tf_op jit(solution)/shard_map/tick1_stream1/pallas_call | solution.py:383
  42.4 0.1 collective-permute-start.5
  42.4 4.3 %collective-permute-start.6 = (bf16[2,96,896]{2,1,0:T(8,128)(2,1)S(1)}, bf16[2,96,896]{2,1,0:T(8,128)(2,1)S(1)}, u32[]{:S(2)}, u32[]{:S(2)}) collective-permute-start(bf16[2,96,896]{2,1,0:T(8,128)(2,1)S(1)} %get-tuple-element.38.refs_2_), channel_id=1, source_target_pairs={{0,28},{1,5},{2,30},{3,7},{4,8},{5,1},{6,10},{7,3},{8,4},{9,13},{1... | collective-permute-start | bytes 1032200 | tf_op jit(solution)/shard_map/ppermute | solution.py:440
  46.7 6.0 %collective-permute-done.12.one_in = bf16[2,96,896]{2,1,0:T(8,128)(2,1)S(1)} collective-permute-done((bf16[2,96,896]{2,1,0:T(8,128)(2,1)S(1)}, bf16[2,96,896]{2,1,0:T(8,128)(2,1)S(1)}, u32[]{:S(2)}, u32[]{:S(2)}) %collective-permute-start.12) | collective-permute-done | bytes 344096 | tf_op jit(solution)/shard_map/ppermute | solution.py:440
  52.7 3.1 %tick2_stream0.1 = (bf16[2,2,2,96,768]{4,3,2,1,0:T(8,128)(2,1)}, bf16[2,2,2,96,768]{4,3,2,1,0:T(8,128)(2,1)}, bf16[2,2,96,128]{3,2,1,0:T(8,128)(2,1)}, bf16[2,2,96,128]{3,2,1,0:T(8,128)(2,1)}) custom-call(f32[2,8,128]{2,1,0:T(8,128)S(1)} %get-tuple-element.29.flags, bf16[2,96,896]{2,1,0:T(8,128)(2,1)S(1)} %collective-permute-done.12.one_in, ...), custom_call_target="tpu_custom_call" | custom-call | bytes 1 | tf_op jit(solution)/shard_map/tick2_stream0/pallas_call | solution.py:416
  55.9 3.1 %tick2_stream1.1 = (bf16[2,2,2,96,768]{4,3,2,1,0:T(8,128)(2,1)}, bf16[2,2,2,96,768]{4,3,2,1,0:T(8,128)(2,1)}, bf16[2,2,96,128]{3,2,1,0:T(8,128)(2,1)}, bf16[2,2,96,128]{3,2,1,0:T(8,128)(2,1)}) custom-call(f32[2,8,128]{2,1,0:T(8,128)S(1)} %get-tuple-element.29.flags, ...), custom_call_target="tpu_custom_call", output_to_operand_aliasing={{0}: (5, {}), {1}: (6, {}), {2}: (7, {}), {3}: (8, {})} | custom-call | bytes 1 | tf_op jit(solution)/shard_map/tick2_stream1/pallas_call | solution.py:416
  (4 shorter events, 0.0 us)
Async XLA Ops:
  2.0 15.7 %collective-permute-start.7 = (bf16[2,96,768]{2,1,0:T(8,128)(2,1)S(1)}, bf16[2,96,768]{2,1,0:T(8,128)(2,1)S(1)}, u32[]{:S(2)}, u32[]{:S(2)}) collective-permute-start(bf16[2,96,768]{2,1,0:T(8,128)(2,1)S(1)} %get-tuple-element.39), channel_id=1, source_target_pairs={{0,4},{1,29},{2,6},{3,31},{4,0},{5,9},{6,2},{7,11},{8,12},{9,5},{1... | collective-permute-start | bytes 884744 | tf_op jit(solution)/shard_map/ppermute | solution.py:440
  5.0 12.7 %collective-permute-start.8 = (bf16[2,96,768]{2,1,0:T(8,128)(2,1)S(1)}, bf16[2,96,768]{2,1,0:T(8,128)(2,1)S(1)}, u32[]{:S(2)}, u32[]{:S(2)}) collective-permute-start(bf16[2,96,768]{2,1,0:T(8,128)(2,1)S(1)} %get-tuple-element.40), channel_id=1, source_target_pairs={{0,1},{1,0},{2,3},{3,2},{4,7},{5,6},{6,5},{7,4},{8,9},{9,8},{10,11... | collective-permute-start | bytes 884744 | tf_op jit(solution)/shard_map/ppermute | solution.py:440
  11.6 13.9 %collective-permute-start.1 = (bf16[2,96,896]{2,1,0:T(8,128)(2,1)S(1)}, bf16[2,96,896]{2,1,0:T(8,128)(2,1)S(1)}, u32[]{:S(2)}, u32[]{:S(2)}) collective-permute-start(bf16[2,96,896]{2,1,0:T(8,128)(2,1)S(1)} %get-tuple-element.31), channel_id=1, source_target_pairs={{0,3},{1,2},{2,1},{3,0},{4,5},{5,4},{6,7},{7,6},{8,11},{9,10},{10,... | collective-permute-start | bytes 1032200 | tf_op jit(solution)/shard_map/ppermute | solution.py:440
  12.9 4.8 %collective-permute-start.9 = (bf16[2,96,128]{2,1,0:T(8,128)(2,1)S(1)}, bf16[2,96,128]{2,1,0:T(8,128)(2,1)S(1)}, u32[]{:S(2)}, u32[]{:S(2)}) collective-permute-start(bf16[2,96,128]{2,1,0:T(8,128)(2,1)S(1)} %get-tuple-element.41), channel_id=1, source_target_pairs={{0,31},{1,6},{2,29},{3,4},{4,9},{5,0},{6,11},{7,2},{8,7},{9,14},{1... | collective-permute-start | bytes 147464 | tf_op jit(solution)/shard_map/ppermute | solution.py:440
  13.9 11.6 %collective-permute-start = (bf16[2,96,768]{2,1,0:T(8,128)(2,1)S(1)}, bf16[2,96,768]{2,1,0:T(8,128)(2,1)S(1)}, u32[]{:S(2)}, u32[]{:S(2)}) collective-permute-start(bf16[2,96,768]{2,1,0:T(8,128)(2,1)S(1)} %get-tuple-element.30), channel_id=1, source_target_pairs={{0,28},{1,5},{2,30},{3,7},{4,8},{5,1},{6,10},{7,3},{8,4},{9,13},{1... | collective-permute-start | bytes 884744 | tf_op jit(solution)/shard_map/ppermute | solution.py:440
  17.7 7.9 %collective-permute-start.2 = (bf16[2,2,96,128]{3,2,1,0:T(8,128)(2,1)S(1)}, bf16[2,2,96,128]{3,2,1,0:T(8,128)(2,1)S(1)}, u32[]{:S(2)}, u32[]{:S(2)}) collective-permute-start(bf16[2,2,96,128]{3,2,1,0:T(8,128)(2,1)S(1)} %get-tuple-element.34), channel_id=1, source_target_pairs={{0,5},{1,28},{2,7},{3,30},{4,3},{5,10},{6,1},{7,8},{8,13},{9,4},{1... | collective-permute-start | bytes 294920 | tf_op jit(solution)/shard_map/ppermute | solution.py:440
  20.0 12.0 %collective-permute-start.11 = (bf16[2,96,896]{2,1,0:T(8,128)(2,1)S(1)}, bf16[2,96,896]{2,1,0:T(8,128)(2,1)S(1)}, u32[]{:S(2)}, u32[]{:S(2)}) collective-permute-start(bf16[2,96,896]{2,1,0:T(8,128)(2,1)S(1)} %get-tuple-element.43), channel_id=1, source_target_pairs={{0,3},{1,2},{2,1},{3,0},{4,5},{5,4},{6,7},{7,6},{8,11},{9,10},{10,... | collective-permute-start | bytes 1032200 | tf_op jit(solution)/shard_map/ppermute | solution.py:440
  22.3 9.5 %collective-permute-start.10 = (bf16[2,96,768]{2,1,0:T(8,128)(2,1)S(1)}, bf16[2,96,768]{2,1,0:T(8,128)(2,1)S(1)}, u32[]{:S(2)}, u32[]{:S(2)}) collective-permute-start(bf16[2,96,768]{2,1,0:T(8,128)(2,1)S(1)} %get-tuple-element.42), channel_id=1, source_target_pairs={{0,28},{1,5},{2,30},{3,7},{4,8},{5,1},{6,10},{7,3},{8,4},{9,13},{1... | collective-permute-start | bytes 884744 | tf_op jit(solution)/shard_map/ppermute | solution.py:440
  27.9 9.8 %collective-permute-start.3 = (bf16[2,96,896]{2,1,0:T(8,128)(2,1)S(1)}, bf16[2,96,896]{2,1,0:T(8,128)(2,1)S(1)}, u32[]{:S(2)}, u32[]{:S(2)}) collective-permute-start(bf16[2,96,896]{2,1,0:T(8,128)(2,1)S(1)} %get-tuple-element.35), channel_id=1, source_target_pairs={{0,1},{1,0},{2,3},{3,2},{4,7},{5,6},{6,5},{7,4},{8,9},{9,8},{10,11... | collective-permute-start | bytes 1032200 | tf_op jit(solution)/shard_map/ppermute | solution.py:440
  29.1 10.9 %collective-permute-start.4 = (bf16[2,96,896]{2,1,0:T(8,128)(2,1)S(1)}, bf16[2,96,896]{2,1,0:T(8,128)(2,1)S(1)}, u32[]{:S(2)}, u32[]{:S(2)}) collective-permute-start(bf16[2,96,896]{2,1,0:T(8,128)(2,1)S(1)} %get-tuple-element.36), channel_id=1, source_target_pairs={{0,4},{1,29},{2,6},{3,31},{4,0},{5,9},{6,2},{7,11},{8,12},{9,5},{1... | collective-permute-start | bytes 1032200 | tf_op jit(solution)/shard_map/ppermute | solution.py:440
  34.3 18.4 %collective-permute-start.12 = (bf16[2,96,896]{2,1,0:T(8,128)(2,1)S(1)}, bf16[2,96,896]{2,1,0:T(8,128)(2,1)S(1)}, u32[]{:S(2)}, u32[]{:S(2)}) collective-permute-start(bf16[2,96,896]{2,1,0:T(8,128)(2,1)S(1)} %get-tuple-element.44.refs_0_), channel_id=1, source_target_pairs={{0,4},{1,29},{2,6},{3,31},{4,0},{5,9},{6,2},{7,11},{8,12},{9,5},{1... | collective-permute-start | bytes 1032200 | tf_op jit(solution)/shard_map/ppermute | solution.py:440
  34.4 18.4 %collective-permute-start.13 = (bf16[2,96,896]{2,1,0:T(8,128)(2,1)S(1)}, bf16[2,96,896]{2,1,0:T(8,128)(2,1)S(1)}, u32[]{:S(2)}, u32[]{:S(2)}) collective-permute-start(bf16[2,96,896]{2,1,0:T(8,128)(2,1)S(1)} %get-tuple-element.45.refs_1_), channel_id=1, source_target_pairs={{0,1},{1,0},{2,3},{3,2},{4,7},{5,6},{6,5},{7,4},{8,9},{9,8},{10,11... | collective-permute-start | bytes 1032200 | tf_op jit(solution)/shard_map/ppermute | solution.py:440
  42.4 13.5 %collective-permute-start.5 = (bf16[2,96,896]{2,1,0:T(8,128)(2,1)S(1)}, bf16[2,96,896]{2,1,0:T(8,128)(2,1)S(1)}, u32[]{:S(2)}, u32[]{:S(2)}) collective-permute-start(bf16[2,96,896]{2,1,0:T(8,128)(2,1)S(1)} %get-tuple-element.37.refs_3_), channel_id=1, source_target_pairs={{0,3},{1,2},{2,1},{3,0},{4,5},{5,4},{6,7},{7,6},{8,11},{9,10},{10,... | collective-permute-start | bytes 1032200 | tf_op jit(solution)/shard_map/ppermute | solution.py:440
  42.4 13.4 %collective-permute-start.6 = (bf16[2,96,896]{2,1,0:T(8,128)(2,1)S(1)}, bf16[2,96,896]{2,1,0:T(8,128)(2,1)S(1)}, u32[]{:S(2)}, u32[]{:S(2)}) collective-permute-start(bf16[2,96,896]{2,1,0:T(8,128)(2,1)S(1)} %get-tuple-element.38.refs_2_), channel_id=1, source_target_pairs={{0,28},{1,5},{2,30},{3,7},{4,8},{5,1},{6,10},{7,3},{8,4},{9,13},{1... | collective-permute-start | bytes 1032200 | tf_op jit(solution)/shard_map/ppermute | solution.py:440
